TPU v7x, 32 devices: a whole 2x2x4 slice. The times are simulated.
32 devices in a mesh: dp: 8 (over y, x, core), mp: 4 (over z).
Axes of the slice: x: 2, y: 2, z: 4, core: 2. Of those that a mesh axis runs over, the one named last changes fastest.
Arguments:
- layer_input: bfloat16 [16384, 2048], P(('dp', 'mp')), may hold values from -6 to 6
- out_grad: bfloat16 [16384, 2048], P(('dp', 'mp')), may hold values from -6 to 6
- norm_attn: float32 [2048], replicated, may hold values from 0.5 to 1.5
- query_norm: float32 [128], replicated, may hold values from 0.5 to 1.5
- key_norm: float32 [128], replicated, may hold values from 0.5 to 1.5
- w_query: bfloat16 [2048, 2048], P('dp', 'mp'), may hold values from -0.125 to 0.125
- key_matrix: bfloat16 [2048, 1024], P('dp', 'mp'), may hold values from -0.125 to 0.125
- value_matrix: bfloat16 [2048, 1024], P('dp', 'mp'), may hold values from -0.125 to 0.125
- w_output: bfloat16 [2048, 2048], P('mp', 'dp'), may hold values from -1 to 1
- norm_mlp: float32 [2048], replicated, may hold values from 0.5 to 1.5
- w_gate: bfloat16 [2048, 6144], P('dp', 'mp'), may hold values from -0.125 to 0.125
- w_up: bfloat16 [2048, 6144], P('dp', 'mp'), may hold values from -0.125 to 0.125
- w_down: bfloat16 [6144, 2048], P('mp', 'dp'), may hold values from -0.078125 to 0.078125
Outputs:
- layer_output: bfloat16 [16384, 2048], P(('dp', 'mp'))
- input_grad: float32 [16384, 2048], P(('dp', 'mp'))
- grad_norm_attn: float32 [2048], replicated
- grad_query_norm: float32 [128], replicated
- grad_key_norm: float32 [128], replicated
- grad_query: float32 [2048, 2048], P('dp', 'mp')
- grad_key: float32 [2048, 1024], P('dp', 'mp')
- grad_value: float32 [2048, 1024], P('dp', 'mp')
- grad_output: float32 [2048, 2048], P('mp', 'dp')
- grad_norm_mlp: float32 [2048], replicated
- grad_gate: float32 [2048, 6144], P('dp', 'mp')
- grad_up: float32 [2048, 6144], P('dp', 'mp')
- grad_down: float32 [6144, 2048], P('mp', 'dp')
All inputs are finite; a program needn't handle non-finite values.
Results may differ from a plain program's by a relative error of at most 0.018.
Values may be sent and summed in bfloat16 or wider, within the bound.
A program may use at most 320 MiB of HBM per device.

v0:
```python
import jax
import jax.numpy as jnp
from jax import lax
from jax.sharding import PartitionSpec as P

HEAD_SIZE = 128
SEQUENCE_LENGTH = 1024


EPSILON = 1e-06
THETA = 1000000.0


def norm_rows(values, gain):
    factor = lax.rsqrt(jnp.mean(values * values, -1, keepdims=True) + EPSILON)
    return (values * factor * gain, factor)


def norm_back(values, factor, gain, upstream):
    scaled = upstream * gain
    inner = jnp.mean(scaled * values, -1, keepdims=True)
    return factor * scaled - values * (factor * factor * factor) * inner


def tables(length, width):
    half_width = width // 2
    frequencies = THETA ** (-(jnp.arange(half_width, dtype=jnp.float32) * 2.0 / width))
    angles = jnp.arange(length, dtype=jnp.float32)[:, None] * frequencies[None, :]
    return (jnp.cos(angles), jnp.sin(angles))


def rotate(values, cosine_table, sine_table):
    half_width = values.shape[-1] // 2
    first_half = values[..., :half_width]
    second_half = values[..., half_width:]
    cosine_part = cosine_table[:, None, :]
    sine_part = sine_table[:, None, :]
    return jnp.concatenate(
        [
            first_half * cosine_part - second_half * sine_part,
            second_half * cosine_part + first_half * sine_part,
        ],
        -1,
    )


def rotate_back(grads, cosine_table, sine_table):
    half_width = grads.shape[-1] // 2
    first_half = grads[..., :half_width]
    second_half = grads[..., half_width:]
    cosine_part = cosine_table[:, None, :]
    sine_part = sine_table[:, None, :]
    return jnp.concatenate(
        [
            first_half * cosine_part + second_half * sine_part,
            second_half * cosine_part - first_half * sine_part,
        ],
        -1,
    )


def matmul(left, right):
    return jnp.dot(left, right, preferred_element_type=jnp.float32)


def dot_last(left, right):
    return lax.dot_general(
        left, right, (((1,), (1,)), ((), ())), preferred_element_type=jnp.float32
    )


def dot_first(left, right):
    return lax.dot_general(
        left, right, (((0,), (0,)), ((), ())), preferred_element_type=jnp.float32
    )


def masked_scores(query_block, keys, start, block_rows, scale):
    raw = (
        jnp.einsum("qhgd,khd->hgqk", query_block, keys, preferred_element_type=jnp.float32) * scale
    )
    query_places = start + jnp.arange(block_rows)[:, None]
    key_places = jnp.arange(keys.shape[0])[None, :]
    return jnp.where(key_places <= query_places, raw, -jnp.inf)


def local(
    layer_input,
    out_grad,
    norm_attn,
    query_norm,
    key_norm,
    w_query,
    key_matrix,
    value_matrix,
    w_output,
    norm_mlp,
    w_gate,
    w_up,
    w_down,
):
    inputs = layer_input.astype(jnp.float32)
    query_full, key_full, value_full, output_full = (
        lax.all_gather(w_query, "dp", axis=0, tiled=True),
        lax.all_gather(key_matrix, "dp", axis=0, tiled=True),
        lax.all_gather(value_matrix, "dp", axis=0, tiled=True),
        lax.all_gather(w_output, "dp", axis=1, tiled=True),
    )
    first_normed, factor_one = norm_rows(inputs, norm_attn)
    normed_all = lax.all_gather(first_normed.astype(jnp.bfloat16), "mp", axis=0, tiled=True)
    total_rows = normed_all.shape[0]
    sequence_batch = total_rows // SEQUENCE_LENGTH
    query_heads = query_full.shape[1] // HEAD_SIZE
    shared_heads = key_full.shape[1] // HEAD_SIZE
    heads_per_group = query_heads // shared_heads
    query_proj = matmul(normed_all, query_full).reshape(
        sequence_batch, SEQUENCE_LENGTH, query_heads, HEAD_SIZE
    )
    key_projected = matmul(normed_all, key_full).reshape(
        sequence_batch, SEQUENCE_LENGTH, shared_heads, HEAD_SIZE
    )
    value_low = (
        matmul(normed_all, value_full)
        .astype(jnp.bfloat16)
        .reshape(sequence_batch, SEQUENCE_LENGTH, shared_heads, HEAD_SIZE)
    )
    cosine_table, sine_table = tables(SEQUENCE_LENGTH, HEAD_SIZE)
    query_normed, query_factor = norm_rows(query_proj, query_norm)
    query_rotated = rotate(query_normed, cosine_table, sine_table).astype(jnp.bfloat16)
    query_rotated = query_rotated.reshape(
        sequence_batch, SEQUENCE_LENGTH, shared_heads, heads_per_group, HEAD_SIZE
    )
    key_normed, key_factor = norm_rows(key_projected, key_norm)
    key_rot = rotate(key_normed, cosine_table, sine_table).astype(jnp.bfloat16)
    block_rows = min(512, SEQUENCE_LENGTH)
    block_count = SEQUENCE_LENGTH // block_rows
    scale = HEAD_SIZE ** (-0.5)
    attended_pieces = []
    log_totals = []
    for seq_index in range(sequence_batch):
        for block_index in range(block_count):
            start = block_index * block_rows
            query_block = query_rotated[seq_index, start : start + block_rows]
            scores = masked_scores(query_block, key_rot[seq_index], start, block_rows, scale)
            largest = jnp.max(scores, -1, keepdims=True)
            expanded = jnp.exp(scores - largest)
            summed = jnp.sum(expanded, -1, keepdims=True)
            probs_low = (expanded / summed).astype(jnp.bfloat16)
            block_out = jnp.einsum(
                "hgqk,khd->qhgd",
                probs_low,
                value_low[seq_index],
                preferred_element_type=jnp.float32,
            )
            attended_pieces.append(block_out.reshape(block_rows, query_heads * HEAD_SIZE))
            log_totals.append(largest + jnp.log(summed))
    attended = jnp.concatenate(attended_pieces, 0).astype(jnp.bfloat16)
    attn_sum = lax.psum_scatter(
        matmul(attended, output_full), "mp", scatter_dimension=0, tiled=True
    )
    middle = inputs + attn_sum
    gate_full, up_full, down_full = (
        lax.all_gather(w_gate, "dp", axis=0, tiled=True),
        lax.all_gather(w_up, "dp", axis=0, tiled=True),
        lax.all_gather(w_down, "dp", axis=1, tiled=True),
    )
    normed_two, factor_two = norm_rows(middle, norm_mlp)
    normed_two_all = lax.all_gather(normed_two.astype(jnp.bfloat16), "mp", axis=0, tiled=True)
    gate_value = matmul(normed_two_all, gate_full)
    up_value = matmul(normed_two_all, up_full)
    hidden_low = (jax.nn.silu(gate_value) * up_value).astype(jnp.bfloat16)
    mlp_sum = lax.psum_scatter(
        matmul(hidden_low, down_full).astype(jnp.bfloat16), "mp", scatter_dimension=0, tiled=True
    ).astype(jnp.float32)
    layer_output = (middle + mlp_sum).astype(jnp.bfloat16)
    grad_rows = lax.all_gather(out_grad, "mp", axis=0, tiled=True)
    gate_back, up_back, down_back = (
        lax.all_gather(w_gate, "dp", axis=0, tiled=True),
        lax.all_gather(w_up, "dp", axis=0, tiled=True),
        lax.all_gather(w_down, "dp", axis=1, tiled=True),
    )
    hidden_grad = dot_last(grad_rows, down_back)
    down_grad = dot_first(hidden_low, grad_rows)
    sigmoid_gate = jax.nn.sigmoid(gate_value)
    gate_grad = (
        hidden_grad * up_value * sigmoid_gate * (1.0 + gate_value * (1.0 - sigmoid_gate))
    ).astype(jnp.bfloat16)
    up_grad = (hidden_grad * gate_value * sigmoid_gate).astype(jnp.bfloat16)
    gate_weight_grad = dot_first(normed_two_all, gate_grad)
    up_weight_grad = dot_first(normed_two_all, up_grad)
    two_grad = lax.psum_scatter(
        dot_last(gate_grad, gate_back) + dot_last(up_grad, up_back),
        "mp",
        scatter_dimension=0,
        tiled=True,
    )
    gain_two_grad = jnp.sum(two_grad * middle * factor_two, 0)
    middle_grad = out_grad.astype(jnp.float32) + norm_back(middle, factor_two, norm_mlp, two_grad)
    mlp_grads = (
        lax.psum_scatter(
            gate_weight_grad.astype(jnp.bfloat16), "dp", scatter_dimension=0, tiled=True
        ).astype(jnp.float32),
        lax.psum_scatter(
            up_weight_grad.astype(jnp.bfloat16), "dp", scatter_dimension=0, tiled=True
        ).astype(jnp.float32),
        lax.psum_scatter(
            down_grad.astype(jnp.bfloat16), "dp", scatter_dimension=1, tiled=True
        ).astype(jnp.float32),
    )
    branch_all = lax.all_gather(middle_grad.astype(jnp.bfloat16), "mp", axis=0, tiled=True)
    output_weight_grad = dot_first(attended, branch_all)
    attended_grad = dot_last(branch_all, output_full).astype(jnp.bfloat16)
    attended_grad = attended_grad.reshape(
        sequence_batch, SEQUENCE_LENGTH, shared_heads, heads_per_group, HEAD_SIZE
    )
    query_grad_seqs = []
    key_grad_seqs = []
    value_grad_seqs = []
    for seq_index in range(sequence_batch):
        key_running = jnp.zeros((SEQUENCE_LENGTH, shared_heads, HEAD_SIZE), jnp.float32)
        value_running = jnp.zeros((SEQUENCE_LENGTH, shared_heads, HEAD_SIZE), jnp.float32)
        query_blocks = []
        for block_index in range(block_count):
            start = block_index * block_rows
            query_block = query_rotated[seq_index, start : start + block_rows]
            scores = masked_scores(query_block, key_rot[seq_index], start, block_rows, scale)
            probs_full = jnp.exp(scores - log_totals[seq_index * block_count + block_index])
            probs_low = probs_full.astype(jnp.bfloat16)
            grad_block = attended_grad[seq_index, start : start + block_rows]
            prob_grad = jnp.einsum(
                "qhgd,khd->hgqk",
                grad_block,
                value_low[seq_index],
                preferred_element_type=jnp.float32,
            )
            row_inner = jnp.sum(probs_full * prob_grad, -1, keepdims=True)
            score_grad = (probs_full * (prob_grad - row_inner)).astype(jnp.bfloat16)
            query_blocks.append(
                jnp.einsum(
                    "hgqk,khd->qhgd",
                    score_grad,
                    key_rot[seq_index],
                    preferred_element_type=jnp.float32,
                )
                * scale
            )
            key_running = (
                key_running
                + jnp.einsum(
                    "hgqk,qhgd->khd", score_grad, query_block, preferred_element_type=jnp.float32
                )
                * scale
            )
            value_running = value_running + jnp.einsum(
                "hgqk,qhgd->khd", probs_low, grad_block, preferred_element_type=jnp.float32
            )
        query_grad_seqs.append(jnp.concatenate(query_blocks, 0))
        key_grad_seqs.append(key_running)
        value_grad_seqs.append(value_running)
    rot_query_grad = jnp.stack(query_grad_seqs, 0).reshape(
        sequence_batch, SEQUENCE_LENGTH, query_heads, HEAD_SIZE
    )
    rot_key_grad = jnp.stack(key_grad_seqs, 0)
    value_grad = (
        jnp.stack(value_grad_seqs, 0)
        .reshape(total_rows, shared_heads * HEAD_SIZE)
        .astype(jnp.bfloat16)
    )
    query_normed_grad = rotate_back(rot_query_grad, cosine_table, sine_table)
    query_gain_grad = jnp.sum(query_normed_grad * query_proj * query_factor, (0, 1, 2))
    query_grad = norm_back(query_proj, query_factor, query_norm, query_normed_grad)
    query_grad = query_grad.reshape(total_rows, query_heads * HEAD_SIZE).astype(jnp.bfloat16)
    key_normed_grad = rotate_back(rot_key_grad, cosine_table, sine_table)
    key_gain_grad = jnp.sum(key_normed_grad * key_projected * key_factor, (0, 1, 2))
    key_grad = norm_back(key_projected, key_factor, key_norm, key_normed_grad)
    key_grad = key_grad.reshape(total_rows, shared_heads * HEAD_SIZE).astype(jnp.bfloat16)
    query_weight_grad = dot_first(normed_all, query_grad)
    key_weight_grad = dot_first(normed_all, key_grad)
    value_weight_grad = dot_first(normed_all, value_grad)
    one_partial = (
        dot_last(query_grad, query_full)
        + dot_last(key_grad, key_full)
        + dot_last(value_grad, value_full)
    )
    one_grad = lax.psum_scatter(
        one_partial.astype(jnp.bfloat16), "mp", scatter_dimension=0, tiled=True
    ).astype(jnp.float32)
    gain_one_grad = jnp.sum(one_grad * inputs * factor_one, 0)
    input_grad = middle_grad + norm_back(inputs, factor_one, norm_attn, one_grad)
    attn_grads = (
        lax.psum_scatter(
            query_weight_grad.astype(jnp.bfloat16), "dp", scatter_dimension=0, tiled=True
        ).astype(jnp.float32),
        lax.psum_scatter(
            key_weight_grad.astype(jnp.bfloat16), "dp", scatter_dimension=0, tiled=True
        ).astype(jnp.float32),
        lax.psum_scatter(
            value_weight_grad.astype(jnp.bfloat16), "dp", scatter_dimension=0, tiled=True
        ).astype(jnp.float32),
        lax.psum_scatter(
            output_weight_grad.astype(jnp.bfloat16), "dp", scatter_dimension=1, tiled=True
        ).astype(jnp.float32),
    )
    gain_sums = lax.psum(
        (gain_one_grad, query_gain_grad, key_gain_grad, gain_two_grad), ("dp", "mp")
    )
    return (
        layer_output,
        input_grad,
        gain_sums[0],
        gain_sums[1],
        gain_sums[2],
        attn_grads[0],
        attn_grads[1],
        attn_grads[2],
        attn_grads[3],
        gain_sums[3],
        mlp_grads[0],
        mlp_grads[1],
        mlp_grads[2],
    )


def solution(mesh):
    in_specs = (
        P(("dp", "mp"), None),
        P(("dp", "mp"), None),
        P(),
        P(),
        P(),
        P("dp", "mp"),
        P("dp", "mp"),
        P("dp", "mp"),
        P("mp", "dp"),
        P(),
        P("dp", "mp"),
        P("dp", "mp"),
        P("mp", "dp"),
    )
    out_specs = (
        P(("dp", "mp"), None),
        P(("dp", "mp"), None),
        P(),
        P(),
        P(),
        P("dp", "mp"),
        P("dp", "mp"),
        P("dp", "mp"),
        P("mp", "dp"),
        P(),
        P("dp", "mp"),
        P("dp", "mp"),
        P("mp", "dp"),
    )
    return jax.shard_map(local, mesh=mesh, in_specs=in_specs, out_specs=out_specs, check_vma=False)
```

profile of v0, /device:TPU:0, one launch (start us, length us, event | category | flops | bytes accessed | tf_op | source)
XLA Modules:
  0.0 2250.1 jit_solution(5911992117468289806)
XLA Ops:
  20.7 15.4 all-gather.16.cloned.1.call-done
  36.1 151.8 %all-gather.12.cloned.1.call-done = bf16[2048,2048]{1,0:T(8,128)(2,1)} async-done(((bf16[512,2048]{1,0:T(8,128)(2,1)}), bf16[2048,2048]{1,0:T(8,128)(2,1)}) %all-gather.12.cloned.1.call-update) | async-done | bytes 8388624 | tf_op jit(solution)/shard_map/all_gather | solution.py:110
  203.0 13.0 all-gather.18.cloned.1.call-done
  216.0 10.5 fusion.137
  289.8 10.3 fusion.120
  300.9 279.8 %reduce-scatter.12.cloned.1.call-done = f32[512,2048]{1,0:T(8,128)} async-done(((f32[2048,2048]{1,0:T(8,128)}), f32[512,2048]{1,0:T(8,128)}) %reduce-scatter.12.cloned.1.call-update) | async-done | bytes 4194320 | tf_op jit(solution)/shard_map/reduce_scatter | solution.py:158
  589.4 39.6 %all-gather.24.cloned.1.call-done = bf16[2048,1536]{1,0:T(8,128)(2,1)} async-done(((bf16[256,1536]{1,0:T(8,128)(2,1)}), bf16[2048,1536]{1,0:T(8,128)(2,1)}) %all-gather.24.cloned.1.call-update) | async-done | bytes 6291472 | tf_op jit(solution)/shard_map/all_gather | solution.py:163
  629.0 151.9 %all-gather.22.cloned.1.call-done = bf16[2048,2048]{1,0:T(8,128)(2,1)} async-done(((bf16[512,2048]{1,0:T(8,128)(2,1)}), bf16[2048,2048]{1,0:T(8,128)(2,1)}) %all-gather.22.cloned.1.call-update) | async-done | bytes 8388624 | tf_op jit(solution)/shard_map/all_gather | solution.py:168
  780.9 19.3 fusion.138
  800.2 26.6 %all-gather.26.cloned.1.call-done = bf16[2048,1536]{1,0:T(8,128)(2,1)} async-done(((bf16[256,1536]{1,0:T(8,128)(2,1)}), bf16[2048,1536]{1,0:T(8,128)(2,1)}) %all-gather.26.cloned.1.call-update) | async-done | bytes 6291472 | tf_op jit(solution)/shard_map/all_gather | solution.py:164
  826.7 19.2 fusion.139
  846.0 29.4 %all-gather.28.cloned.1.call-done = bf16[1536,2048]{1,0:T(8,128)(2,1)} async-done(((bf16[1536,256]{1,0:T(8,128)(2,1)}), bf16[1536,2048]{1,0:T(8,128)(2,1)}) %all-gather.28.cloned.1.call-update) | async-done | bytes 6291472 | tf_op jit(solution)/shard_map/all_gather | solution.py:165
  875.3 151.3 %all-gather.30.cloned.1.call-done = bf16[2048,2048]{1,0:T(8,128)(2,1)} async-done(((bf16[512,2048]{1,0:T(8,128)(2,1)}), bf16[2048,2048]{1,0:T(8,128)(2,1)}) %all-gather.30.cloned.1.call-update) | async-done | bytes 8388624 | tf_op jit(solution)/shard_map/all_gather | solution.py:176
  1026.6 29.8 %multiply_convert_fusion = (bf16[2048,1536]{1,0:T(8,128)(2,1)}, bf16[2048,1536]{1,0:T(8,128)(2,1)}, bf16[2048,1536]{1,0:T(8,128)(2,1)}) fusion(f32[2048,1536]{1,0:T(8,128)} %fusion.138, f32[2048,1536]{1,0:T(8,128)} %fusion.139, bf16[2048,2048]{1,0:T(8,128)(2,1)} %all-gather.30.cloned.1.call-done, bf16[1536,2048]{1,0:T(8,128)(2,1)} %all-gather.28.cloned.1.call-done), kind=kOutput, calls=%fused_computation.1 | convolution fusion | flops 12935233536 | bytes 58720256 | tf_op jit(solution)/shard_map/dot_general | solution.py:67
  1056.5 19.9 fusion.140
  1076.4 23.0 %convolution_add_fusion = f32[2048,2048]{1,0:T(8,128)} fusion(f32[2048,2048]{1,0:T(8,128)} %fusion.140, bf16[2048,1536]{1,0:T(8,128)(2,1)} %get-tuple-element.29, bf16[2048,1536]{1,0:T(8,128)(2,1)} %all-gather.26.cloned.1.call-done), kind=kOutput, calls=%fused_computation.47 | convolution fusion | flops 12889096192 | bytes 46137344 | tf_op jit(solution)/shard_map/dot_general | solution.py:67
  1099.4 19.4 convolution_convert_fusion
  1118.9 259.1 %reduce-scatter.16.cloned.1.call-done = f32[512,2048]{1,0:T(8,128)} async-done(((f32[2048,2048]{1,0:T(8,128)}), f32[512,2048]{1,0:T(8,128)}) %reduce-scatter.16.cloned.1.call-update) | async-done | bytes 4194320 | tf_op jit(solution)/shard_map/reduce_scatter | solution.py:191
  1383.2 142.5 %reduce-scatter.14.cloned.1.call-done = bf16[512,2048]{1,0:T(8,128)(2,1)} async-done(((bf16[2048,2048]{1,0:T(8,128)(2,1)}), bf16[512,2048]{1,0:T(8,128)(2,1)}) %reduce-scatter.14.cloned.1.call-update) | async-done | bytes 2097168 | tf_op jit(solution)/shard_map/reduce_scatter | solution.py:172
  1532.5 19.4 convolution_convert_fusion.3
  1552.0 19.2 convolution_convert_fusion.2
  1576.7 19.1 convolution_convert_fusion.1
  1595.9 87.1 %all-gather.32.cloned.1.call-done = bf16[2048,2048]{1,0:T(8,128)(2,1)} async-done(((bf16[512,2048]{1,0:T(8,128)(2,1)}), bf16[2048,2048]{1,0:T(8,128)(2,1)}) %all-gather.32.cloned.1.call-update) | async-done | bytes 8388624 | tf_op jit(solution)/shard_map/all_gather | solution.py:210
  1817.5 10.5 convolution_convert_fusion.4
  1852.3 9.6 convolution_convert_fusion.5
  1880.0 16.1 add_convert_fusion
  1903.7 12.3 reduce-scatter.24.cloned.1.call-done
  1917.6 37.9 %reduce-scatter.22.cloned.1.call-done = bf16[256,256]{1,0:T(8,128)(2,1)} async-done(((bf16[2048,256]{1,0:T(8,128)(2,1)}), bf16[256,256]{1,0:T(8,128)(2,1)}) %reduce-scatter.22.cloned.1.call-update) | async-done | bytes 131088 | tf_op jit(solution)/shard_map/reduce_scatter | solution.py:294
  1957.2 43.1 %reduce-scatter.26.cloned.1.call-done = bf16[512,256]{1,0:T(8,128)(2,1)} async-done(((bf16[512,2048]{1,0:T(8,128)(2,1)}), bf16[512,256]{1,0:T(8,128)(2,1)}) %reduce-scatter.26.cloned.1.call-update) | async-done | bytes 262160 | tf_op jit(solution)/shard_map/reduce_scatter | solution.py:300
  2002.1 43.4 %reduce-scatter.20.cloned.1.call-done = bf16[256,512]{1,0:T(8,128)(2,1)} async-done(((bf16[2048,512]{1,0:T(8,128)(2,1)}), bf16[256,512]{1,0:T(8,128)(2,1)}) %reduce-scatter.20.cloned.1.call-update) | async-done | bytes 262160 | tf_op jit(solution)/shard_map/reduce_scatter | solution.py:291
  2047.2 145.2 %reduce-scatter.18.cloned.1.call-done = bf16[512,2048]{1,0:T(8,128)(2,1)} async-done(((bf16[2048,2048]{1,0:T(8,128)(2,1)}), bf16[512,2048]{1,0:T(8,128)(2,1)}) %reduce-scatter.18.cloned.1.call-update) | async-done | bytes 2097168 | tf_op jit(solution)/shard_map/reduce_scatter | solution.py:285
  2195.6 41.4 %all-reduce = (f32[2048]{0:T(1024)}, f32[128]{0:T(128)}, f32[128]{0:T(128)}, f32[2048]{0:T(1024)}) all-reduce(f32[2048]{0:T(1024)S(1)} %get-tuple-element.15, f32[128]{0:T(128)S(1)} %bitcast_reduce_fusion, f32[128]{0:T(128)S(1)} %bitcast_reduce_fusion.1, f32[2048]{0:T(1024)S(1)} %copy-done.78), channel_id=1, replica_groups=mesh['dp'=8,'mp'=4] {'dp','mp'}, use_global_device_ids=true, to_apply=%region_25.26 | all-reduce | flops 4352 | bytes 34816 | tf_op jit(solution)/shard_map/psum | solution.py:304
  (393 shorter events, 317.9 us)
Async XLA Ops:
  7.2 28.9 %all-gather.16.cloned.1.call-start = ((), (), s32[]{:S(2)}) async-start(), calls=%async_computation.13 | async-start | bytes 1179648 | tf_op jit(solution)/shard_map/all_gather | solution.py:105
  7.9 180.0 %all-gather.12.cloned.1.call-start = ((), (), s32[]{:S(2)}) async-start(), calls=%async_computation.11 | async-start | bytes 10485760 | tf_op jit(solution)/shard_map/all_gather | solution.py:110
  14.7 201.3 %all-gather.18.cloned.1.call-start = ((), (), s32[]{:S(2)}) async-start(), calls=%async_computation.14 | async-start | bytes 2359296 | tf_op jit(solution)/shard_map/all_gather | solution.py:104
  15.4 240.5 %all-gather.14.cloned.1.call-start = ((), (), s32[]{:S(2)}) async-start(), calls=%async_computation.12 | async-start | bytes 1179648 | tf_op jit(solution)/shard_map/all_gather | solution.py:106
  16.0 273.8 %all-gather.20.cloned.1.call-start = ((), (), s32[]{:S(2)}) async-start(), calls=%async_computation.15 | async-start | bytes 2359296 | tf_op jit(solution)/shard_map/all_gather | solution.py:107
  16.6 564.1 %reduce-scatter.12.cloned.1.call-start = ((), (), s32[]{:S(2)}) async-start(), calls=%async_computation.16 | async-start | bytes 20971520 | tf_op jit(solution)/shard_map/reduce_scatter | solution.py:158
  300.1 280.6 %copy-start.10 = (bf16[512,2048]{1,0:T(8,128)(2,1)S(1)}, bf16[512,2048]{1,0:T(8,128)(2,1)}, u32[]{:S(2)}) copy-start(bf16[512,2048]{1,0:T(8,128)(2,1)} %param.13) | copy-start | bytes 6291460
  300.1 328.9 %all-gather.24.cloned.1.call-start = ((), (), s32[]{:S(2)}) async-start(), calls=%async_computation.18 | async-start | bytes 7077888 | tf_op jit(solution)/shard_map/all_gather | solution.py:163
  300.9 284.7 %copy-start.56 = (f32[2048]{0:T(1024)S(1)}, f32[2048]{0:T(1024)}, u32[]{:S(2)}) copy-start(f32[2048]{0:T(1024)} %param.22) | copy-start | bytes 24580
  300.9 480.0 %all-gather.22.cloned.1.call-start = ((), (), s32[]{:S(2)}) async-start(), calls=%async_computation.17 | async-start | bytes 10485760 | tf_op jit(solution)/shard_map/all_gather | solution.py:168
  587.3 239.4 %all-gather.26.cloned.1.call-start = ((), (), s32[]{:S(2)}) async-start(), calls=%async_computation.19 | async-start | bytes 7077888 | tf_op jit(solution)/shard_map/all_gather | solution.py:164
  588.0 287.3 %all-gather.28.cloned.1.call-start = ((), (), s32[]{:S(2)}) async-start(), calls=%async_computation.20 | async-start | bytes 7077888 | tf_op jit(solution)/shard_map/all_gather | solution.py:165
  588.6 438.0 %all-gather.30.cloned.1.call-start = ((), (), s32[]{:S(2)}) async-start(), calls=%async_computation.22 | async-start | bytes 10485760 | tf_op jit(solution)/shard_map/all_gather | solution.py:176
  589.4 788.7 %reduce-scatter.16.cloned.1.call-start = ((), (), s32[]{:S(2)}) async-start(), calls=%async_computation.23 | async-start | bytes 20971520 | tf_op jit(solution)/shard_map/reduce_scatter | solution.py:191
  1099.4 426.3 %reduce-scatter.14.cloned.1.call-start = ((), (), s32[]{:S(2)}) async-start(), calls=%async_computation.21 | async-start | bytes 10485760 | tf_op jit(solution)/shard_map/reduce_scatter | solution.py:172
  1118.8 259.3 %copy-start.80 = (f32[512]{0:T(512)S(1)}, f32[512]{0:T(512)}, u32[]{:S(2)}) copy-start(f32[512]{0:T(512)} %copy-done.79) | copy-start | bytes 6148
  1118.8 406.8 %copy-start.31 = (bf16[512,2048]{1,0:T(8,128)(2,1)S(1)}, bf16[512,2048]{1,0:T(8,128)(2,1)}, u32[]{:S(2)}) copy-start(bf16[512,2048]{1,0:T(8,128)(2,1)} %param.14) | copy-start | bytes 6291460
  1118.8 406.8 %copy-start.81 = (f32[512]{0:T(512)S(1)}, f32[512]{0:T(512)}, u32[]{:S(2)}) copy-start(f32[512]{0:T(512)} %get-tuple-element.59) | copy-start | bytes 6148
  1118.9 564.1 %all-gather.32.cloned.1.call-start = ((), (), s32[]{:S(2)}) async-start(), calls=%async_computation.24 | async-start | bytes 10485760 | tf_op jit(solution)/shard_map/all_gather | solution.py:210
  1532.4 363.7 %reduce-scatter.28.cloned.1.call-start = ((), (), s32[]{:S(2)}) async-start(), calls=%async_computation.30 | async-start | bytes 7077888 | tf_op jit(solution)/shard_map/reduce_scatter | solution.py:200
  1551.9 346.8 %reduce-scatter.30.cloned.1.call-start = ((), (), s32[]{:S(2)}) async-start(), calls=%async_computation.31 | async-start | bytes 7077888 | tf_op jit(solution)/shard_map/reduce_scatter | solution.py:203
  1571.3 329.9 %reduce-scatter.32.cloned.1.call-start = ((), (), s32[]{:S(2)}) async-start(), calls=%async_computation.32 | async-start | bytes 7077888 | tf_op jit(solution)/shard_map/reduce_scatter | solution.py:206
  1595.8 320.2 %reduce-scatter.24.cloned.1.call-start = ((), (), s32[]{:S(2)}) async-start(), calls=%async_computation.28 | async-start | bytes 1179648 | tf_op jit(solution)/shard_map/reduce_scatter | solution.py:297
  1795.7 159.9 %reduce-scatter.22.cloned.1.call-start = ((), (), s32[]{:S(2)}) async-start(), calls=%async_computation.27 | async-start | bytes 1179648 | tf_op jit(solution)/shard_map/reduce_scatter | solution.py:294
  1813.9 186.4 %reduce-scatter.26.cloned.1.call-start = ((), (), s32[]{:S(2)}) async-start(), calls=%async_computation.29 | async-start | bytes 2359296 | tf_op jit(solution)/shard_map/reduce_scatter | solution.py:300
  1828.0 217.4 %reduce-scatter.20.cloned.1.call-start = ((), (), s32[]{:S(2)}) async-start(), calls=%async_computation.26 | async-start | bytes 2359296 | tf_op jit(solution)/shard_map/reduce_scatter | solution.py:291
  1861.9 330.5 %reduce-scatter.18.cloned.1.call-start = ((), (), s32[]{:S(2)}) async-start(), calls=%async_computation.25 | async-start | bytes 10485760 | tf_op jit(solution)/shard_map/reduce_scatter | solution.py:285
  1896.1 296.3 %copy-start.11 = (bf16[512,2048]{1,0:T(8,128)(2,1)S(1)}, bf16[512,2048]{1,0:T(8,128)(2,1)}, u32[]{:S(2)}) copy-start(bf16[512,2048]{1,0:T(8,128)(2,1)} %param.13) | copy-start | bytes 6291460
  1896.1 296.3 %copy-start.58 = (f32[2048]{0:T(1024)S(1)}, f32[2048]{0:T(1024)}, u32[]{:S(2)}) copy-start(f32[2048]{0:T(1024)} %param.15) | copy-start | bytes 24580
  1896.2 296.3 %copy-start.67 = (f32[512]{0:T(512)S(1)}, f32[512]{0:T(512)}, u32[]{:S(2)}) copy-start(f32[512]{0:T(512)} %copy-done.66) | copy-start | bytes 6148
  1901.3 294.3 %copy-start.78 = (f32[2048]{0:T(1024)S(1)}, f32[2048]{0:T(1024)}, u32[]{:S(2)}) copy-start(f32[2048]{0:T(1024)} %get-tuple-element.13) | copy-start | bytes 24580
  1901.3 335.7 %copy-start.83 = (f32[512]{0:T(512)S(1)}, f32[512]{0:T(512)}, u32[]{:S(2)}) copy-start(f32[512]{0:T(512)} %get-tuple-element.57) | copy-start | bytes 6148
  (100 other events, 1308.6 us)
Sparse Core Ops, SparseCore 0:
  9.9 26.1 all-gather.15
  38.3 149.6 all-gather.11
  189.8 26.1 all-gather.17
  217.7 23.4 all-gather.13
  243.0 28.1 all-gather.19
  300.2 280.4 reduce-scatter.11
  582.7 46.2 all-gather.23
  631.2 149.6 all-gather.21
  782.9 43.7 all-gather.25
  828.6 46.6 all-gather.27
  877.0 149.6 all-gather.29
  1099.5 278.5 reduce-scatter.15
  1380.4 145.1 reduce-scatter.13
  1532.6 150.3 all-gather.31
  1686.2 59.9 reduce-scatter.27
  1749.8 61.7 reduce-scatter.29
  1814.8 61.7 reduce-scatter.31
  1879.9 36.0 reduce-scatter.23
  1919.5 36.0 reduce-scatter.21
  1959.0 41.2 reduce-scatter.25
  2004.2 41.2 reduce-scatter.19
  2047.9 144.4 reduce-scatter.17
where the time goes:
time: 2260 us; the launch traced here: 2250 us
  waiting for transfers between devices  1630 us (72%)
  matrix products  371 us (16%)
  other arithmetic  122 us (5%)
  local copies, waits for them, and re-layouts  63.5 us (3%)
  blocking collectives  41.4 us (2%)
    reduce_scatter x1, waiting for transfers between devices, local(): lax.psum_scatter(matmul(attended, output_full), 'mp', scatter_dimension=0...  280 us
    reduce_scatter x1, waiting for transfers between devices, local(): lax.psum_scatter(dot_last(gate_grad, gate_back) + dot_last(up_grad, up_ba...  259 us
    all_gather x1, waiting for transfers between devices, local(): lax.all_gather(normed_two.astype(jnp.bfloat16), 'mp', axis=0, tiled=True)  152 us
    all_gather x1, waiting for transfers between devices, local(): lax.all_gather(first_normed.astype(jnp.bfloat16), 'mp', axis=0, tiled=True)  152 us
    all_gather x1, waiting for transfers between devices, local(): grad_rows = lax.all_gather(out_grad, 'mp', axis=0, tiled=True)  151 us
    reduce_scatter x1, waiting for transfers between devices, local(): lax.psum_scatter(one_partial.astype(jnp.bfloat16), 'mp', scatter_dimensio...  145 us
    reduce_scatter x1, waiting for transfers between devices, local(): lax.psum_scatter(matmul(hidden_low, down_full).astype(jnp.bfloat16), 'mp'...  142 us
    dot_general x7, matrix products, dot_last(): lax.dot_general(left, right, (((1,), (1,)), ((), ())), preferred_element_...  116 us
  transfers between devices with their start and end apart: 22, of which 17 were waited for; matrix products, arithmetic and copies ran while one was open for 20% of the time, Pallas kernels for 0%

commit v1 on v0

--- a/solution.py
+++ b/solution.py
@@ -1,6 +1,10 @@
+import functools
+
 import jax
 import jax.numpy as jnp
 from jax import lax
+from jax.experimental import pallas as pl
+from jax.experimental.pallas import tpu as pltpu
 from jax.sharding import PartitionSpec as P
 
 HEAD_SIZE = 128
@@ -84,7 +88,7 @@
     return jnp.where(key_places <= query_places, raw, -jnp.inf)
 
 
-def local(
+def generic(
     layer_input,
     out_grad,
     norm_attn,
@@ -321,6 +325,854 @@
     )
 
 
+ROW_BLOCK = 256
+
+
+def wide_tables(length):
+    cosine_table, sine_table = tables(length, HEAD_SIZE)
+    return (
+        jnp.concatenate([cosine_table, cosine_table], 1),
+        jnp.concatenate([-sine_table, sine_table], 1),
+    )
+
+
+def turn(values, cosines, sines):
+    return values * cosines + pltpu.roll(values, HEAD_SIZE // 2, 1) * sines
+
+
+def turn_back(values, cosines, sines):
+    return values * cosines - pltpu.roll(values, HEAD_SIZE // 2, 1) * sines
+
+
+def causal(rows):
+    query_places = lax.broadcasted_iota(jnp.int32, (rows, rows), 0)
+    key_places = lax.broadcasted_iota(jnp.int32, (rows, rows), 1)
+    return key_places <= query_places
+
+
+def attend_kernel(
+    core, own, other, w0, w1, w2, w3_low, w3_high, cosines, sines, query_gain, key_gain,
+    proj, query_rot, key_rot, value, attended, log_total,
+):
+    half = own.shape[0]
+    length = 2 * half
+    scale = HEAD_SIZE ** (-0.5)
+    query_cols = query_rot.shape[1]
+    heads = query_cols // HEAD_SIZE
+    for h in range(2):
+        here = core[0] == h
+        rows = slice(h * half, (h + 1) * half)
+        block = None
+        start = 0
+        for weight in (w0, w1, w2, w3_low, w3_high):
+            cols = slice(start, start + weight.shape[0])
+            start = cols.stop
+            tokens = jnp.where(here, own[:, cols], other[:, cols])
+            term = matmul(tokens, weight[...])
+            block = term if block is None else block + term
+        proj[rows, :] = block
+        cos_rows, sin_rows = cosines[rows, :], sines[rows, :]
+        for head in range(heads):
+            cols = slice(head * HEAD_SIZE, (head + 1) * HEAD_SIZE)
+            normed, _ = norm_rows(block[:, cols], query_gain[...])
+            query_rot[rows, cols] = turn(normed, cos_rows, sin_rows).astype(jnp.bfloat16)
+        cols = slice(query_cols, query_cols + HEAD_SIZE)
+        normed, _ = norm_rows(block[:, cols], key_gain[...])
+        key_rot[rows, :] = turn(normed, cos_rows, sin_rows).astype(jnp.bfloat16)
+        value[rows, :] = block[:, query_cols + HEAD_SIZE :].astype(jnp.bfloat16)
+    allowed = causal(ROW_BLOCK)
+
+    def place(start):
+        return pl.ds(pl.multiple_of((start + core[0] * half) % length, ROW_BLOCK), ROW_BLOCK)
+
+    lane = lax.broadcasted_iota(jnp.int32, (ROW_BLOCK, HEAD_SIZE), 1)
+    for start in range(0, length, ROW_BLOCK):
+        rows = slice(start, start + ROW_BLOCK)
+        logs = jnp.zeros((ROW_BLOCK, HEAD_SIZE), jnp.float32)
+        for head in range(heads):
+            cols = slice(head * HEAD_SIZE, (head + 1) * HEAD_SIZE)
+            query = query_rot[rows, cols]
+            scores = [jnp.where(allowed, dot_last(query, key_rot[rows, :]) * scale, -jnp.inf)]
+            if start:
+                scores.append(dot_last(query, key_rot[:start, :]) * scale)
+            largest = functools.reduce(
+                jnp.maximum, [jnp.max(s, -1, keepdims=True) for s in scores]
+            )
+            expanded = [jnp.exp(s - largest) for s in scores]
+            summed = sum(jnp.sum(e, -1, keepdims=True) for e in expanded)
+            out = matmul(expanded[0].astype(jnp.bfloat16), value[rows, :])
+            if start:
+                out = out + matmul(expanded[1].astype(jnp.bfloat16), value[:start, :])
+            attended[place(start), cols] = (out / summed).astype(jnp.bfloat16)
+            logs = jnp.where(lane == head, largest + jnp.log(summed), logs)
+        log_total[rows, :] = logs
+
+
+def attend(core, own, other, weights, cosines, sines, query_gain, key_gain, planes, query_cols):
+    half, width = own.shape
+    length = 2 * half
+    cols = weights[0].shape[1]
+    group = cols // planes
+    whole = lambda shape: pl.BlockSpec(shape, lambda g, core: (0, 0))
+    column = lambda rows, width: pl.BlockSpec((rows, width), lambda g, core: (0, g))
+    shape = jax.ShapeDtypeStruct
+    return pl.pallas_call(
+        attend_kernel,
+        grid_spec=pltpu.PrefetchScalarGridSpec(
+            num_scalar_prefetch=1,
+            grid=(planes,),
+            in_specs=[whole((half, width))] * 2
+            + [column(weight.shape[0], group) for weight in weights]
+            + [whole((length, HEAD_SIZE))] * 2
+            + [whole((1, HEAD_SIZE))] * 2,
+            out_specs=[
+                column(length, group),
+                column(length, query_cols),
+                column(length, HEAD_SIZE),
+                column(length, HEAD_SIZE),
+                column(length, query_cols),
+                column(length, HEAD_SIZE),
+            ],
+        ),
+        out_shape=[
+            shape((length, cols), jnp.float32),
+            shape((length, planes * query_cols), jnp.bfloat16),
+            shape((length, planes * HEAD_SIZE), jnp.bfloat16),
+            shape((length, planes * HEAD_SIZE), jnp.bfloat16),
+            shape((length, planes * query_cols), jnp.bfloat16),
+            shape((length, planes * HEAD_SIZE), jnp.float32),
+        ],
+        compiler_params=pltpu.CompilerParams(vmem_limit_bytes=56 * 2**20),
+        cost_estimate=pl.CostEstimate(
+            flops=2 * length * width * cols + 3 * planes * query_cols * length**2,
+            bytes_accessed=30 * 2**20,
+            transcendentals=planes * 2 * length**2,
+        ),
+    )(core, own, other, *weights, cosines, sines, query_gain, key_gain)
+
+
+def attend_back_kernel(
+    core, own, other, o0, o1, o2, o3_low, o3_high, cosines, sines, query_gain, key_gain,
+    proj, query_rot, key_rot, value, log_total,
+    proj_grad, gain_grads, grad, key_total, value_total,
+):
+    half = own.shape[0]
+    length = 2 * half
+    part = o0.shape[1]
+    scale = HEAD_SIZE ** (-0.5)
+    query_cols = query_rot.shape[1]
+    heads = query_cols // HEAD_SIZE
+
+    @pl.when(pl.program_id(0) == 0)
+    def _():
+        gain_grads[...] = jnp.zeros_like(gain_grads)
+
+    low = pl.program_id(0) < pl.num_programs(0) // 2
+    corner = jnp.where(low, o3_low[...], o3_high[...])
+    for h in range(2):
+        here = core[0] == h
+        block = None
+        for k, weight in enumerate((o0[...], o1[...], o2[...], corner)):
+            cols = slice(k * part, (k + 1) * part)
+            tokens = jnp.where(here, own[:, cols], other[:, cols])
+            term = dot_last(tokens, weight)
+            block = term if block is None else block + term
+        grad[h * half : (h + 1) * half, :] = block.astype(jnp.bfloat16)
+    key_total[...] = jnp.zeros_like(key_total)
+    value_total[...] = jnp.zeros_like(value_total)
+    allowed = causal(ROW_BLOCK)
+
+    def fold(values):
+        return jnp.sum(values.reshape(-1, 8, HEAD_SIZE), 0)
+
+    def place(start):
+        return pl.ds(pl.multiple_of((start + core[0] * half) % length, ROW_BLOCK), ROW_BLOCK)
+
+    for start in range(0, length, ROW_BLOCK):
+        rows = slice(start, start + ROW_BLOCK)
+        for head in range(heads):
+            cols = slice(head * HEAD_SIZE, (head + 1) * HEAD_SIZE)
+            query = query_rot[rows, cols]
+            upstream = grad[rows, cols]
+            logs = log_total[rows, head : head + 1]
+            spans = [rows] + ([slice(0, start)] if start else [])
+            probs, prob_grads = [], []
+            for n, span in enumerate(spans):
+                raw = dot_last(query, key_rot[span, :]) * scale
+                if n == 0:
+                    raw = jnp.where(allowed, raw, -jnp.inf)
+                probs.append(jnp.exp(raw - logs))
+                prob_grads.append(dot_last(upstream, value[span, :]))
+            inner = sum(jnp.sum(p * d, -1, keepdims=True) for p, d in zip(probs, prob_grads))
+            query_back = None
+            for span, p, d in zip(spans, probs, prob_grads):
+                score_grad = (p * (d - inner)).astype(jnp.bfloat16)
+                term = matmul(score_grad, key_rot[span, :])
+                query_back = term if query_back is None else query_back + term
+                key_total[span, :] += dot_first(score_grad, query)
+                value_total[span, :] += dot_first(p.astype(jnp.bfloat16), upstream)
+            normed_grad = turn_back(query_back * scale, cosines[rows, :], sines[rows, :])
+            values = proj[rows, cols]
+            _, factor = norm_rows(values, query_gain[...])
+            gain_grads[:8, :] += fold(normed_grad * values * factor)
+            back = norm_back(values, factor, query_gain[...], normed_grad)
+            proj_grad[place(start), cols] = back.astype(jnp.bfloat16)
+    for start in range(0, length, ROW_BLOCK):
+        rows = slice(start, start + ROW_BLOCK)
+        cols = slice(query_cols, query_cols + HEAD_SIZE)
+        normed_grad = turn_back(key_total[rows, :] * scale, cosines[rows, :], sines[rows, :])
+        values = proj[rows, cols]
+        _, factor = norm_rows(values, key_gain[...])
+        gain_grads[8:, :] += fold(normed_grad * values * factor)
+        back = norm_back(values, factor, key_gain[...], normed_grad)
+        proj_grad[place(start), cols] = back.astype(jnp.bfloat16)
+        proj_grad[place(start), query_cols + HEAD_SIZE :] = value_total[rows, :].astype(
+            jnp.bfloat16
+        )
+
+
+def attend_back(
+    core, own, other, weights, cosines, sines, query_gain, key_gain, saved, planes, query_cols
+):
+    half, width = own.shape
+    length = 2 * half
+    part = weights[0].shape[1]
+    proj, query_rot, key_rot, value, log_total = saved
+    cols = proj.shape[1]
+    group = cols // planes
+    whole = lambda shape: pl.BlockSpec(shape, lambda g, core: (0, 0))
+    column = lambda rows, width: pl.BlockSpec((rows, width), lambda g, core: (0, g))
+    shape = jax.ShapeDtypeStruct
+    return pl.pallas_call(
+        attend_back_kernel,
+        grid_spec=pltpu.PrefetchScalarGridSpec(
+            num_scalar_prefetch=1,
+            grid=(planes,),
+            in_specs=[whole((half, width))] * 2
+            + [pl.BlockSpec((query_cols, part), lambda g, core: (g, 0))] * 3
+            + [
+                pl.BlockSpec((query_cols, part), lambda g, core: (jnp.minimum(g, 1), 0)),
+                pl.BlockSpec((query_cols, part), lambda g, core: (jnp.maximum(g - 2, 0), 0)),
+            ]
+            + [whole((length, HEAD_SIZE))] * 2
+            + [whole((1, HEAD_SIZE))] * 2
+            + [
+                column(length, group),
+                column(length, query_cols),
+                column(length, HEAD_SIZE),
+                column(length, HEAD_SIZE),
+                column(length, HEAD_SIZE),
+            ],
+            out_specs=[column(length, group), whole((16, HEAD_SIZE))],
+            scratch_shapes=[
+                pltpu.VMEM((length, query_cols), jnp.bfloat16),
+                pltpu.VMEM((length, HEAD_SIZE), jnp.float32),
+                pltpu.VMEM((length, HEAD_SIZE), jnp.float32),
+            ],
+        ),
+        out_shape=[
+            shape((length, cols), jnp.bfloat16),
+            shape((16, HEAD_SIZE), jnp.float32),
+        ],
+        compiler_params=pltpu.CompilerParams(vmem_limit_bytes=56 * 2**20),
+        cost_estimate=pl.CostEstimate(
+            flops=length * width * cols + 8 * planes * query_cols * length**2,
+            bytes_accessed=30 * 2**20,
+            transcendentals=planes * 2 * length**2,
+        ),
+    )(core, own, other, *weights, cosines, sines, query_gain, key_gain, *saved)
+
+
+def feed_kernel(*refs):
+    token_tiles, grad_tiles = refs[:4], refs[4:8]
+    gate_up, down = refs[8:10]
+    all_tokens, all_grads, all_hidden, all_gate, all_up = refs[-13:-8]
+    out_tiles, two_tiles = refs[-8:-4], refs[-4:]
+    step = pl.program_id(0)
+    units = down.shape[1]
+    width = down.shape[2]
+    hidden_count = down.shape[0] * units
+    gate_t = gate_up[:, :units, :].reshape(hidden_count, width)
+    up_t = gate_up[:, units:, :].reshape(hidden_count, width)
+    down_t = down[...].reshape(hidden_count, width)
+
+    def select(tiles):
+        low = jnp.where(step == 0, tiles[0][...], tiles[1][...])
+        high = jnp.where(step == 2, tiles[2][...], tiles[3][...])
+        return jnp.where(step < 2, low, high)
+
+    all_tokens[...] = select(token_tiles)
+    all_grads[...] = select(grad_tiles)
+    tokens = all_tokens[...]
+    grads = all_grads[...]
+    for start in range(0, hidden_count, 256):
+        cols = slice(start, start + 256)
+        gate = dot_last(tokens, gate_t[cols])
+        up = dot_last(tokens, up_t[cols])
+        hidden_grad = dot_last(grads, down_t[cols])
+        sigmoid_gate = 1.0 / (1.0 + jnp.exp(-gate))
+        silu = gate * sigmoid_gate
+        all_hidden[:, cols] = (silu * up).astype(jnp.bfloat16)
+        all_gate[:, cols] = (
+            hidden_grad * up * sigmoid_gate * (1.0 + gate * (1.0 - sigmoid_gate))
+        ).astype(jnp.bfloat16)
+        all_up[:, cols] = (hidden_grad * silu).astype(jnp.bfloat16)
+    hidden, gate_grad, up_grad = all_hidden[...], all_gate[...], all_up[...]
+    for start in range(0, width, 512):
+        cols = slice(start, start + 512)
+        out = matmul(hidden, down_t[:, cols]).astype(jnp.bfloat16)
+        two = (matmul(gate_grad, gate_t[:, cols]) + matmul(up_grad, up_t[:, cols])).astype(
+            jnp.bfloat16
+        )
+        for tile in range(4):
+
+            @pl.when(step == tile)
+            def _():
+                out_tiles[tile][:, cols] = out
+                two_tiles[tile][:, cols] = two
+
+
+def feed(index, earlier, tokens, grads, gate_up, down):
+    tile, width = 256, gate_up.shape[2]
+    hidden_count = down.shape[0] * down.shape[1]
+    count = 16 * tile
+    placed = lambda t: (index * 4 + t, 0)
+    spec = pl.BlockSpec
+    shape = jax.ShapeDtypeStruct
+    kept = [] if earlier is None else list(earlier)
+    once = pl.Buffered(1)
+    blocks = [
+        spec((tile, width), lambda t, row=row: (row, 0), pipeline_mode=once)
+        for _, row in tokens + grads
+    ]
+    return pl.pallas_call(
+        feed_kernel,
+        grid=(4,),
+        in_specs=blocks
+        + [
+            spec(gate_up.shape, lambda t: (0, 0, 0), pipeline_mode=once),
+            spec(down.shape, lambda t: (0, 0, 0), pipeline_mode=once),
+        ]
+        + [spec(memory_space=pl.ANY)] * len(kept),
+        out_specs=[spec((tile, width), placed)] * 2
+        + [spec((tile, hidden_count), placed)] * 3
+        + [spec((tile, width), lambda t: (0, 0))] * 8,
+        out_shape=[shape((count, width), jnp.bfloat16)] * 2
+        + [shape((count, hidden_count), jnp.bfloat16)] * 3
+        + [shape((tile, width), jnp.bfloat16)] * 8,
+        input_output_aliases={10 + k: k for k in range(len(kept))},
+        compiler_params=pltpu.CompilerParams(vmem_limit_bytes=60 * 2**20),
+        cost_estimate=pl.CostEstimate(
+            flops=48 * tile * width * hidden_count,
+            bytes_accessed=40 * 2**20,
+            transcendentals=4 * tile * hidden_count,
+        ),
+    )(*[array for array, _ in tokens + grads], gate_up, down, *kept)
+
+
+def columns_kernel(transposed, place, left, w0, w1, w2, w3_low, w3_high, own, other):
+    rows = own.shape[0]
+
+    def write(lines, result):
+        for ref, kind in ((own, jnp.float32), (other, jnp.bfloat16)):
+            start = 0 if ref is own else rows
+            ref[...] = result(lines[start : start + rows]).astype(kind)
+
+    for k, weight in enumerate((w0, w1, w2)):
+
+        @pl.when(pl.program_id(0) == k)
+        def _():
+            step = dot_last if transposed else matmul
+            write(left, lambda lines: step(lines, weight[...]))
+
+    @pl.when(pl.program_id(0) == 3)
+    def _():
+        if transposed:
+            write(
+                left,
+                lambda lines: jnp.concatenate(
+                    [dot_last(lines, w3_low[...]), dot_last(lines, w3_high[...])], 1
+                ),
+            )
+        else:
+            middle = w3_low.shape[0]
+            write(
+                left,
+                lambda lines: matmul(lines[:, :middle], w3_low[...])
+                + matmul(lines[:, middle:], w3_high[...]),
+            )
+
+
+def columns(place, left, weights, transposed):
+    length, depth = left.shape
+    rows = length // 2
+    part = weights[0].shape[0 if transposed else 1]
+    width = 4 * part
+    whole = lambda array: pl.BlockSpec(array.shape, lambda k, place: (0, 0))
+    block = pl.BlockSpec((rows, part), lambda k, place: (0, k ^ place[0]))
+    shape = jax.ShapeDtypeStruct
+    return pl.pallas_call(
+        functools.partial(columns_kernel, transposed),
+        grid_spec=pltpu.PrefetchScalarGridSpec(
+            num_scalar_prefetch=1,
+            grid=(4,),
+            in_specs=[whole(array) for array in (left, *weights)],
+            out_specs=[block, block],
+        ),
+        out_shape=[shape((rows, width), jnp.float32), shape((rows, width), jnp.bfloat16)],
+        compiler_params=pltpu.CompilerParams(vmem_limit_bytes=56 * 2**20),
+        cost_estimate=pl.CostEstimate(
+            flops=2 * length * depth * width, bytes_accessed=20 * 2**20, transcendentals=0
+        ),
+    )(place, left, *weights)
+
+
+def tile_call(kernel, place, ins, outs, kept):
+    width = 2048
+    tile = 256
+
+    def spec(cut, columns):
+        if cut == "rows":
+            return pl.BlockSpec((tile, columns), lambda t, place: (t, 0))
+        if cut == "low" or cut == "high":
+            return pl.BlockSpec((tile, columns), lambda t, place: (0, 0))
+        return pl.BlockSpec((cut, columns), lambda t, place: (0, 0))
+
+    return pl.pallas_call(
+        kernel,
+        grid_spec=pltpu.PrefetchScalarGridSpec(
+            num_scalar_prefetch=1,
+            grid=(2,),
+            in_specs=[spec(cut, array.shape[1]) for array, cut in ins],
+            out_specs=[spec(cut, shape.shape[1]) for shape, cut in outs],
+        ),
+        out_shape=[shape for shape, _ in outs],
+        compiler_params=pltpu.CompilerParams(vmem_limit_bytes=56 * 2**20),
+        cost_estimate=pl.CostEstimate(
+            flops=20 * 2**20, bytes_accessed=kept * 2**20, transcendentals=0
+        ),
+    )(place, *[array for array, _ in ins])
+
+
+def put(low_ref, high_ref, values):
+    first = pl.program_id(0) == 0
+
+    @pl.when(first)
+    def _():
+        low_ref[...] = values
+
+    @pl.when(jnp.logical_not(first))
+    def _():
+        high_ref[...] = values
+
+
+def choose(low_ref, high_ref):
+    return jnp.where(pl.program_id(0) == 0, low_ref[...], high_ref[...]).astype(jnp.float32)
+
+
+def add_gain(gain_ref, values):
+    @pl.when(pl.program_id(0) == 0)
+    def _():
+        gain_ref[...] = jnp.zeros_like(gain_ref)
+
+    gain_ref[...] += jnp.sum(values.reshape(-1, 8, values.shape[1]), 0)
+
+
+def relabelled(ref, values, place):
+    width = values.shape[1] // 4
+    for k in range(4):
+        start = pl.multiple_of((place[0] ^ k) * width, width)
+        ref[:, pl.ds(start, width)] = values[:, k * width : (k + 1) * width]
+
+
+def first_norm_kernel(place, inputs, gain, normed):
+    values, _ = norm_rows(inputs[...].astype(jnp.float32), gain[...])
+    relabelled(normed, values.astype(jnp.bfloat16), place)
+
+
+def middle_kernel(place, inputs, own, other, gain, middle, low, high):
+    values = inputs[...].astype(jnp.float32) + own[...] + other[...].astype(jnp.float32)
+    middle[...] = values
+    put(low, high, norm_rows(values, gain[...])[0].astype(jnp.bfloat16))
+
+
+def middle_back_kernel(
+    place, middle, cotangent, own_low, own_high, x_low, x_high, y_low, y_high, gain,
+    middle_grad, branch, gain_grad,
+):
+    two_grad = choose(own_low, own_high) + choose(x_low, x_high) + choose(y_low, y_high)
+    values = middle[...]
+    _, factor = norm_rows(values, gain[...])
+    add_gain(gain_grad, two_grad * values * factor)
+    grads = cotangent[...].astype(jnp.float32) + norm_back(values, factor, gain[...], two_grad)
+    middle_grad[...] = grads
+    relabelled(branch, grads.astype(jnp.bfloat16), place)
+
+
+def input_back_kernel(
+    place, inputs, middle_grad, own, other, gain, input_grad, rounded, gain_grad
+):
+    one_grad = own[...] + other[...].astype(jnp.float32)
+    values = inputs[...].astype(jnp.float32)
+    _, factor = norm_rows(values, gain[...])
+    add_gain(gain_grad, one_grad * values * factor)
+    grads = middle_grad[...] + norm_back(values, factor, gain[...], one_grad)
+    input_grad[...] = grads
+    rounded[...] = grads.astype(jnp.bfloat16)
+
+
+def output_kernel(
+    place, middle, own_low, own_high, x_low, x_high, y_low, y_high, output
+):
+    total_out = choose(own_low, own_high) + choose(x_low, x_high) + choose(y_low, y_high)
+    output[...] = (middle[...] + total_out).astype(jnp.bfloat16)
+
+
+def exchange(values, bit):
+    return lax.ppermute(values, "dp", [(i, i ^ bit) for i in range(8)])
+
+
+def swap_halves(values):
+    pairs = []
+    for i in range(8):
+        for m in range(4):
+            if (i & 1) != (m & 1):
+                pairs.append((i * 4 + m, (i ^ 1) * 4 + (m ^ 1)))
+    return lax.ppermute(values, ("dp", "mp"), pairs)
+
+
+def after(values, earlier):
+    return lax.optimization_barrier((values, earlier))[0]
+
+
+def gather_weights(block):
+    half = block.shape[0] // 2
+    over_x = exchange(block, 2)
+    over_y = exchange(block, 4)
+    return [
+        block,
+        over_x,
+        over_y,
+        exchange(over_x[:half], 4),
+        exchange(over_y[half:], 2),
+    ]
+
+
+def gather_near(low, high):
+    return [exchange(low, 2), exchange(high, 2), exchange(low, 4), exchange(high, 4)]
+
+
+def gather_far(near):
+    return [exchange(near[0], 4), exchange(near[3], 2)]
+
+
+def both_cores(halves):
+    return list(halves) + [exchange(half, 1) for half in halves]
+
+
+def add_low(left, right):
+    return (left.astype(jnp.float32) + right.astype(jnp.float32)).astype(jnp.bfloat16)
+
+
+def pick(values, index, width, axis):
+    return lax.dynamic_slice_in_dim(values, index * width, width, axis)
+
+
+def in_order(own, other, core, axis=0):
+    return jnp.where(
+        core == 0,
+        jnp.concatenate([own, other], axis),
+        jnp.concatenate([other, own], axis),
+    )
+
+
+def total(values):
+    for bit in (1, 2, 4):
+        values = values + exchange(values, bit)
+    for bit in (1, 2):
+        values = values + lax.ppermute(values, "mp", [(i, i ^ bit) for i in range(4)])
+    return values
+
+
+def fast(
+    layer_input,
+    out_grad,
+    norm_attn,
+    query_norm,
+    key_norm,
+    w_query,
+    key_matrix,
+    value_matrix,
+    w_output,
+    norm_mlp,
+    w_gate,
+    w_up,
+    w_down,
+):
+    bf16, f32 = jnp.bfloat16, jnp.float32
+    device = lax.axis_index("dp")
+    core = device & 1
+    place = jnp.reshape(device >> 1, (1,)).astype(jnp.int32)
+    core_index = jnp.reshape(core, (1,)).astype(jnp.int32)
+    crossing = core != (lax.axis_index("mp") & 1)
+    planes = 4
+    rows = layer_input.shape[0]
+    width = layer_input.shape[1]
+    units = w_gate.shape[1] // 8
+    array = jax.ShapeDtypeStruct
+
+    query_cols = w_query.shape[1] // 2
+    key_cols = key_matrix.shape[1] // 2
+
+    def heads_of(which):
+        return jnp.concatenate(
+            [
+                pick(w_query, which, query_cols, 1),
+                pick(key_matrix, which, key_cols, 1),
+                pick(value_matrix, which, key_cols, 1),
+            ],
+            1,
+        )
+
+    qkv_pair = in_order(heads_of(core), exchange(heads_of(1 - core), 1), core)
+    out_rows = w_output.shape[0] // 2
+    out_pair = in_order(
+        pick(w_output, core, out_rows, 0),
+        exchange(pick(w_output, 1 - core, out_rows, 0), 1),
+        core,
+        1,
+    )
+    qkv_z = lax.all_gather(qkv_pair, "mp", axis=1, tiled=True)
+    out_z = lax.all_gather(out_pair, "mp", axis=0, tiled=True)
+
+    pieces = jnp.concatenate(
+        [w.reshape(8, units, w.shape[1]) for w in (w_gate.T, w_up.T, w_down)], 1
+    )
+    feed_own = lax.all_to_all(pieces, "dp", 0, 0)
+    feed_own = jnp.swapaxes(feed_own, 0, 1).reshape(3 * units, width)
+
+    inputs = jnp.where(crossing, swap_halves(layer_input), layer_input)
+    cotangent = jnp.where(crossing, swap_halves(out_grad), out_grad)
+
+    qkv_z = after(qkv_z, feed_own)
+    qkv_chips = gather_weights(qkv_z)
+    out_z = after(out_z, qkv_chips)
+    out_chips = gather_weights(out_z)
+    gate_up = lax.all_gather(feed_own[: 2 * units], "mp", axis=0)
+    down = lax.all_gather(feed_own[2 * units :], "mp", axis=0)
+
+    gain_one, gain_two = norm_attn[None, :], norm_mlp[None, :]
+    gain_query, gain_key = query_norm[None, :], key_norm[None, :]
+    (normed,) = tile_call(
+        first_norm_kernel,
+        place,
+        [(inputs, "rows"), (gain_one, 1)],
+        [(array((rows, width), bf16), "rows")],
+        4,
+    )
+    normed_other = exchange(normed, 1)
+    cosines, sines = wide_tables(2 * rows)
+    proj, query_rot, key_rot, value_low, attended, log_total = attend(
+        core_index,
+        normed,
+        normed_other,
+        qkv_chips,
+        cosines,
+        sines,
+        gain_query,
+        gain_key,
+        planes,
+        query_cols,
+    )
+    branch_own, branch_other = columns(place, attended, out_chips, False)
+    middle, tokens_low, tokens_high = tile_call(
+        middle_kernel,
+        place,
+        [(inputs, "rows"), (branch_own, "rows"), (exchange(branch_other, 1), "rows"), (gain_two, 1)],
+        [
+            (array((rows, width), f32), "rows"),
+            (array((rows // 2, width), bf16), "low"),
+            (array((rows // 2, width), bf16), "high"),
+        ],
+        14,
+    )
+
+    grads_low, grads_high = after(
+        (cotangent[: rows // 2], cotangent[rows // 2 :]), (out_chips[1], out_chips[2])
+    )
+    grads_near = gather_near(grads_low, grads_high)
+    tokens_near = gather_near(tokens_low, tokens_high)
+    tokens_far = gather_far(tokens_near)
+    grads_far = gather_far(after(grads_near, tokens_near))
+
+    def quarters(low, high, near, far):
+        halves = [[low, high], near[:2], near[2:], far]
+        return [[(half, 0) for half in both_cores(pair)] for pair in halves]
+
+    token_blocks = quarters(tokens_low, tokens_high, tokens_near, tokens_far)
+    grad_blocks = quarters(grads_low, grads_high, grads_near, grads_far)
+    kept = None
+    outs, twos = [], []
+    for k in range(4):
+        made = feed(k, kept, token_blocks[k], grad_blocks[k], gate_up, down)
+        kept, out_tiles, two_tiles = made[:5], made[5:9], made[9:]
+        outs.append(out_tiles)
+        twos.append([add_low(two_tiles[n], exchange(two_tiles[n + 2], 1)) for n in range(2)])
+    all_tokens, all_grads, all_hidden, all_gate, all_up = kept
+
+    def collect(blocks):
+        (own, over_x, over_y, corner) = blocks
+        x_high = exchange(over_x[1], 2)
+        y_low = exchange(over_y[0], 4)
+        low = exchange(corner[0], 4)
+        high = exchange(corner[1], 2)
+        x_low = exchange(add_low(over_x[0], low), 2)
+        y_high = exchange(add_low(over_y[1], high), 4)
+        return [own[0], own[1], x_low, x_high, y_low, y_high]
+
+    two_parts = collect(twos)
+    gate_weight_grad = dot_first(all_gate, all_tokens).astype(bf16)
+    up_weight_grad = dot_first(all_up, all_tokens).astype(bf16)
+    down_grad = dot_first(all_hidden, all_grads).astype(bf16)
+    outs = after(outs, two_parts)
+    out_parts = collect(
+        [[add_low(tiles[n], exchange(tiles[n + 2], 1)) for n in range(2)] for tiles in outs]
+    )
+    halves = ("low", "high") * 3
+    middle_grad, branch, gain_two_part = tile_call(
+        middle_back_kernel,
+        place,
+        [(middle, "rows"), (cotangent, "rows"), *zip(two_parts, halves), (gain_two, 1)],
+        [
+            (array((rows, width), f32), "rows"),
+            (array((rows, width), bf16), "rows"),
+            (array((8, width), f32), 8),
+        ],
+        18,
+    )
+
+    def over_z(grad):
+        return lax.psum_scatter(grad, "mp", scatter_dimension=0, tiled=True)
+
+    def unspread(own):
+        pieces = jnp.swapaxes(own.reshape(own.shape[0], 8, -1), 0, 1)
+        return lax.all_to_all(pieces, "dp", 0, 0)
+
+    gate_up_own = unspread(
+        jnp.concatenate([over_z(gate_weight_grad), over_z(up_weight_grad)], 0)
+    )
+    gate_own = gate_up_own[:, :units].reshape(8 * units, -1).T.astype(f32)
+    up_own = gate_up_own[:, units:].reshape(8 * units, -1).T.astype(f32)
+    down_own = unspread(over_z(down_grad)).reshape(8 * units, -1).astype(f32)
+
+    branch_pair = exchange(branch, 1)
+    proj_grad, head_gains = attend_back(
+        core_index,
+        branch,
+        branch_pair,
+        out_chips,
+        cosines,
+        sines,
+        gain_query,
+        gain_key,
+        (proj, query_rot, key_rot, value_low, log_total),
+        planes,
+        query_cols,
+    )
+
+    def chip_grads(left, right, along):
+        blocks = []
+        for k in range(4):
+            pair = []
+            for n in range(2):
+                if along == 0:
+                    part = left.shape[1] // 8
+                    first = left[:, (2 * k + n) * part : (2 * k + n + 1) * part]
+                    pair.append(dot_first(first, right))
+                else:
+                    part, depth = right.shape[1] // 4, left.shape[1] // 2
+                    first = left[:, n * depth : (n + 1) * depth]
+                    pair.append(dot_first(first, right[:, k * part : (k + 1) * part]))
+            blocks.append([half.astype(bf16) for half in pair])
+        return blocks
+
+    def gathered(parts):
+        own_low, own_high, x_low, x_high, y_low, y_high = [p.astype(f32) for p in parts]
+        return jnp.concatenate(
+            [own_low + x_low + y_low, own_high + x_high + y_high], 0
+        ).astype(bf16)
+
+    branch_all = jnp.concatenate([branch, branch_pair], 0)
+    out_sum = over_z(gathered(collect(chip_grads(attended, branch_all, 1))))
+    normed_all = jnp.concatenate([normed, normed_other], 0)
+    one_own, one_other = columns(place, proj_grad, qkv_chips, True)
+    qkv_sum = lax.psum_scatter(
+        gathered(collect(chip_grads(normed_all, proj_grad, 0))),
+        "mp",
+        scatter_dimension=1,
+        tiled=True,
+    )
+    input_grad, rounded_grad, gain_one_part = tile_call(
+        input_back_kernel,
+        place,
+        [
+            (inputs, "rows"),
+            (middle_grad, "rows"),
+            (one_own, "rows"),
+            (exchange(one_other, 1), "rows"),
+            (gain_one, 1),
+        ],
+        [
+            (array((rows, width), f32), "rows"),
+            (array((rows, width), bf16), "rows"),
+            (array((8, width), f32), 8),
+        ],
+        18,
+    )
+    (layer_output,) = tile_call(
+        output_kernel,
+        place,
+        [(middle, "rows"), *zip(out_parts, halves)],
+        [(array((rows, width), bf16), "rows")],
+        12,
+    )
+    pair_rows = qkv_sum.shape[0] // 2
+    qkv_other = exchange(pick(qkv_sum, 1 - core, pair_rows, 0), 1)
+    qkv_own = pick(qkv_sum, core, pair_rows, 0)
+
+    def both(start, stop):
+        return in_order(qkv_own[:, start:stop], qkv_other[:, start:stop], core, 1).astype(f32)
+
+    pair_cols = out_sum.shape[1] // 2
+    out_other = exchange(pick(out_sum, 1 - core, pair_cols, 1), 1)
+    out_own = pick(out_sum, core, pair_cols, 1)
+    gain_sums = total(
+        jnp.concatenate(
+            [
+                jnp.sum(gain_one_part, 0),
+                jnp.sum(head_gains[:8], 0),
+                jnp.sum(head_gains[8:], 0),
+                jnp.sum(gain_two_part, 0),
+            ]
+        )
+    )
+    return (
+        jnp.where(crossing, swap_halves(layer_output), layer_output),
+        jnp.where(crossing, swap_halves(rounded_grad).astype(f32), input_grad),
+        gain_sums[:width],
+        gain_sums[width : width + HEAD_SIZE],
+        gain_sums[width + HEAD_SIZE : width + 2 * HEAD_SIZE],
+        both(0, query_cols),
+        both(query_cols, query_cols + key_cols),
+        both(query_cols + key_cols, query_cols + 2 * key_cols),
+        in_order(out_own, out_other, core, 0).astype(f32),
+        gain_sums[width + 2 * HEAD_SIZE :],
+        gate_own,
+        up_own,
+        down_own,
+    )
+
+
 def solution(mesh):
     in_specs = (
         P(("dp", "mp"), None),
@@ -352,4 +1204,6 @@
         P("dp", "mp"),
         P("mp", "dp"),
     )
+    whole_sequences = dict(mesh.shape) == {"dp": 8, "mp": 4}
+    local = fast if whole_sequences else generic
     return jax.shard_map(local, mesh=mesh, in_specs=in_specs, out_specs=out_specs, check_vma=False)

time: 2260 us -> 977 us (0.43)
  waiting for transfers between devices: 1630 us -> 366 us
  Pallas kernels: 0 us -> 275 us
  matrix products: 371 us -> 99.3 us
  starting transfers between devices: 0.89 us -> 106 us
  other arithmetic: 122 us -> 58.9 us
  blocking collectives: 41.4 us -> 0 us
  local copies, waits for them, and re-layouts: 63.5 us -> 38.1 us
    reduce_scatter x11 -> x5, waiting for transfers between devices: 963 us -> 0.01 us  [the longest x4 0.01 us: over_z(): return lax.psum_scatter(grad, 'mp', scatter_dimension=0, tiled=True)]
    all_gather x11 -> x4, waiting for transfers between devices: 666 us -> 7.57 us  [the longest x1 7.56 us: fast(): qkv_z = lax.all_gather(qkv_pair, 'mp', axis=1, tiled=True)]
    ppermute x0 -> x93, waiting for transfers between devices: none -> 332 us  [the longest x87 332 us: exchange(): return lax.ppermute(values, 'dp', [(i, i ^ bit) for i in range(8)])]
    dot_general x38 -> x0, matrix products: 283 us -> none  [the longest x7 116 us: dot_last(): lax.dot_general(left, right, (((1,), (1,)), ((), ())), preferred_element_...]
    pallas_call x0 -> x13, Pallas kernels: none -> 275 us  [the longest x4 147 us: feed(): pl.pallas_call(feed_kernel, grid=(4,), in_specs=blocks + [spec(gate_up.sh...]
    ppermute x0 -> x93, starting transfers between devices: none -> 93.1 us  [the longest x87 83 us: exchange(): return lax.ppermute(values, 'dp', [(i, i ^ bit) for i in range(8)])]
    psum x1 -> x0, blocking collectives: 41.4 us -> none  [local(): lax.psum((gain_one_grad, query_gain_grad, key_gain_grad, gain_two_grad),...]
    reduce_sum x16 -> x3, other arithmetic: 38.5 us -> 1.73 us  [the longest x1 0.86 us: fast(): jnp.sum(gain_two_part, 0)]
  transfers between devices with their start and end apart: 22 -> 105, of which waited for: 17 -> 34; matrix products, arithmetic and copies ran while one was open for 20% -> 17% of each run, Pallas kernels for 0% -> 25%
where the time goes in v1:
time: 977 us; the launch traced here: 959 us
  waiting for transfers between devices  366 us (37%)
  Pallas kernels  275 us (28%)
  starting transfers between devices  106 us (11%)
  matrix products  99.3 us (10%)
  other arithmetic  58.9 us (6%)
  local copies, waits for them, and re-layouts  38.1 us (4%)
  between operations  15.5 us (2%)
    ppermute x87, waiting for transfers between devices, exchange(): return lax.ppermute(values, 'dp', [(i, i ^ bit) for i in range(8)])  332 us
    pallas_call x4, Pallas kernels, feed(): pl.pallas_call(feed_kernel, grid=(4,), in_specs=blocks + [spec(gate_up.sh...  147 us
    dot_general x19, matrix products, dot_first(): lax.dot_general(left, right, (((0,), (0,)), ((), ())), preferred_element_...  99.3 us
    ppermute x87, starting transfers between devices, exchange(): return lax.ppermute(values, 'dp', [(i, i ^ bit) for i in range(8)])  83 us
    pallas_call x1, Pallas kernels, attend_back(): pl.pallas_call(attend_back_kernel, grid_spec=pltpu.PrefetchScalarGridSpec...  40.3 us
    pallas_call x5, Pallas kernels, tile_call(): pl.pallas_call(kernel, grid_spec=pltpu.PrefetchScalarGridSpec(num_scalar_...  35 us
    convert_element_type x16, other arithmetic, add_low(): (left.astype(jnp.float32) + right.astype(jnp.float32)).astype(jnp.bfloat16)  29.3 us
    pallas_call x1, Pallas kernels, attend(): pl.pallas_call(attend_kernel, grid_spec=pltpu.PrefetchScalarGridSpec(num_...  27.7 us
  transfers between devices with their start and end apart: 105, of which 34 were waited for; matrix products, arithmetic and copies ran while one was open for 17% of the time, Pallas kernels for 25%

profile of v1, /device:TPU:0, one launch (start us, length us, event | category | flops | bytes accessed | tf_op | source)
XLA Modules:
  0.0 959.5 jit_solution(84764575737484861)
XLA Ops:
  22.6 26.8 %all-to-all-done = bf16[8,576,256]{2,1,0:T(8,128)(2,1)S(1)} async-done(((bf16[8,576,256]{2,1,0:T(8,128)(2,1)}), bf16[8,576,256]{2,1,0:T(8,128)(2,1)S(1)}, u32[]{:S(2)}, u32[]{:S(2)}) %all-to-all-start) | async-done | bytes 2359328 | tf_op jit(solution)/shard_map/all_to_all | solution.py:951
  71.1 37.4 %collective-permute-done.4.w2 = bf16[512,2048]{1,0:T(8,128)(2,1)} collective-permute-done((bf16[512,2048]{1,0:T(8,128)(2,1)}, bf16[512,2048]{1,0:T(8,128)(2,1)}, u32[]{:S(2)}, u32[]{:S(2)}) %collective-permute-start.4) | collective-permute-done | bytes 2097184 | tf_op jit(solution)/shard_map/ppermute | solution.py:832
  117.4 16.5 %collective-permute-done.6.w3_high = bf16[256,2048]{1,0:T(8,128)(2,1)} collective-permute-done((bf16[256,2048]{1,0:T(8,128)(2,1)S(1)}, bf16[256,2048]{1,0:T(8,128)(2,1)}, u32[]{:S(2)}, u32[]{:S(2)}) %collective-permute-start.6) | collective-permute-done | bytes 1048608 | tf_op jit(solution)/shard_map/ppermute | solution.py:832
  143.3 17.0 %collective-permute-done.9.w2.o2 = bf16[1024,512]{1,0:T(8,128)(2,1)S(1)} collective-permute-done((bf16[1024,512]{1,0:T(8,128)(2,1)}, bf16[1024,512]{1,0:T(8,128)(2,1)S(1)}, u32[]{:S(2)}, u32[]{:S(2)}) %collective-permute-start.9) | collective-permute-done | bytes 1048608 | tf_op jit(solution)/shard_map/ppermute | solution.py:832
  165.6 27.7 %shard_map.229 = (f32[1024,2048]{1,0:T(8,128)}, bf16[1024,1024]{1,0:T(8,128)(2,1)}, bf16[1024,512]{1,0:T(8,128)(2,1)}, bf16[1024,512]{1,0:T(8,128)(2,1)}, bf16[1...) custom-call(s32[1]{0:T(128)} %bitcast.1.core, bf16[512,2048]{1,0:T(8,128)(2,1)} %shard_map.228.own, ...), custom_call_target="tpu_custom_call" | custom-call | flops 11811160064 | bytes 31457280 | tf_op jit(solution)/shard_map/pallas_call | solution.py:419
  194.1 9.3 shard_map.230
  215.6 15.3 %collective-permute-done.30.refs_4_ = bf16[256,2048]{1,0:T(8,128)(2,1)S(1)} collective-permute-done((bf16[256,2048]{1,0:T(8,128)(2,1)S(1)}, bf16[256,2048]{1,0:T(8,128)(2,1)S(1)}, u32[]{:S(2)}, u32[]{:S(2)}) %collective-permute-start.30) | collective-permute-done | bytes 1048608 | tf_op jit(solution)/shard_map/ppermute | solution.py:832
  234.4 19.1 %collective-permute-done.31.refs_5_ = bf16[256,2048]{1,0:T(8,128)(2,1)} collective-permute-done((bf16[256,2048]{1,0:T(8,128)(2,1)S(1)}, bf16[256,2048]{1,0:T(8,128)(2,1)}, u32[]{:S(2)}, u32[]{:S(2)}) %collective-permute-start.31) | collective-permute-done | bytes 1048608 | tf_op jit(solution)/shard_map/ppermute | solution.py:832
  253.9 22.0 %collective-permute-done.26.refs_0_ = bf16[256,2048]{1,0:T(8,128)(2,1)S(1)} collective-permute-done((bf16[256,2048]{1,0:T(8,128)(2,1)}, bf16[256,2048]{1,0:T(8,128)(2,1)S(1)}, u32[]{:S(2)}, u32[]{:S(2)}) %collective-permute-start.26) | collective-permute-done | bytes 1048608 | tf_op jit(solution)/shard_map/ppermute | solution.py:832
  276.4 21.6 %collective-permute-done.27.refs_1_ = bf16[256,2048]{1,0:T(8,128)(2,1)S(1)} collective-permute-done((bf16[256,2048]{1,0:T(8,128)(2,1)}, bf16[256,2048]{1,0:T(8,128)(2,1)S(1)}, u32[]{:S(2)}, u32[]{:S(2)}) %collective-permute-start.27) | collective-permute-done | bytes 1048608 | tf_op jit(solution)/shard_map/ppermute | solution.py:832
  306.5 36.9 %shard_map.232 = (bf16[4096,2048]{1,0:T(8,128)(2,1)}, bf16[4096,2048]{1,0:T(8,128)(2,1)}, bf16[4096,768]{1,0:T(8,128)(2,1)}, bf16[4096,768]{1,0:T(8,128)(2,1)}, ...) custom-call(bf16[256,2048]{1,0:T(8,128)(2,1)} %get-tuple-element.112, ...), custom_call_target="tpu_custom_call" | custom-call | flops 19327352832 | bytes 41943040 | tf_op jit(solution)/shard_map/pallas_call | solution.py:648
  347.5 36.4 %shard_map.233 = (bf16[4096,2048]{1,0:T(8,128)(2,1)}, bf16[4096,2048]{1,0:T(8,128)(2,1)}, bf16[4096,768]{1,0:T(8,128)(2,1)}, bf16[4096,768]{1,0:T(8,128)(2,1)}, ...) custom-call(bf16[256,2048]{1,0:T(8,128)(2,1)} %collective-permute-do, ...), custom_call_target="tpu_custom_call", output_to_operand_aliasing={{0}: (10, {}), {1}: (11, {}), {2}: (12, {}), {3}: (13, {}),... | custom-call | flops 19327352832 | bytes 41943040 | tf_op jit(solution)/shard_map/pallas_call | solution.py:648
  384.0 7.6 collective-permute-done.34.refs_0_
  392.6 37.0 %shard_map.234 = (bf16[4096,2048]{1,0:T(8,128)(2,1)}, bf16[4096,2048]{1,0:T(8,128)(2,1)}, bf16[4096,768]{1,0:T(8,128)(2,1)}, bf16[4096,768]{1,0:T(8,128)(2,1)}, ...) custom-call(bf16[256,2048]{1,0:T(8,128)(2,1)} %copy-done.49, ...), custom_call_target="tpu_custom_call", output_to_operand_aliasing={{0}: (10, {}), {1}: (11, {}), {2}: (12, {}), {3}: (13, {}),... | custom-call | flops 19327352832 | bytes 41943040 | tf_op jit(solution)/shard_map/pallas_call | solution.py:648
  429.7 36.5 %shard_map.235 = (bf16[4096,2048]{1,0:T(8,128)(2,1)}, bf16[4096,2048]{1,0:T(8,128)(2,1)}, bf16[4096,768]{1,0:T(8,128)(2,1)}, bf16[4096,768]{1,0:T(8,128)(2,1)}, ...) custom-call(bf16[256,2048]{1,0:T(8,128)(2,1)} %copy-done.58, ...), custom_call_target="tpu_custom_call", output_to_operand_aliasing={{0}: (10, {}), {1}: (11, {}), {2}: (12, {}), {3}: (13, {}),... | custom-call | flops 19327352832 | bytes 41943040 | tf_op jit(solution)/shard_map/pallas_call | solution.py:648
  466.2 20.1 %convolution_convert_fusion = bf16[768,2048]{1,0:T(8,128)(2,1)} fusion(bf16[4096,768]{1,0:T(8,128)(2,1)} %get-tuple-element.199, bf16[4096,2048]{1,0:T(8,128)(2,1)} %get-tuple-element.200), kind=kOutput, calls=%fused_computation.15 | convolution fusion | flops 12886474752 | bytes 26214400 | tf_op jit(solution)/shard_map/dot_general | solution.py:77
  487.7 20.5 %convolution_convert_fusion.1 = bf16[768,2048]{1,0:T(8,128)(2,1)} fusion(bf16[4096,768]{1,0:T(8,128)(2,1)} %get-tuple-element.198, bf16[4096,2048]{1,0:T(8,128)(2,1)} %get-tuple-element.197), kind=kOutput, calls=%fused_computation.16 | convolution fusion | flops 12886474752 | bytes 26214400 | tf_op jit(solution)/shard_map/dot_general | solution.py:77
  517.1 21.4 %collective-permute-done.46 = bf16[256,2048]{1,0:T(8,128)(2,1)S(1)} collective-permute-done((bf16[256,2048]{1,0:T(8,128)(2,1)S(1)}, bf16[256,2048]{1,0:T(8,128)(2,1)S(1)}, u32[]{:S(2)}, u32[]{:S(2)}) %collective-permute-start.46) | collective-permute-done | bytes 1048608 | tf_op jit(solution)/shard_map/ppermute | solution.py:832
  548.0 16.5 %collective-permute-done.49.x_high = bf16[256,2048]{1,0:T(8,128)(2,1)S(1)} collective-permute-done((bf16[256,2048]{1,0:T(8,128)(2,1)S(1)}, bf16[256,2048]{1,0:T(8,128)(2,1)S(1)}, u32[]{:S(2)}, u32[]{:S(2)}) %collective-permute-start.49) | collective-permute-done | bytes 1048608 | tf_op jit(solution)/shard_map/ppermute | solution.py:832
  566.5 19.0 %collective-permute-done.47.x_low = bf16[256,2048]{1,0:T(8,128)(2,1)S(1)} collective-permute-done((bf16[256,2048]{1,0:T(8,128)(2,1)S(1)}, bf16[256,2048]{1,0:T(8,128)(2,1)S(1)}, u32[]{:S(2)}, u32[]{:S(2)}) %collective-permute-start.47) | collective-permute-done | bytes 1048608 | tf_op jit(solution)/shard_map/ppermute | solution.py:832
  588.5 19.9 %convolution_convert_fusion.2 = bf16[768,2048]{1,0:T(8,128)(2,1)} fusion(bf16[4096,768]{1,0:T(8,128)(2,1)} %get-tuple-element.196, bf16[4096,2048]{1,0:T(8,128)(2,1)} %get-tuple-element.197), kind=kOutput, calls=%fused_computation.17 | convolution fusion | flops 12886474752 | bytes 26214400 | tf_op jit(solution)/shard_map/dot_general | solution.py:77
  609.4 10.6 %shard_map.237 = (f32[512,2048]{1,0:T(8,128)}, bf16[512,2048]{1,0:T(8,128)(2,1)}, f32[8,2048]{1,0:T(8,128)}) custom-call(s32[1]{0:T(128)} %bitcast.place, f32[512,2048]{1,0:T(8,128)} %get-tuple-element.111.middle, bf16[512,2048]{1,0:T(8,128)(2,1)} %copy-done.8, bf16[256,2048]{1,0:T(8,128)(2,1)} %add_convert_fusion.19.own_low, ...), custom_call_target="tpu_custom_call" | custom-call | flops 20971520 | bytes 18874368 | tf_op jit(solution)/shard_map/pallas_call | solution.py:741
  635.1 40.3 %shard_map.238 = (bf16[1024,2048]{1,0:T(8,128)(2,1)}, f32[16,128]{1,0:T(8,128)}) custom-call(s32[1]{0:T(128)} %bitcast.1.core, bf16[512,2048]{1,0:T(8,128)(2,1)} %get-tuple-element.182.own, bf16[512,2048]{1,0:T(8,128)(2,1)} %copy-done.12, bf16[1024,512]{1,0:T(8,128)(2,1)} %all-gather.7.cloned.1.call-done.w0.o0, bf16[1024,512]{1,0:T(8,128)(2,1)} %copy-done.43, ...), custom_call_target="tpu_custom_call" | custom-call | flops 12884901888 | bytes 31457280 | tf_op jit(solution)/shard_map/pallas_call | solution.py:546
  694.2 16.1 %shard_map.239 = (f32[512,2048]{1,0:T(8,128)}, bf16[512,2048]{1,0:T(8,128)(2,1)}) custom-call(s32[1]{0:T(128)} %bitcast.place, bf16[1024,2048]{1,0:T(8,128)(2,1)} %get-tuple-element.188.left, bf16[512,2048]{1,0:T(8,128)(2,1)} %all-gather.5.cloned.1.call-done.w0, bf16[512,2048]{1,0:T(8,128)(2,1)} %collective-permute-done.3.w1, ...), custom_call_target="tpu_custom_call" | custom-call | flops 8589934592 | bytes 20971520 | tf_op jit(solution)/shard_map/pallas_call | solution.py:714
  733.1 11.7 %collective-permute-done.87 = bf16[512,512]{1,0:T(8,128)(2,1)S(1)} collective-permute-done((bf16[512,512]{1,0:T(8,128)(2,1)S(1)}, bf16[512,512]{1,0:T(8,128)(2,1)S(1)}, u32[]{:S(2)}, u32[]{:S(2)}) %collective-permute-start.87) | collective-permute-done | bytes 524320 | tf_op jit(solution)/shard_map/ppermute | solution.py:832
  756.6 10.8 %collective-permute-done.83 = bf16[256,2048]{1,0:T(8,128)(2,1)} collective-permute-done((bf16[256,2048]{1,0:T(8,128)(2,1)}, bf16[256,2048]{1,0:T(8,128)(2,1)}, u32[]{:S(2)}, u32[]{:S(2)}) %collective-permute-start.83) | collective-permute-done | bytes 1048608 | tf_op jit(solution)/shard_map/ppermute | solution.py:832
  772.9 16.9 %collective-permute-done.68 = bf16[256,2048]{1,0:T(8,128)(2,1)} collective-permute-done((bf16[256,2048]{1,0:T(8,128)(2,1)S(1)}, bf16[256,2048]{1,0:T(8,128)(2,1)}, u32[]{:S(2)}, u32[]{:S(2)}) %collective-permute-start.68) | collective-permute-done | bytes 1048608 | tf_op jit(solution)/shard_map/ppermute | solution.py:832
  800.8 9.2 shard_map.240
  818.5 16.2 %collective-permute-done.82 = bf16[256,2048]{1,0:T(8,128)(2,1)} collective-permute-done((bf16[256,2048]{1,0:T(8,128)(2,1)}, bf16[256,2048]{1,0:T(8,128)(2,1)}, u32[]{:S(2)}, u32[]{:S(2)}) %collective-permute-start.82) | collective-permute-done | bytes 1048608 | tf_op jit(solution)/shard_map/ppermute | solution.py:832
  841.2 22.7 %collective-permute-done.75 = f32[4352]{0:T(1024)S(1)} collective-permute-done((f32[4352]{0:T(1024)S(1)}, f32[4352]{0:T(1024)S(1)}, u32[]{:S(2)}, u32[]{:S(2)}) %collective-permute-start.75) | collective-permute-done | bytes 17440 | tf_op jit(solution)/shard_map/ppermute | solution.py:832
  882.3 11.2 %collective-permute-done.61.x_low = bf16[256,2048]{1,0:T(8,128)(2,1)} collective-permute-done((bf16[256,2048]{1,0:T(8,128)(2,1)}, bf16[256,2048]{1,0:T(8,128)(2,1)}, u32[]{:S(2)}, u32[]{:S(2)}) %collective-permute-start.61) | collective-permute-done | bytes 1048608 | tf_op jit(solution)/shard_map/ppermute | solution.py:832
  919.3 19.8 %collective-permute-start.92 = (bf16[256,256]{1,0:T(8,128)(2,1)S(1)}, bf16[256,256]{1,0:T(8,128)(2,1)S(1)}, u32[]{:S(2)}, u32[]{:S(2)}) collective-permute-start(bf16[256,256]{1,0:T(8,128)(2,1)S(1)} %get-tuple-element.249), channel_id=1, source_target_pairs={{0,4},{4,0},{8,12},{12,8},{16,20},{20,16},{24,28},{28,24},{1,5},{5... | collective-permute-start | bytes 393224 | tf_op jit(solution)/shard_map/ppermute | solution.py:832
  (426 shorter events, 273.8 us)
Async XLA Ops:
  7.2 53.7 %all-gather.5.cloned.1.call-start = ((), (), s32[]{:S(2)}) async-start(), calls=%async_computation.8 | async-start | bytes 2621440 | tf_op jit(solution)/shard_map/all_gather | solution.py:945
  20.0 97.4 %all-gather.7.cloned.1.call-start = ((), (), s32[]{:S(2)}) async-start(), calls=%async_computation.9 | async-start | bytes 1310720 | tf_op jit(solution)/shard_map/all_gather | solution.py:946
  22.6 283.9 %all-gather.11.cloned.1.call-start = ((), (), s32[]{:S(2)}) async-start(), calls=%async_computation.11 | async-start | bytes 3932160 | tf_op jit(solution)/shard_map/all_gather | solution.py:962
  51.2 255.3 %all-gather.9.cloned.1.call-start = ((), (), s32[]{:S(2)}) async-start(), calls=%async_computation.10 | async-start | bytes 7864320 | tf_op jit(solution)/shard_map/all_gather | solution.py:961
  60.8 47.6 %collective-permute-start.4 = (bf16[512,2048]{1,0:T(8,128)(2,1)}, bf16[512,2048]{1,0:T(8,128)(2,1)}, u32[]{:S(2)}, u32[]{:S(2)}) collective-permute-start(bf16[512,2048]{1,0:T(8,128)(2,1)} %all-gather.5.cloned.1.call-done.w0), channel_id=1, source_target_pairs={{0,16},{4,20},{8,24},{12,28},{16,0},{20,4},{24,8},{28,12},{1,17},{... | collective-permute-start | bytes 6291464 | tf_op jit(solution)/shard_map/ppermute | solution.py:832
  62.2 48.9 %collective-permute-start.3 = (bf16[512,2048]{1,0:T(8,128)(2,1)}, bf16[512,2048]{1,0:T(8,128)(2,1)}, u32[]{:S(2)}, u32[]{:S(2)}) collective-permute-start(bf16[512,2048]{1,0:T(8,128)(2,1)} %all-gather.5.cloned.1.call-done.w0), channel_id=1, source_target_pairs={{0,8},{4,12},{8,0},{12,4},{16,24},{20,28},{24,16},{28,20},{1,9},{5... | collective-permute-start | bytes 6291464 | tf_op jit(solution)/shard_map/ppermute | solution.py:832
  67.9 726.8 %reduce-scatter.14.cloned.1.call-start = ((), (), s32[]{:S(2)}) async-start(), calls=%async_computation.16 | async-start | bytes 3932160 | tf_op jit(solution)/shard_map/reduce_scatter | solution.py:1055
  117.4 46.8 %collective-permute-start.1 = (bf16[512,2048]{1,0:T(8,128)(2,1)}, bf16[512,2048]{1,0:T(8,128)(2,1)S(1)}, u32[]{:S(2)}, u32[]{:S(2)}) collective-permute-start(bf16[512,2048]{1,0:T(8,128)(2,1)} %shard_map.228.own), channel_id=1, source_target_pairs={{0,4},{4,0},{8,12},{12,8},{16,20},{20,16},{24,28},{28,24},{1,5},{5... | collective-permute-start | bytes 6291464 | tf_op jit(solution)/shard_map/ppermute | solution.py:832
  139.3 64.2 %collective-permute-start.15 = (bf16[512,2048]{1,0:T(8,128)(2,1)}, bf16[512,2048]{1,0:T(8,128)(2,1)S(1)}, u32[]{:S(2)}, u32[]{:S(2)}) collective-permute-start(bf16[512,2048]{1,0:T(8,128)(2,1)} %param.14), channel_id=1, source_target_pairs={{1,4},{3,6},{4,1},{6,3},{9,12},{11,14},{12,9},{14,11},{17,20},{19,... | collective-permute-start | bytes 6291464 | tf_op jit(solution)/shard_map/ppermute | solution.py:841
  205.6 47.9 %collective-permute-start.31 = (bf16[256,2048]{1,0:T(8,128)(2,1)S(1)}, bf16[256,2048]{1,0:T(8,128)(2,1)}, u32[]{:S(2)}, u32[]{:S(2)}) collective-permute-start(bf16[256,2048]{1,0:T(8,128)(2,1)S(1)} %get-tuple-element.115.refs_5_), channel_id=1, source_target_pairs={{0,16},{4,20},{8,24},{12,28},{16,0},{20,4},{24,8},{28,12},{1,17},{... | collective-permute-start | bytes 3145736 | tf_op jit(solution)/shard_map/ppermute | solution.py:832
  207.8 46.1 %collective-permute-start.23 = (bf16[256,2048]{1,0:T(8,128)(2,1)S(1)}, bf16[256,2048]{1,0:T(8,128)(2,1)}, u32[]{:S(2)}, u32[]{:S(2)}) collective-permute-start(bf16[256,2048]{1,0:T(8,128)(2,1)S(1)} %get-tuple-element.115.refs_5_), channel_id=1, source_target_pairs={{0,8},{4,12},{8,0},{12,4},{16,24},{20,28},{24,16},{28,20},{1,9},{5... | collective-permute-start | bytes 3145736 | tf_op jit(solution)/shard_map/ppermute | solution.py:832
  232.7 65.3 %collective-permute-start.27 = (bf16[256,2048]{1,0:T(8,128)(2,1)}, bf16[256,2048]{1,0:T(8,128)(2,1)S(1)}, u32[]{:S(2)}, u32[]{:S(2)}) collective-permute-start(bf16[256,2048]{1,0:T(8,128)(2,1)} %get-tuple-element.113.refs_1_), channel_id=1, source_target_pairs={{0,16},{4,20},{8,24},{12,28},{16,0},{20,4},{24,8},{28,12},{1,17},{... | collective-permute-start | bytes 3145736 | tf_op jit(solution)/shard_map/ppermute | solution.py:832
  343.4 48.7 %collective-permute-start.38 = (bf16[256,2048]{1,0:T(8,128)(2,1)}, bf16[256,2048]{1,0:T(8,128)(2,1)S(1)}, u32[]{:S(2)}, u32[]{:S(2)}) collective-permute-start(bf16[256,2048]{1,0:T(8,128)(2,1)} %copy-done.50), channel_id=1, source_target_pairs={{0,16},{4,20},{8,24},{12,28},{16,0},{20,4},{24,8},{28,12},{1,17},{... | collective-permute-start | bytes 3145736 | tf_op jit(solution)/shard_map/ppermute | solution.py:832
  343.5 48.8 %collective-permute-start.39 = (bf16[256,2048]{1,0:T(8,128)(2,1)}, bf16[256,2048]{1,0:T(8,128)(2,1)S(1)}, u32[]{:S(2)}, u32[]{:S(2)}) collective-permute-start(bf16[256,2048]{1,0:T(8,128)(2,1)} %collective-permute-done.31.refs_5_), channel_id=1, source_target_pairs={{0,8},{4,12},{8,0},{12,4},{16,24},{20,28},{24,16},{28,20},{1,9},{5... | collective-permute-start | bytes 3145736 | tf_op jit(solution)/shard_map/ppermute | solution.py:832
  343.9 47.7 %collective-permute-start.34 = (bf16[256,2048]{1,0:T(8,128)(2,1)}, bf16[256,2048]{1,0:T(8,128)(2,1)S(1)}, u32[]{:S(2)}, u32[]{:S(2)}) collective-permute-start(bf16[256,2048]{1,0:T(8,128)(2,1)} %collective-permute-done.18.refs_0_), channel_id=1, source_target_pairs={{0,16},{4,20},{8,24},{12,28},{16,0},{20,4},{24,8},{28,12},{1,17},{... | collective-permute-start | bytes 3145736 | tf_op jit(solution)/shard_map/ppermute | solution.py:832
  486.4 385.6 %reduce-scatter.12.cloned.1.call-start = ((), (), s32[]{:S(2)}) async-start(), calls=%async_computation.15 | async-start | bytes 3932160 | tf_op jit(solution)/shard_map/reduce_scatter | solution.py:1055
  486.4 58.2 %collective-permute-start.42 = (bf16[256,2048]{1,0:T(8,128)(2,1)}, bf16[256,2048]{1,0:T(8,128)(2,1)S(1)}, u32[]{:S(2)}, u32[]{:S(2)}) collective-permute-start(bf16[256,2048]{1,0:T(8,128)(2,1)} %get-tuple-element.150), channel_id=1, source_target_pairs={{0,4},{4,0},{8,12},{12,8},{16,20},{20,16},{24,28},{28,24},{1,5},{5... | collective-permute-start | bytes 3145736 | tf_op jit(solution)/shard_map/ppermute | solution.py:832
  508.3 363.7 %reduce-scatter.10.cloned.1.call-start = ((), (), s32[]{:S(2)}) async-start(), calls=%async_computation.14 | async-start | bytes 3932160 | tf_op jit(solution)/shard_map/reduce_scatter | solution.py:1055
  608.4 309.9 %reduce-scatter.8.cloned.1.call-start = ((), (), s32[]{:S(2)}) async-start(), calls=%async_computation.13 | async-start | bytes 1310720 | tf_op jit(solution)/shard_map/reduce_scatter | solution.py:1055
  608.9 113.4 %collective-permute-start.58 = (bf16[256,2048]{1,0:T(8,128)(2,1)}, bf16[256,2048]{1,0:T(8,128)(2,1)}, u32[]{:S(2)}, u32[]{:S(2)}) collective-permute-start(bf16[256,2048]{1,0:T(8,128)(2,1)} %get-tuple-element.170), channel_id=1, source_target_pairs={{0,4},{4,0},{8,12},{12,8},{16,20},{20,16},{24,28},{28,24},{1,5},{5... | collective-permute-start | bytes 3145736 | tf_op jit(solution)/shard_map/ppermute | solution.py:832
  627.4 95.2 %collective-permute-start.60 = (bf16[256,2048]{1,0:T(8,128)(2,1)}, bf16[256,2048]{1,0:T(8,128)(2,1)}, u32[]{:S(2)}, u32[]{:S(2)}) collective-permute-start(bf16[256,2048]{1,0:T(8,128)(2,1)} %add_convert_fusion.6), channel_id=1, source_target_pairs={{0,16},{4,20},{8,24},{12,28},{16,0},{20,4},{24,8},{28,12},{1,17},{... | collective-permute-start | bytes 3145736 | tf_op jit(solution)/shard_map/ppermute | solution.py:832
  680.0 69.8 %collective-permute-start.79 = (bf16[256,2048]{1,0:T(8,128)(2,1)}, bf16[256,2048]{1,0:T(8,128)(2,1)}, u32[]{:S(2)}, u32[]{:S(2)}) collective-permute-start(bf16[256,2048]{1,0:T(8,128)(2,1)} %convolution_convert_fusion.8), channel_id=1, source_target_pairs={{0,16},{4,20},{8,24},{12,28},{16,0},{20,4},{24,8},{28,12},{1,17},{... | collective-permute-start | bytes 3145736 | tf_op jit(solution)/shard_map/ppermute | solution.py:832
  744.8 55.5 %collective-permute-start.72 = (bf16[512,2048]{1,0:T(8,128)(2,1)}, bf16[512,2048]{1,0:T(8,128)(2,1)}, u32[]{:S(2)}, u32[]{:S(2)}) collective-permute-start(bf16[512,2048]{1,0:T(8,128)(2,1)} %get-tuple-element.190), channel_id=1, source_target_pairs={{0,4},{4,0},{8,12},{12,8},{16,20},{20,16},{24,28},{28,24},{1,5},{5... | collective-permute-start | bytes 6291464 | tf_op jit(solution)/shard_map/ppermute | solution.py:832
  749.8 61.0 %collective-permute-start.81 = (bf16[256,2048]{1,0:T(8,128)(2,1)}, bf16[256,2048]{1,0:T(8,128)(2,1)}, u32[]{:S(2)}, u32[]{:S(2)}) collective-permute-start(bf16[256,2048]{1,0:T(8,128)(2,1)} %convolution_convert_fusion.7), channel_id=1, source_target_pairs={{0,16},{4,20},{8,24},{12,28},{16,0},{20,4},{24,8},{28,12},{1,17},{... | collective-permute-start | bytes 3145736 | tf_op jit(solution)/shard_map/ppermute | solution.py:832
  772.6 62.2 %collective-permute-start.82 = (bf16[256,2048]{1,0:T(8,128)(2,1)}, bf16[256,2048]{1,0:T(8,128)(2,1)}, u32[]{:S(2)}, u32[]{:S(2)}) collective-permute-start(bf16[256,2048]{1,0:T(8,128)(2,1)} %convolution_convert_fusion.5), channel_id=1, source_target_pairs={{0,8},{4,12},{8,0},{12,4},{16,24},{20,28},{24,16},{28,20},{1,9},{5... | collective-permute-start | bytes 3145736 | tf_op jit(solution)/shard_map/ppermute | solution.py:832
  789.8 46.7 %collective-permute-start.84 = (bf16[256,2048]{1,0:T(8,128)(2,1)}, bf16[256,2048]{1,0:T(8,128)(2,1)}, u32[]{:S(2)}, u32[]{:S(2)}) collective-permute-start(bf16[256,2048]{1,0:T(8,128)(2,1)} %fusion.2), channel_id=1, source_target_pairs={{0,16},{4,20},{8,24},{12,28},{16,0},{20,4},{24,8},{28,12},{1,17},{... | collective-permute-start | bytes 3145736 | tf_op jit(solution)/shard_map/ppermute | solution.py:832
  796.7 78.2 %all-to-all-start.2 = ((bf16[8,192,256]{2,1,0:T(8,128)(2,1)}), bf16[8,192,256]{2,1,0:T(8,128)(2,1)S(1)}, u32[]{:S(2)}, u32[]{:S(2)}) async-start(bf16[8,192,256]{2,1,0:T(8,128)(2,1)} %bitcast.55), calls=%async_computation.7 | async-start | bytes 1572864 | tf_op jit(solution)/shard_map/all_to_all | solution.py:1059
  800.3 141.2 %reduce-scatter.6.cloned.1.call-start = ((), (), s32[]{:S(2)}) async-start(), calls=%async_computation.12 | async-start | bytes 2621440 | tf_op jit(solution)/shard_map/reduce_scatter | solution.py:1109
  800.3 66.7 %collective-permute-start.56 = (bf16[256,2048]{1,0:T(8,128)(2,1)}, bf16[256,2048]{1,0:T(8,128)(2,1)}, u32[]{:S(2)}, u32[]{:S(2)}) collective-permute-start(bf16[256,2048]{1,0:T(8,128)(2,1)} %get-tuple-element.166), channel_id=1, source_target_pairs={{0,4},{4,0},{8,12},{12,8},{16,20},{20,16},{24,28},{28,24},{1,5},{5... | collective-permute-start | bytes 3145736 | tf_op jit(solution)/shard_map/ppermute | solution.py:832
  810.8 67.7 %collective-permute-start.57 = (bf16[256,2048]{1,0:T(8,128)(2,1)}, bf16[256,2048]{1,0:T(8,128)(2,1)}, u32[]{:S(2)}, u32[]{:S(2)}) collective-permute-start(bf16[256,2048]{1,0:T(8,128)(2,1)} %get-tuple-element.168), channel_id=1, source_target_pairs={{0,4},{4,0},{8,12},{12,8},{16,20},{20,16},{24,28},{28,24},{1,5},{5... | collective-permute-start | bytes 3145736 | tf_op jit(solution)/shard_map/ppermute | solution.py:832
  816.7 65.5 %collective-permute-start.63 = (bf16[256,2048]{1,0:T(8,128)(2,1)}, bf16[256,2048]{1,0:T(8,128)(2,1)}, u32[]{:S(2)}, u32[]{:S(2)}) collective-permute-start(bf16[256,2048]{1,0:T(8,128)(2,1)} %add_convert_fusion.4), channel_id=1, source_target_pairs={{0,8},{4,12},{8,0},{12,4},{16,24},{20,28},{24,16},{28,20},{1,9},{5... | collective-permute-start | bytes 3145736 | tf_op jit(solution)/shard_map/ppermute | solution.py:832
  834.8 47.5 %collective-permute-start.65 = (bf16[256,2048]{1,0:T(8,128)(2,1)}, bf16[256,2048]{1,0:T(8,128)(2,1)}, u32[]{:S(2)}, u32[]{:S(2)}) collective-permute-start(bf16[256,2048]{1,0:T(8,128)(2,1)} %add_convert_fusion.3), channel_id=1, source_target_pairs={{0,16},{4,20},{8,24},{12,28},{16,0},{20,4},{24,8},{28,12},{1,17},{... | collective-permute-start | bytes 3145736 | tf_op jit(solution)/shard_map/ppermute | solution.py:832
  (138 other events, 3072.7 us)
Sparse Core Ops, SparseCore 0:
  12.2 48.5 all-gather.4
  63.0 33.6 all-gather.6
  98.3 70.0 all-gather.10
  170.4 119.2 all-gather.8
  486.5 59.0 reduce-scatter.13
  547.8 60.2 reduce-scatter.11
  610.4 60.2 reduce-scatter.9
  749.9 26.2 reduce-scatter.7
  867.1 45.7 reduce-scatter.5

commit v2 on v1

--- a/solution.py
+++ b/solution.py
@@ -583,91 +583,439 @@
     )(core, own, other, *weights, cosines, sines, query_gain, key_gain, *saved)
 
 
-def feed_kernel(*refs):
-    token_tiles, grad_tiles = refs[:4], refs[4:8]
-    gate_up, down = refs[8:10]
-    all_tokens, all_grads, all_hidden, all_gate, all_up = refs[-13:-8]
-    out_tiles, two_tiles = refs[-8:-4], refs[-4:]
-    step = pl.program_id(0)
-    units = down.shape[1]
-    width = down.shape[2]
-    hidden_count = down.shape[0] * units
-    gate_t = gate_up[:, :units, :].reshape(hidden_count, width)
-    up_t = gate_up[:, units:, :].reshape(hidden_count, width)
-    down_t = down[...].reshape(hidden_count, width)
-
-    def select(tiles):
-        low = jnp.where(step == 0, tiles[0][...], tiles[1][...])
-        high = jnp.where(step == 2, tiles[2][...], tiles[3][...])
-        return jnp.where(step < 2, low, high)
-
-    all_tokens[...] = select(token_tiles)
-    all_grads[...] = select(grad_tiles)
-    tokens = all_tokens[...]
-    grads = all_grads[...]
-    for start in range(0, hidden_count, 256):
-        cols = slice(start, start + 256)
-        gate = dot_last(tokens, gate_t[cols])
-        up = dot_last(tokens, up_t[cols])
-        hidden_grad = dot_last(grads, down_t[cols])
-        sigmoid_gate = 1.0 / (1.0 + jnp.exp(-gate))
-        silu = gate * sigmoid_gate
-        all_hidden[:, cols] = (silu * up).astype(jnp.bfloat16)
-        all_gate[:, cols] = (
-            hidden_grad * up * sigmoid_gate * (1.0 + gate * (1.0 - sigmoid_gate))
-        ).astype(jnp.bfloat16)
-        all_up[:, cols] = (hidden_grad * silu).astype(jnp.bfloat16)
-    hidden, gate_grad, up_grad = all_hidden[...], all_gate[...], all_up[...]
-    for start in range(0, width, 512):
-        cols = slice(start, start + 512)
-        out = matmul(hidden, down_t[:, cols]).astype(jnp.bfloat16)
-        two = (matmul(gate_grad, gate_t[:, cols]) + matmul(up_grad, up_t[:, cols])).astype(
-            jnp.bfloat16
+MESH = pl.DeviceIdType.MESH
+
+
+def neighbours():
+    me = lax.axis_index("dp")
+    x, y = (me // 2) % 2, me // 4
+    return me, me + 2 - 4 * x, me + 4 - 8 * y
+
+
+def greet(others):
+    barrier = pltpu.get_barrier_semaphore()
+    for other in others:
+        pl.semaphore_signal(barrier, inc=1, device_id={"dp": other}, device_id_type=MESH)
+    pl.semaphore_wait(barrier, len(others))
+
+
+def column_places(width):
+    me = lax.axis_index("dp")
+    core, x, y = me % 2, (me // 2) % 2, me // 4
+    block = 256
+    places = []
+    for n in range(width // block):
+        here = core if n < 4 else 1 - core
+        far_x = 1 - x if n % 2 else x
+        far_y = 1 - y if (n // 2) % 2 else y
+        start = (4 * far_y + 2 * far_x + here) * block
+        places.append(pl.ds(pl.multiple_of(start, block), block))
+    return places
+
+
+def split_columns(target, values):
+    for n, cols in enumerate(column_places(values.shape[1])):
+        target[:, n * 256 : (n + 1) * 256] = values[:, cols]
+
+
+def merge_columns(target, sums):
+    for n, cols in enumerate(column_places(sums.shape[1])):
+        target[:, cols] = sums[:, n * 256 : (n + 1) * 256].astype(target.dtype)
+
+
+def both_halves(left, own, other):
+    half = own.shape[1]
+    return dot_last(left[:, :half], own[...]) + dot_last(left[:, half:], other[...])
+
+
+def hidden_kernel(
+    x_tokens_out, y_tokens_out, x_grads_out, y_grads_out,
+    own_tokens, x_tokens, y_tokens, own_grads, x_grads, y_grads,
+    gate_own, gate_other, up_own, up_other,
+    all_tokens, all_grads, hidden, gate_slope, up_slope,
+    far_tokens, far_grads, send, receive,
+):
+    block, chunk = pl.program_id(0), pl.program_id(1)
+    _, over_x, over_y = neighbours()
+    half = far_tokens.shape[0] // 2
+    low, high = pl.ds(0, half), pl.ds(half, half)
+    copies = [
+        pltpu.make_async_remote_copy(
+            src_ref=source.at[rows],
+            dst_ref=target.at[rows],
+            send_sem=send.at[n],
+            recv_sem=receive.at[n],
+            device_id={"dp": other},
+            device_id_type=MESH,
         )
-        for tile in range(4):
-
-            @pl.when(step == tile)
-            def _():
-                out_tiles[tile][:, cols] = out
-                two_tiles[tile][:, cols] = two
-
-
-def feed(index, earlier, tokens, grads, gate_up, down):
-    tile, width = 256, gate_up.shape[2]
-    hidden_count = down.shape[0] * down.shape[1]
-    count = 16 * tile
-    placed = lambda t: (index * 4 + t, 0)
+        for n, (source, target, rows, other) in enumerate(
+            (
+                (x_tokens_out, far_tokens, low, over_y),
+                (y_tokens_out, far_tokens, high, over_x),
+                (x_grads_out, far_grads, low, over_y),
+                (y_grads_out, far_grads, high, over_x),
+            )
+        )
+    ]
+
+    @pl.when((block == 0) & (chunk == 0))
+    def _():
+        greet((over_x, over_y))
+        for transfer in copies:
+            transfer.start()
+
+    parts = ((own_tokens, own_grads), (x_tokens, x_grads), (y_tokens, y_grads), (far_tokens, far_grads))
+    for n, (tokens, grads) in enumerate(parts):
+
+        @pl.when((block == n) & (chunk == 0))
+        def _():
+            if n == 3:
+                for transfer in copies:
+                    transfer.wait_recv()
+            split_columns(all_tokens, tokens)
+            split_columns(all_grads, grads)
+
+    values = all_tokens[...]
+    gate = both_halves(values, gate_own, gate_other)
+    up = both_halves(values, up_own, up_other)
+    sigmoid_gate = 1.0 / (1.0 + jnp.exp(-gate))
+    silu = gate * sigmoid_gate
+    hidden[...] = (silu * up).astype(jnp.bfloat16)
+    gate_slope[...] = (up * sigmoid_gate * (1.0 + gate * (1.0 - sigmoid_gate))).astype(
+        jnp.bfloat16
+    )
+    up_slope[...] = silu.astype(jnp.bfloat16)
+
+    @pl.when((block == 3) & (chunk == pl.num_programs(1) - 1))
+    def _():
+        for transfer in copies:
+            transfer.wait_send()
+
+
+def gather_hidden(tokens, grads, weights):
+    rows, width = tokens[0].shape
+    hidden_count, half = weights[0].shape
+    chunk = 512
     spec = pl.BlockSpec
     shape = jax.ShapeDtypeStruct
-    kept = [] if earlier is None else list(earlier)
-    once = pl.Buffered(1)
-    blocks = [
-        spec((tile, width), lambda t, row=row: (row, 0), pipeline_mode=once)
-        for _, row in tokens + grads
+    outside = spec(memory_space=pl.ANY)
+    whole = spec((rows, width), lambda b, c: (0, 0), pipeline_mode=pl.Buffered(1))
+    bf16 = jnp.bfloat16
+    return pl.pallas_call(
+        hidden_kernel,
+        grid=(4, hidden_count // chunk),
+        in_specs=[outside] * 4 + [whole] * 6 + [spec((chunk, half), lambda b, c: (c, 0))] * 4,
+        out_specs=[spec((rows, width), lambda b, c: (b, 0))] * 2
+        + [spec((rows, chunk), lambda b, c: (b, c))] * 3,
+        out_shape=[shape((4 * rows, width), bf16)] * 2 + [shape((4 * rows, hidden_count), bf16)] * 3,
+        scratch_shapes=[pltpu.VMEM((rows, width), bf16)] * 2
+        + [pltpu.SemaphoreType.DMA((4,)), pltpu.SemaphoreType.DMA((4,))],
+        compiler_params=pltpu.CompilerParams(
+            collective_id=1, has_side_effects=True, vmem_limit_bytes=60 * 2**20
+        ),
+        cost_estimate=pl.CostEstimate(
+            flops=16 * rows * width * hidden_count,
+            bytes_accessed=60 * 2**20,
+            transcendentals=4 * rows * hidden_count,
+        ),
+    )(*tokens[1:], *grads[1:], *tokens, *grads, *weights)
+
+
+def reduce_copies(corner, send_x, send_y, got_corner, got_x, got_y, send, receive):
+    _, over_x, over_y = neighbours()
+    half = corner.shape[0] // 2
+    low, high = pl.ds(0, half), pl.ds(half, half)
+    plan = [
+        (corner.at[low], got_corner.at[low], over_y),
+        (corner.at[high], got_corner.at[high], over_x),
+        (send_y.at[low], got_y.at[low], over_y),
+        (send_y.at[high], got_y.at[high], over_y),
+        (send_x.at[high], got_x.at[high], over_x),
+        (send_x.at[low], got_x.at[low], over_x),
     ]
+    return [
+        pltpu.make_async_remote_copy(
+            src_ref=source,
+            dst_ref=target,
+            send_sem=send.at[n],
+            recv_sem=receive.at[n],
+            device_id={"dp": other},
+            device_id_type=MESH,
+        )
+        for n, (source, target, other) in enumerate(plan)
+    ]
+
+
+def corner_copies(corner, got_corner, send, receive, first):
+    _, over_x, over_y = neighbours()
+    half = corner.shape[0] // 2
+    return [
+        pltpu.make_async_remote_copy(
+            src_ref=corner.at[rows],
+            dst_ref=got_corner.at[rows],
+            send_sem=send.at[first + n],
+            recv_sem=receive.at[first + n],
+            device_id={"dp": other},
+            device_id_type=MESH,
+        )
+        for n, (rows, other) in enumerate(
+            ((pl.ds(0, half), over_y), (pl.ds(half, half), over_x))
+        )
+    ]
+
+
+def add_into(target, rows, other):
+    total_rows = target[rows, :].astype(jnp.float32) + other[rows, :].astype(jnp.float32)
+    target[rows, :] = total_rows.astype(target.dtype)
+
+
+def feed_back_kernel(
+    grads, hidden, gate_slope, up_slope,
+    gate_own, gate_other, up_own, up_other, down_own, down_other,
+    gate_grad, up_grad, out_own, out_x, out_y, two_grad,
+    out_sum, two_sum, out_corner, keep_x, keep_y, got_out, local, corner, send_x, send_y, got_corner, got_x, got_y, send, receive,
+):
+    turn_index, chunk = pl.program_id(0), pl.program_id(1)
+    last = chunk == pl.num_programs(1) - 1
+    rows = grads.shape[0]
+    low, high = slice(0, rows // 2), slice(rows // 2, rows)
+    copies = reduce_copies(corner, send_x, send_y, got_corner, got_x, got_y, send, receive)
+    copies += corner_copies(out_corner, got_out, send, receive, len(copies))
+    writes = [
+        pltpu.make_async_copy(source, target, local.at[n])
+        for n, (source, target) in enumerate(
+            ((keep_y, out_y), (keep_x, out_x), (out_corner, out_own))
+        )
+    ]
+
+    @pl.when((turn_index == 0) & (chunk == 0))
+    def _():
+        _, over_x, over_y = neighbours()
+        greet((over_x, over_y))
+
+    @pl.when(chunk == 0)
+    def _():
+        out_sum[...] = jnp.zeros_like(out_sum)
+        two_sum[...] = jnp.zeros_like(two_sum)
+
+    hidden_grad = both_halves(grads[...], down_own, down_other)
+    gate_back = (hidden_grad * gate_slope[...].astype(jnp.float32)).astype(jnp.bfloat16)
+    up_back = (hidden_grad * up_slope[...].astype(jnp.float32)).astype(jnp.bfloat16)
+    gate_grad[...] = gate_back
+    up_grad[...] = up_back
+    active = hidden[...]
+    half = down_own.shape[1]
+    for n, (gate, up, down) in enumerate(
+        ((gate_own, up_own, down_own), (gate_other, up_other, down_other))
+    ):
+        for part in range(0, half, 512):
+            cols = slice(part, part + 512)
+            place = slice(n * half + part, n * half + part + 512)
+            out_sum[:, place] += matmul(active, down[:, cols])
+            two_sum[:, place] += matmul(gate_back, gate[:, cols]) + matmul(up_back, up[:, cols])
+
+    @pl.when(last & (turn_index == 0))
+    def _():
+        merge_columns(corner, two_sum)
+        copies[0].start()
+        copies[1].start()
+        merge_columns(out_corner, out_sum)
+        copies[6].start()
+        copies[7].start()
+
+    @pl.when(last & (turn_index == 1))
+    def _():
+        merge_columns(send_y, two_sum)
+        copies[2].start()
+        merge_columns(keep_y, out_sum)
+
+    @pl.when((chunk == 0) & (turn_index == 2))
+    def _():
+        copies[1].wait_recv()
+        add_into(send_y, high, got_corner)
+        copies[3].start()
+
+    @pl.when(last & (turn_index == 2))
+    def _():
+        merge_columns(send_x, two_sum)
+        copies[4].start()
+        copies[0].wait_recv()
+        add_into(send_x, low, got_corner)
+        copies[5].start()
+        merge_columns(keep_x, out_sum)
+        copies[7].wait_recv()
+        add_into(keep_y, high, got_out)
+        writes[0].start()
+
+    @pl.when(last & (turn_index == 3))
+    def _():
+        copies[6].wait_recv()
+        add_into(keep_x, low, got_out)
+        writes[1].start()
+        copies[6].wait_send()
+        copies[7].wait_send()
+        merge_columns(out_corner, out_sum)
+        writes[2].start()
+        merge_columns(two_grad, two_sum)
+        copies[2].wait_recv()
+        copies[3].wait_recv()
+        two_grad[...] += got_y[...].astype(jnp.float32)
+        copies[4].wait_recv()
+        copies[5].wait_recv()
+        two_grad[...] += got_x[...].astype(jnp.float32)
+        for transfer in copies[:6]:
+            transfer.wait_send()
+        for write in writes:
+            write.wait()
+
+
+def feed_back(grads, saved, weights):
+    rows, width = grads.shape[0] // 4, grads.shape[1]
+    hidden_count, half = weights[0].shape
+    chunk = 512
+    spec = pl.BlockSpec
+    shape = jax.ShapeDtypeStruct
+    bf16, f32 = jnp.bfloat16, jnp.float32
+    block = lambda q, c: (3 - q, 0)
+    piece = lambda q, c: (3 - q, c)
     return pl.pallas_call(
-        feed_kernel,
-        grid=(4,),
-        in_specs=blocks
+        feed_back_kernel,
+        grid=(4, hidden_count // chunk),
+        in_specs=[spec((rows, width), block)]
+        + [spec((rows, chunk), piece)] * 3
+        + [spec((chunk, half), lambda q, c: (c, 0))] * 6,
+        out_specs=[spec((rows, chunk), piece)] * 2
+        + [spec(memory_space=pl.ANY)] * 3
+        + [spec((rows, width), lambda q, c: (0, 0))],
+        out_shape=[shape((4 * rows, hidden_count), bf16)] * 2
+        + [shape((rows, width), bf16)] * 3
+        + [shape((rows, width), f32)],
+        scratch_shapes=[pltpu.VMEM((rows, width), f32)] * 2
+        + [pltpu.VMEM((rows, width), bf16)] * 4
+        + [pltpu.SemaphoreType.DMA((3,))]
+        + [pltpu.VMEM((rows, width), bf16)] * 6
+        + [pltpu.SemaphoreType.DMA((8,)), pltpu.SemaphoreType.DMA((8,))],
+        compiler_params=pltpu.CompilerParams(
+            collective_id=2, has_side_effects=True, vmem_limit_bytes=62 * 2**20
+        ),
+        cost_estimate=pl.CostEstimate(
+            flops=32 * rows * width * hidden_count,
+            bytes_accessed=80 * 2**20,
+            transcendentals=0,
+        ),
+    )(grads, *saved, *weights)
+
+
+def outer_kernel(extra, left_own, left_other, right_own, right_other, *refs):
+    weights = refs[:extra]
+    total_out, *spread = refs[extra : extra + (3 if extra else 1)]
+    own, corner, send_x, send_y, got_corner, got_x, got_y, send, receive = refs[-9:]
+    step = pl.program_id(0)
+    half = own.shape[0] // 2
+    low, high = slice(0, half), slice(half, 2 * half)
+    copies = reduce_copies(corner, send_x, send_y, got_corner, got_x, got_y, send, receive)
+
+    @pl.when(step == 0)
+    def _():
+        _, over_x, over_y = neighbours()
+        greet((over_x, over_y))
+
+    @pl.when(step < 8)
+    def _():
+        result = dot_first(left_own[...], right_own[...]) + dot_first(
+            left_other[...], right_other[...]
+        )
+        order = (corner, corner, send_y, send_y, send_x, send_x, own, own)
+        starts = (0, 1, 2, None, None, 4, None, None)
+        for n, (target, first) in enumerate(zip(order, starts)):
+
+            @pl.when(step == n)
+            def _():
+                target[high if n % 2 else low, :] = result.astype(target.dtype)
+                if first is not None:
+                    copies[first].start()
+
+    for n, weight in enumerate(weights):
+
+        @pl.when(step == 8 + n)
+        def _():
+            me = lax.axis_index("dp")
+            x, y = (me // 2) % 2, me // 4
+            k = min(n, 3)
+            far_x = 1 - x if k % 2 else x
+            far_y = 1 - y if k // 2 else y
+            part = 512
+            start = (2 * far_y + far_x) * part + (part // 2 if n == 4 else 0)
+            cols = pl.ds(pl.multiple_of(start, 256), weight.shape[0])
+            spread[0][:, cols] = dot_last(right_own[...], weight[...])
+            spread[1][:, cols] = dot_last(right_other[...], weight[...]).astype(jnp.bfloat16)
+
+    last = pl.num_programs(0) - 1
+
+    @pl.when(step == min(9, 7 + extra))
+    def _():
+        copies[1].wait_recv()
+        add_into(send_y, high, got_corner)
+        copies[3].start()
+        copies[0].wait_recv()
+        add_into(send_x, low, got_corner)
+        copies[5].start()
+
+    @pl.when(step == last)
+    def _():
+        for n in (2, 4, 3, 5):
+            copies[n].wait_recv()
+        total_out[...] = (
+            own[...] + got_x[...].astype(jnp.float32) + got_y[...].astype(jnp.float32)
+        ).astype(total_out.dtype)
+        for transfer in copies:
+            transfer.wait_send()
+
+
+def outer(lefts, rights, by_left, collective_id, weights=()):
+    rows = 512
+    wide = lefts[0][0].shape[1]
+    right_wide = rights[0][0].shape[1]
+    turn_of = lambda s: 6 - 2 * (jnp.minimum(s, 7) // 2) + jnp.minimum(s, 7) % 2
+    if by_left:
+        size = (wide // 8, right_wide)
+        left_size = (rows, wide // 8)
+        place_left = lambda row: lambda s: (row, turn_of(s))
+        place_right = lambda row: lambda s: (row, 0)
+    else:
+        size = (wide // 2, right_wide // 4)
+        left_size = (rows, wide // 2)
+        place_left = lambda row: lambda s: (row, s % 2)
+        place_right = lambda row: lambda s: (row, 3 - s // 2)
+    both = (2 * size[0], size[1])
+    spec, shape = pl.BlockSpec, jax.ShapeDtypeStruct
+    out_specs = [spec(both, lambda s: (0, 0))]
+    out_shape = [shape(both, jnp.bfloat16)]
+    if weights:
+        out_specs += [spec((rows, wide), lambda s: (0, 0))] * 2
+        out_shape += [shape((rows, wide), jnp.float32), shape((rows, wide), jnp.bfloat16)]
+    made = pl.pallas_call(
+        functools.partial(outer_kernel, len(weights)),
+        grid=(8 + len(weights),),
+        in_specs=[spec(left_size, place_left(row)) for _, row in lefts]
+        + [spec((rows, size[1]), place_right(row)) for _, row in rights]
         + [
-            spec(gate_up.shape, lambda t: (0, 0, 0), pipeline_mode=once),
-            spec(down.shape, lambda t: (0, 0, 0), pipeline_mode=once),
-        ]
-        + [spec(memory_space=pl.ANY)] * len(kept),
-        out_specs=[spec((tile, width), placed)] * 2
-        + [spec((tile, hidden_count), placed)] * 3
-        + [spec((tile, width), lambda t: (0, 0))] * 8,
-        out_shape=[shape((count, width), jnp.bfloat16)] * 2
-        + [shape((count, hidden_count), jnp.bfloat16)] * 3
-        + [shape((tile, width), jnp.bfloat16)] * 8,
-        input_output_aliases={10 + k: k for k in range(len(kept))},
-        compiler_params=pltpu.CompilerParams(vmem_limit_bytes=60 * 2**20),
+            spec(weight.shape, lambda s: (0, 0), pipeline_mode=pl.Buffered(1))
+            for weight in weights
+        ],
+        out_specs=out_specs,
+        out_shape=out_shape,
+        scratch_shapes=[pltpu.VMEM(both, jnp.float32)]
+        + [pltpu.VMEM(both, jnp.bfloat16)] * 6
+        + [pltpu.SemaphoreType.DMA((6,)), pltpu.SemaphoreType.DMA((6,))],
+        compiler_params=pltpu.CompilerParams(
+            collective_id=collective_id, has_side_effects=True, vmem_limit_bytes=60 * 2**20
+        ),
         cost_estimate=pl.CostEstimate(
-            flops=48 * tile * width * hidden_count,
-            bytes_accessed=40 * 2**20,
-            transcendentals=4 * tile * hidden_count,
+            flops=4 * rows * wide * right_wide, bytes_accessed=16 * 2**20, transcendentals=0
         ),
-    )(*[array for array, _ in tokens + grads], gate_up, down, *kept)
+    )(*[array for array, _ in (*lefts, *rights)], *weights)
+    return made if weights else made[0]
 
 
 def columns_kernel(transposed, place, left, w0, w1, w2, w3_low, w3_high, own, other):
@@ -754,18 +1102,6 @@
     )(place, *[array for array, _ in ins])
 
 
-def put(low_ref, high_ref, values):
-    first = pl.program_id(0) == 0
-
-    @pl.when(first)
-    def _():
-        low_ref[...] = values
-
-    @pl.when(jnp.logical_not(first))
-    def _():
-        high_ref[...] = values
-
-
 def choose(low_ref, high_ref):
     return jnp.where(pl.program_id(0) == 0, low_ref[...], high_ref[...]).astype(jnp.float32)
 
@@ -790,17 +1126,16 @@
     relabelled(normed, values.astype(jnp.bfloat16), place)
 
 
-def middle_kernel(place, inputs, own, other, gain, middle, low, high):
+def middle_kernel(place, inputs, own, other, gain, middle, normed):
     values = inputs[...].astype(jnp.float32) + own[...] + other[...].astype(jnp.float32)
     middle[...] = values
-    put(low, high, norm_rows(values, gain[...])[0].astype(jnp.bfloat16))
+    normed[...] = norm_rows(values, gain[...])[0].astype(jnp.bfloat16)
 
 
 def middle_back_kernel(
-    place, middle, cotangent, own_low, own_high, x_low, x_high, y_low, y_high, gain,
-    middle_grad, branch, gain_grad,
+    place, middle, cotangent, two, gain, middle_grad, branch, gain_grad
 ):
-    two_grad = choose(own_low, own_high) + choose(x_low, x_high) + choose(y_low, y_high)
+    two_grad = two[...]
     values = middle[...]
     _, factor = norm_rows(values, gain[...])
     add_gain(gain_grad, two_grad * values * factor)
@@ -821,11 +1156,9 @@
     rounded[...] = grads.astype(jnp.bfloat16)
 
 
-def output_kernel(
-    place, middle, own_low, own_high, x_low, x_high, y_low, y_high, output
-):
-    total_out = choose(own_low, own_high) + choose(x_low, x_high) + choose(y_low, y_high)
-    output[...] = (middle[...] + total_out).astype(jnp.bfloat16)
+def output_kernel(place, middle, own, over_x, over_y, output):
+    parts = [part[...].astype(jnp.float32) for part in (own, over_x, over_y)]
+    output[...] = (middle[...] + parts[0] + parts[1] + parts[2]).astype(jnp.bfloat16)
 
 
 def exchange(values, bit):
@@ -845,29 +1178,13 @@
     return lax.optimization_barrier((values, earlier))[0]
 
 
-def gather_weights(block):
-    half = block.shape[0] // 2
-    over_x = exchange(block, 2)
-    over_y = exchange(block, 4)
-    return [
-        block,
-        over_x,
-        over_y,
-        exchange(over_x[:half], 4),
-        exchange(over_y[half:], 2),
-    ]
-
-
-def gather_near(low, high):
-    return [exchange(low, 2), exchange(high, 2), exchange(low, 4), exchange(high, 4)]
+def gather_near(block):
+    return [exchange(block, 2), exchange(block, 4)]
 
 
 def gather_far(near):
-    return [exchange(near[0], 4), exchange(near[3], 2)]
-
-
-def both_cores(halves):
-    return list(halves) + [exchange(half, 1) for half in halves]
+    half = near[0].shape[0] // 2
+    return [exchange(near[0][:half], 4), exchange(near[1][half:], 2)]
 
 
 def add_low(left, right):
@@ -918,7 +1235,7 @@
     planes = 4
     rows = layer_input.shape[0]
     width = layer_input.shape[1]
-    units = w_gate.shape[1] // 8
+    units = w_gate.shape[1] // planes
     array = jax.ShapeDtypeStruct
 
     query_cols = w_query.shape[1] // 2
@@ -943,23 +1260,35 @@
         1,
     )
     qkv_z = lax.all_gather(qkv_pair, "mp", axis=1, tiled=True)
-    out_z = lax.all_gather(out_pair, "mp", axis=0, tiled=True)
-
     pieces = jnp.concatenate(
-        [w.reshape(8, units, w.shape[1]) for w in (w_gate.T, w_up.T, w_down)], 1
-    )
-    feed_own = lax.all_to_all(pieces, "dp", 0, 0)
-    feed_own = jnp.swapaxes(feed_own, 0, 1).reshape(3 * units, width)
-
-    inputs = jnp.where(crossing, swap_halves(layer_input), layer_input)
-    cotangent = jnp.where(crossing, swap_halves(out_grad), out_grad)
+        [w.reshape(planes, units, w.shape[1]) for w in (w_gate.T, w_up.T, w_down)], 1
+    )
+
+    def piece_for(k):
+        return pick(pieces, place[0] ^ k, 1, 0)[0]
+
+    feed_own = jnp.concatenate(
+        [piece_for(0)] + [exchange(piece_for(k), 2 * k) for k in (1, 2, 3)], 1
+    )
 
     qkv_z = after(qkv_z, feed_own)
-    qkv_chips = gather_weights(qkv_z)
-    out_z = after(out_z, qkv_chips)
-    out_chips = gather_weights(out_z)
-    gate_up = lax.all_gather(feed_own[: 2 * units], "mp", axis=0)
-    down = lax.all_gather(feed_own[2 * units :], "mp", axis=0)
+    qkv_near = gather_near(qkv_z)
+    moved = swap_halves(after(layer_input, qkv_z))
+    moved_grad = swap_halves(after(out_grad, qkv_z))
+    out_z = lax.all_gather(
+        after(out_pair, (moved, moved_grad, qkv_near)), "mp", axis=0, tiled=True
+    )
+
+    qkv_chips = [qkv_z, *qkv_near, *gather_far(qkv_near)]
+    inputs = jnp.where(crossing, moved, layer_input)
+    cotangent = jnp.where(crossing, moved_grad, out_grad)
+
+    out_near = gather_near(after(out_z, qkv_chips))
+    feed_own = after(feed_own, (out_z, qkv_chips))
+    gate_half, up_half, down_half = [
+        lax.all_gather(feed_own[n * units : (n + 1) * units], "mp", axis=0, tiled=True)
+        for n in range(3)
+    ]
 
     gain_one, gain_two = norm_attn[None, :], norm_mlp[None, :]
     gain_query, gain_key = query_norm[None, :], key_norm[None, :]
@@ -970,7 +1299,7 @@
         [(array((rows, width), bf16), "rows")],
         4,
     )
-    normed_other = exchange(normed, 1)
+    normed_other = after(exchange(normed, 1), (out_z, cotangent))
     cosines, sines = wide_tables(2 * rows)
     proj, query_rot, key_rot, value_low, attended, log_total = attend(
         core_index,
@@ -984,65 +1313,62 @@
         planes,
         query_cols,
     )
+    out_near = after(out_near, attended)
+    out_chips = [out_z, *out_near, *gather_far(out_near)]
+    grads_near = gather_near(after(cotangent, qkv_chips))
     branch_own, branch_other = columns(place, attended, out_chips, False)
-    middle, tokens_low, tokens_high = tile_call(
+    middle, tokens = tile_call(
         middle_kernel,
         place,
-        [(inputs, "rows"), (branch_own, "rows"), (exchange(branch_other, 1), "rows"), (gain_two, 1)],
+        [(inputs, "rows"), (branch_own, "rows"), (after(exchange(branch_other, 1), grads_near), "rows"), (gain_two, 1)],
         [
             (array((rows, width), f32), "rows"),
-            (array((rows // 2, width), bf16), "low"),
-            (array((rows // 2, width), bf16), "high"),
+            (array((rows, width), bf16), "rows"),
         ],
         14,
     )
 
-    grads_low, grads_high = after(
-        (cotangent[: rows // 2], cotangent[rows // 2 :]), (out_chips[1], out_chips[2])
-    )
-    grads_near = gather_near(grads_low, grads_high)
-    tokens_near = gather_near(tokens_low, tokens_high)
-    tokens_far = gather_far(tokens_near)
-    grads_far = gather_far(after(grads_near, tokens_near))
-
-    def quarters(low, high, near, far):
-        halves = [[low, high], near[:2], near[2:], far]
-        return [[(half, 0) for half in both_cores(pair)] for pair in halves]
-
-    token_blocks = quarters(tokens_low, tokens_high, tokens_near, tokens_far)
-    grad_blocks = quarters(grads_low, grads_high, grads_near, grads_far)
-    kept = None
-    outs, twos = [], []
-    for k in range(4):
-        made = feed(k, kept, token_blocks[k], grad_blocks[k], gate_up, down)
-        kept, out_tiles, two_tiles = made[:5], made[5:9], made[9:]
-        outs.append(out_tiles)
-        twos.append([add_low(two_tiles[n], exchange(two_tiles[n + 2], 1)) for n in range(2)])
-    all_tokens, all_grads, all_hidden, all_gate, all_up = kept
-
-    def collect(blocks):
-        (own, over_x, over_y, corner) = blocks
-        x_high = exchange(over_x[1], 2)
-        y_low = exchange(over_y[0], 4)
-        low = exchange(corner[0], 4)
-        high = exchange(corner[1], 2)
-        x_low = exchange(add_low(over_x[0], low), 2)
-        y_high = exchange(add_low(over_y[1], high), 4)
-        return [own[0], own[1], x_low, x_high, y_low, y_high]
-
-    two_parts = collect(twos)
-    gate_weight_grad = dot_first(all_gate, all_tokens).astype(bf16)
-    up_weight_grad = dot_first(all_up, all_tokens).astype(bf16)
-    down_grad = dot_first(all_hidden, all_grads).astype(bf16)
-    outs = after(outs, two_parts)
-    out_parts = collect(
-        [[add_low(tiles[n], exchange(tiles[n + 2], 1)) for n in range(2)] for tiles in outs]
-    )
-    halves = ("low", "high") * 3
+    gate_half = after(gate_half, attended)
+    up_half = after(up_half, tokens)
+    gate_w, up_w = [[half, exchange(half, 1)] for half in (gate_half, up_half)]
+    tokens_near = gather_near(tokens)
+    all_tokens, all_grads, all_hidden, gate_slope, up_slope = gather_hidden(
+        [tokens, *tokens_near], [cotangent, *grads_near], [*gate_w, *up_w]
+    )
+    down_half = after(down_half, tokens_near)
+    down_w = [down_half, exchange(down_half, 1)]
+
+    def over_z(grad):
+        return lax.psum_scatter(grad, "mp", scatter_dimension=0, tiled=True)
+
+    def weight_grad(left, right):
+        half = right.shape[1] // 2
+        other = exchange(dot_first(left, right[:, half:]).astype(bf16), 1)
+        return (dot_first(left, right[:, :half]) + other.astype(f32)).astype(bf16)
+
+    down_local = weight_grad(all_hidden, all_grads)
+    down_sum = over_z(down_local)
+    all_gate, all_up, out_own, out_x, out_y, two_grad = feed_back(
+        after(all_grads, down_local),
+        [all_hidden, gate_slope, up_slope],
+        [*gate_w, *up_w, *down_w],
+    )
+    half = width // 2
+    gate_other = dot_first(all_gate, all_tokens[:, half:]).astype(bf16)
+    up_other = dot_first(all_up, all_tokens[:, half:]).astype(bf16)
+    all_gate, all_up = after((all_gate, all_up), (gate_other, up_other))
+
+    def own_half(left, other):
+        own = dot_first(left, all_tokens[:, :half])
+        return (own + exchange(other, 1).astype(f32)).astype(bf16)
+
+    gate_local = own_half(all_gate, gate_other)
+    up_local = own_half(all_up, up_other)
+    gate_sum, up_sum = over_z(gate_local), over_z(up_local)
     middle_grad, branch, gain_two_part = tile_call(
         middle_back_kernel,
         place,
-        [(middle, "rows"), (cotangent, "rows"), *zip(two_parts, halves), (gain_two, 1)],
+        [(middle, "rows"), (cotangent, "rows"), (two_grad, "rows"), (gain_two, 1)],
         [
             (array((rows, width), f32), "rows"),
             (array((rows, width), bf16), "rows"),
@@ -1051,21 +1377,24 @@
         18,
     )
 
-    def over_z(grad):
-        return lax.psum_scatter(grad, "mp", scatter_dimension=0, tiled=True)
-
     def unspread(own):
-        pieces = jnp.swapaxes(own.reshape(own.shape[0], 8, -1), 0, 1)
-        return lax.all_to_all(pieces, "dp", 0, 0)
-
-    gate_up_own = unspread(
-        jnp.concatenate([over_z(gate_weight_grad), over_z(up_weight_grad)], 0)
-    )
-    gate_own = gate_up_own[:, :units].reshape(8 * units, -1).T.astype(f32)
-    up_own = gate_up_own[:, units:].reshape(8 * units, -1).T.astype(f32)
-    down_own = unspread(over_z(down_grad)).reshape(8 * units, -1).astype(f32)
-
-    branch_pair = exchange(branch, 1)
+        cols = own.shape[1] // planes
+        got = [own[:, :cols]] + [
+            exchange(own[:, k * cols : (k + 1) * cols], 2 * k) for k in (1, 2, 3)
+        ]
+        return jnp.concatenate(got, 1), cols
+
+    def chips_in_order(got, cols, rows):
+        return jnp.concatenate([pick(got[rows], place[0] ^ k, cols, 1) for k in range(planes)], 0)
+
+    gate_up_got, cols = unspread(jnp.concatenate([gate_sum, up_sum], 0))
+    gate_own = chips_in_order(gate_up_got, cols, slice(0, units)).T.astype(f32)
+    up_own = chips_in_order(gate_up_got, cols, slice(units, 2 * units)).T.astype(f32)
+    down_got, cols = unspread(down_sum)
+    down_own = chips_in_order(down_got, cols, slice(0, units)).astype(f32)
+
+    branch_pair = after(exchange(branch, 1), (gate_local, up_local))
+    out_parts = [out_own, exchange(after(out_x, branch_pair), 2), exchange(after(out_y, branch_pair), 4)]
     proj_grad, head_gains = attend_back(
         core_index,
         branch,
@@ -1080,38 +1409,23 @@
         query_cols,
     )
 
-    def chip_grads(left, right, along):
-        blocks = []
-        for k in range(4):
-            pair = []
-            for n in range(2):
-                if along == 0:
-                    part = left.shape[1] // 8
-                    first = left[:, (2 * k + n) * part : (2 * k + n + 1) * part]
-                    pair.append(dot_first(first, right))
-                else:
-                    part, depth = right.shape[1] // 4, left.shape[1] // 2
-                    first = left[:, n * depth : (n + 1) * depth]
-                    pair.append(dot_first(first, right[:, k * part : (k + 1) * part]))
-            blocks.append([half.astype(bf16) for half in pair])
-        return blocks
-
-    def gathered(parts):
-        own_low, own_high, x_low, x_high, y_low, y_high = [p.astype(f32) for p in parts]
-        return jnp.concatenate(
-            [own_low + x_low + y_low, own_high + x_high + y_high], 0
-        ).astype(bf16)
-
-    branch_all = jnp.concatenate([branch, branch_pair], 0)
-    out_sum = over_z(gathered(collect(chip_grads(attended, branch_all, 1))))
-    normed_all = jnp.concatenate([normed, normed_other], 0)
-    one_own, one_other = columns(place, proj_grad, qkv_chips, True)
-    qkv_sum = lax.psum_scatter(
-        gathered(collect(chip_grads(normed_all, proj_grad, 0))),
-        "mp",
-        scatter_dimension=1,
-        tiled=True,
-    )
+    out_parts = after(out_parts, proj_grad)
+    (layer_output,) = tile_call(
+        output_kernel,
+        place,
+        [(middle, "rows")] + [(part, "rows") for part in out_parts],
+        [(array((rows, width), bf16), "rows")],
+        12,
+    )
+    proj_grad = after(proj_grad, (layer_output, down_own))
+    qkv_local, one_own, one_other = outer(
+        [(normed, 0), (normed_other, 0)], [(proj_grad, 0), (proj_grad, 1)], True, 3, qkv_chips
+    )
+    qkv_sum = lax.psum_scatter(qkv_local, "mp", scatter_dimension=1, tiled=True)
+    output_moved = swap_halves(layer_output)
+    attended = after(attended, (qkv_local, output_moved, gate_sum, up_sum))
+    out_local = outer([(attended, 0), (attended, 1)], [(branch, 0), (branch_pair, 0)], False, 4)
+    out_sum = over_z(after(out_local, qkv_sum))
     input_grad, rounded_grad, gain_one_part = tile_call(
         input_back_kernel,
         place,
@@ -1129,35 +1443,28 @@
         ],
         18,
     )
-    (layer_output,) = tile_call(
-        output_kernel,
-        place,
-        [(middle, "rows"), *zip(out_parts, halves)],
-        [(array((rows, width), bf16), "rows")],
-        12,
-    )
-    pair_rows = qkv_sum.shape[0] // 2
-    qkv_other = exchange(pick(qkv_sum, 1 - core, pair_rows, 0), 1)
-    qkv_own = pick(qkv_sum, core, pair_rows, 0)
-
-    def both(start, stop):
-        return in_order(qkv_own[:, start:stop], qkv_other[:, start:stop], core, 1).astype(f32)
-
-    pair_cols = out_sum.shape[1] // 2
-    out_other = exchange(pick(out_sum, 1 - core, pair_cols, 1), 1)
-    out_own = pick(out_sum, core, pair_cols, 1)
     gain_sums = total(
-        jnp.concatenate(
+        after(jnp.concatenate(
             [
                 jnp.sum(gain_one_part, 0),
                 jnp.sum(head_gains[:8], 0),
                 jnp.sum(head_gains[8:], 0),
                 jnp.sum(gain_two_part, 0),
             ]
-        )
-    )
+        ), out_local)
+    )
+    pair_rows = qkv_sum.shape[0] // 2
+    qkv_other = exchange(pick(qkv_sum, 1 - core, pair_rows, 0), 1)
+    qkv_own = pick(qkv_sum, core, pair_rows, 0)
+
+    def both(start, stop):
+        return in_order(qkv_own[:, start:stop], qkv_other[:, start:stop], core, 1).astype(f32)
+
+    pair_cols = out_sum.shape[1] // 2
+    out_other = exchange(pick(out_sum, 1 - core, pair_cols, 1), 1)
+    out_own = pick(out_sum, core, pair_cols, 1)
     return (
-        jnp.where(crossing, swap_halves(layer_output), layer_output),
+        jnp.where(crossing, output_moved, layer_output),
         jnp.where(crossing, swap_halves(rounded_grad).astype(f32), input_grad),
         gain_sums[:width],
         gain_sums[width : width + HEAD_SIZE],

time: 977 us -> 917 us (0.939); the launches traced: 959 us -> 912 us
  Pallas kernels: 275 us -> 393 us
  waiting for transfers between devices: 366 us -> 304 us
  matrix products: 99.3 us -> 61.2 us
  other arithmetic: 58.9 us -> 22.5 us
  local copies, waits for them, and re-layouts: 38.1 us -> 23.6 us
  starting transfers between devices: 106 us -> 91.5 us
    pallas_call x4, Pallas kernels: 147 us -> 284 us  [the longest x1 115 us: feed_back(): pl.pallas_call(feed_back_kernel, grid=(4, hidden_count // chunk), in_spec...]
    ppermute x87 -> x40, waiting for transfers between devices: 332 us -> 236 us  [exchange(): return lax.ppermute(values, 'dp', [(i, i ^ bit) for i in range(8)])]
    dot_general x19 -> x6, matrix products: 99.3 us -> 61.2 us  [dot_first(): lax.dot_general(left, right, (((0,), (0,)), ((), ())), preferred_element_...]
    convert_element_type x19 -> x3, other arithmetic: 32.2 us -> 1.49 us  [the longest x1 1.26 us: fast(): down_own = chips_in_order(down_got, cols, slice(0, units)).astype(f32)]
    all_to_all x3 -> x0, waiting for transfers between devices: 26.8 us -> none  [the longest x1 26.8 us: fast(): feed_own = lax.all_to_all(pieces, 'dp', 0, 0)]
    ppermute x2, waiting for transfers between devices: 0.01 us -> 20.7 us  [total(): lax.ppermute(values, 'mp', [(i, i ^ bit) for i in range(4)])]
    reduce_scatter x4, waiting for transfers between devices: 0.01 us -> 17 us  [over_z(): return lax.psum_scatter(grad, 'mp', scatter_dimension=0, tiled=True)]
    pallas_call x2 -> x1, Pallas kernels: 25.4 us -> 9.16 us  [columns(): pl.pallas_call(functools.partial(columns_kernel, transposed), grid_spec=p...]
  transfers between devices with their start and end apart: 105 -> 56, of which waited for: 34 -> 29; matrix products, arithmetic and copies ran while one was open for 17% -> 10% of each run, Pallas kernels for 25% -> 43%
where the time goes in v2:
time: 917 us; the launch traced here: 912 us
  Pallas kernels  393 us (43%)
  waiting for transfers between devices  304 us (33%)
  starting transfers between devices  91.5 us (10%)
  matrix products  61.2 us (7%)
  local copies, waits for them, and re-layouts  23.6 us (3%)
  other arithmetic  22.5 us (2%)
  between operations  15.1 us (2%)
    ppermute x40, waiting for transfers between devices, exchange(): return lax.ppermute(values, 'dp', [(i, i ^ bit) for i in range(8)])  236 us
    pallas_call x1, Pallas kernels, feed_back(): pl.pallas_call(feed_back_kernel, grid=(4, hidden_count // chunk), in_spec...  115 us
    pallas_call x2, Pallas kernels, outer(): pl.pallas_call(functools.partial(outer_kernel, len(weights)), grid=(8 + l...  104 us
    ppermute x40, starting transfers between devices, exchange(): return lax.ppermute(values, 'dp', [(i, i ^ bit) for i in range(8)])  78 us
    pallas_call x1, Pallas kernels, gather_hidden(): pl.pallas_call(hidden_kernel, grid=(4, hidden_count // chunk), in_specs=[...  64.8 us
    dot_general x6, matrix products, dot_first(): lax.dot_general(left, right, (((0,), (0,)), ((), ())), preferred_element_...  61.2 us
    pallas_call x1, Pallas kernels, attend_back(): pl.pallas_call(attend_back_kernel, grid_spec=pltpu.PrefetchScalarGridSpec...  40 us
    pallas_call x5, Pallas kernels, tile_call(): pl.pallas_call(kernel, grid_spec=pltpu.PrefetchScalarGridSpec(num_scalar_...  32.7 us
  transfers between devices with their start and end apart: 56, of which 29 were waited for; matrix products, arithmetic and copies ran while one was open for 10% of the time, Pallas kernels for 43%

profile of v2, /device:TPU:0, one launch (start us, length us, event | category | flops | bytes accessed | tf_op | source)
XLA Modules:
  0.0 911.8 jit_solution(7106130000558018170)
XLA Ops:
  18.5 13.5 %collective-permute-done.3 = bf16[1152,256]{1,0:T(8,128)(2,1)S(1)} collective-permute-done((bf16[1152,256]{1,0:T(8,128)(2,1)S(1)}, bf16[1152,256]{1,0:T(8,128)(2,1)S(1)}, u32[]{:S(2)}, u32[]{:S(2)}) %collective-permute-start.3) | collective-permute-done | bytes 589856 | tf_op jit(solution)/shard_map/ppermute | solution.py:1165
  32.0 12.1 %collective-permute-done.2 = bf16[1152,256]{1,0:T(8,128)(2,1)S(1)} collective-permute-done((bf16[1152,256]{1,0:T(8,128)(2,1)S(1)}, bf16[1152,256]{1,0:T(8,128)(2,1)S(1)}, u32[]{:S(2)}, u32[]{:S(2)}) %collective-permute-start.2) | collective-permute-done | bytes 589856 | tf_op jit(solution)/shard_map/ppermute | solution.py:1165
  44.7 16.9 %all-gather.6.cloned.1.call-done.w0.refs_0_ = bf16[512,2048]{1,0:T(8,128)(2,1)} async-done(((bf16[512,512]{1,0:T(8,128)(2,1)}), bf16[512,2048]{1,0:T(8,128)(2,1)}) %all-gather.6.cloned.1.call-update) | async-done | bytes 2097168 | tf_op jit(solution)/shard_map/all_gather | solution.py:1262
  71.3 42.8 %collective-permute-done.8.w1.refs_1_ = bf16[512,2048]{1,0:T(8,128)(2,1)} collective-permute-done((bf16[512,2048]{1,0:T(8,128)(2,1)}, bf16[512,2048]{1,0:T(8,128)(2,1)}, u32[]{:S(2)}, u32[]{:S(2)}) %collective-permute-start.8) | collective-permute-done | bytes 2097184 | tf_op jit(solution)/shard_map/ppermute | solution.py:1165
  120.6 21.8 %collective-permute-done.10.w3_low.refs_3_ = bf16[256,2048]{1,0:T(8,128)(2,1)S(1)} collective-permute-done((bf16[256,2048]{1,0:T(8,128)(2,1)S(1)}, bf16[256,2048]{1,0:T(8,128)(2,1)S(1)}, u32[]{:S(2)}, u32[]{:S(2)}) %collective-permute-start.10) | collective-permute-done | bytes 1048608 | tf_op jit(solution)/shard_map/ppermute | solution.py:1165
  159.5 27.5 %shard_map.229 = (f32[1024,2048]{1,0:T(8,128)}, bf16[1024,1024]{1,0:T(8,128)(2,1)}, bf16[1024,512]{1,0:T(8,128)(2,1)}, bf16[1024,512]{1,0:T(8,128)(2,1)}, bf16[1...) custom-call(s32[1]{0:T(128)} %bitcast.10.core, bf16[512,2048]{1,0:T(8,128)(2,1)} %shard_map.228.own.left_own, ...), custom_call_target="tpu_custom_call" | custom-call | flops 11811160064 | bytes 31457280 | tf_op jit(solution)/shard_map/pallas_call | solution.py:419
  191.3 10.6 %collective-permute-done.14.w3_low.o3_low = bf16[512,512]{1,0:T(8,128)(2,1)S(1)} collective-permute-done((bf16[512,512]{1,0:T(8,128)(2,1)S(1)}, bf16[512,512]{1,0:T(8,128)(2,1)S(1)}, u32[]{:S(2)}, u32[]{:S(2)}) %collective-permute-start.14) | collective-permute-done | bytes 524320 | tf_op jit(solution)/shard_map/ppermute | solution.py:1165
  204.3 9.2 %shard_map.230 = (f32[512,2048]{1,0:T(8,128)}, bf16[512,2048]{1,0:T(8,128)(2,1)}) custom-call(s32[1]{0:T(128)} %bitcast.place, bf16[1024,1024]{1,0:T(8,128)(2,1)} %get-tuple-element.128.left.left_own.left_other, bf16[1024,512]{1,0:T(8,128)(2,1)} %all-gather.8.cloned.1.call-done.w0.o0, bf16[1024,512]{1,0:T(8,128)(2,1)} %copy-done.11, ...), custom_call_target="tpu_custom_call" | custom-call | flops 4294967296 | bytes 20971520 | tf_op jit(solution)/shard_map/pallas_call | solution.py:1062
  213.5 34.5 %collective-permute-done.17.x_grads_out.x_grads = bf16[512,2048]{1,0:T(8,128)(2,1)S(1)} collective-permute-done((bf16[512,2048]{1,0:T(8,128)(2,1)S(1)}, bf16[512,2048]{1,0:T(8,128)(2,1)S(1)}, u32[]{:S(2)}, u32[]{:S(2)}) %collective-permute-start.17) | collective-permute-done | bytes 2097184 | tf_op jit(solution)/shard_map/ppermute | solution.py:1165
  250.6 6.1 shard_map.231
  256.7 13.9 %all-gather.12.cloned.1.call-done.up_own = bf16[1536,1024]{1,0:T(8,128)(2,1)} async-done(((bf16[384,1024]{1,0:T(8,128)(2,1)}), bf16[1536,1024]{1,0:T(8,128)(2,1)}) %all-gather.12.cloned.1.call-update) | async-done | bytes 3145744 | tf_op jit(solution)/shard_map/all_gather | solution.py:1289
  273.9 45.1 %collective-permute-done.19.x_tokens_out.x_tokens = bf16[512,2048]{1,0:T(8,128)(2,1)} collective-permute-done((bf16[512,2048]{1,0:T(8,128)(2,1)}, bf16[512,2048]{1,0:T(8,128)(2,1)}, u32[]{:S(2)}, u32[]{:S(2)}) %collective-permute-start.19) | collective-permute-done | bytes 2097184 | tf_op jit(solution)/shard_map/ppermute | solution.py:1165
  321.9 64.8 %shard_map.232 = (bf16[2048,2048]{1,0:T(8,128)(2,1)}, bf16[2048,2048]{1,0:T(8,128)(2,1)}, bf16[2048,1536]{1,0:T(8,128)(2,1)}, bf16[2048,1536]{1,0:T(8,128)(2,1)}, bf16[2048,1536]{1,0:T(8,128)(2,1)}) custom-call(bf16[512,2048]{1,0:T(8,128)(2,1)} %collective-permute-done.19.x_tokens_out.x_tokens, ...), custom_call_target="tpu_custom_call" | custom-call | flops 25769803776 | bytes 62914560 | tf_op jit(solution)/shard_map/pallas_call | solution.py:704
  386.7 11.3 %fusion.3 = bf16[1536,1024]{1,0:T(8,128)(2,1)} fusion(bf16[2048,1536]{1,0:T(8,128)(2,1)} %get-tuple-element.91.hidden, bf16[2048,2048]{1,0:T(8,128)(2,1)} %get-tuple-element.92.grads), kind=kOutput, calls=%fused_computation.9 | convolution fusion | flops 6444023808 | bytes 13631488 | tf_op jit(solution)/shard_map/dot_general | solution.py:77
  398.5 9.8 %collective-permute-done.23 = bf16[1536,1024]{1,0:T(8,128)(2,1)S(1)} collective-permute-done((bf16[1536,1024]{1,0:T(8,128)(2,1)}, bf16[1536,1024]{1,0:T(8,128)(2,1)S(1)}, u32[]{:S(2)}, u32[]{:S(2)}) %collective-permute-start.23) | collective-permute-done | bytes 3145760 | tf_op jit(solution)/shard_map/ppermute | solution.py:1165
  408.3 11.3 %add_convert_fusion.2 = bf16[1536,1024]{1,0:T(8,128)(2,1)} fusion(bf16[1536,1024]{1,0:T(8,128)(2,1)S(1)} %collective-permute-done.23, bf16[2048,1536]{1,0:T(8,128)(2,1)} %get-tuple-element.91.hidden, bf16[2048,2048]{1,0:T(8,128)(2,1)} %get-tuple-element.92.grads), kind=kOutput, calls=%fused_computation.2 | convolution fusion | flops 6447169536 | bytes 16777216 | tf_op jit(solution)/shard_map/dot_general | solution.py:77
  420.0 115.1 %shard_map.233 = (bf16[2048,1536]{1,0:T(8,128)(2,1)}, bf16[2048,1536]{1,0:T(8,128)(2,1)}, bf16[512,2048]{1,0:T(8,128)(2,1)}, bf16[512,2048]{1,0:T(8,128)(2,1)}, ...) custom-call(bf16[2048,2048]{1,0:T(8,128)(2,1)} %get-tuple-element.92.grads, bf16[2048,1536]{1,0:T(8,128)(2,1)} %get-tuple-element.91.hidden, ...), custom_call_target="tpu_custom_call" | custom-call | flops 51539607552 | bytes 83886080 | tf_op jit(solution)/shard_map/pallas_call | solution.py:881
  535.1 10.3 %convolution_convert_fusion.1 = bf16[1536,1024]{1,0:T(8,128)(2,1)S(1)} fusion(bf16[2048,1536]{1,0:T(8,128)(2,1)} %get-tuple-element.103, bf16[2048,2048]{1,0:T(8,128)(2,1)} %get-tuple-element.102), kind=kOutput, calls=%fused_computation.8 | convolution fusion | flops 6444023808 | bytes 13631488 | tf_op jit(solution)/shard_map/dot_general | solution.py:77
  545.5 8.9 convolution_convert_fusion
  554.5 8.2 add_convert_fusion.1
  568.6 11.3 %add_convert_fusion = bf16[1536,1024]{1,0:T(8,128)(2,1)} fusion(bf16[1536,1024]{1,0:T(8,128)(2,1)S(1)} %collective-permute-done.27, bf16[2048,1536]{1,0:T(8,128)(2,1)} %get-tuple-element.104, bf16[2048,2048]{1,0:T(8,128)(2,1)} %get-tuple-element.102), kind=kOutput, calls=%fused_computation | convolution fusion | flops 6447169536 | bytes 16777216 | tf_op jit(solution)/shard_map/dot_general | solution.py:77
  580.0 8.1 shard_map.234
  600.7 40.0 %shard_map.235 = (bf16[1024,2048]{1,0:T(8,128)(2,1)}, f32[16,128]{1,0:T(8,128)}) custom-call(s32[1]{0:T(128)} %bitcast.10.core, bf16[512,2048]{1,0:T(8,128)(2,1)} %get-tuple-element.99.own.right_own, bf16[512,2048]{1,0:T(8,128)(2,1)} %copy-done.17, bf16[1024,512]{1,0:T(8,128)(2,1)} %all-gather.8.cloned.1.call-done.w0.o0, bf16[1024,512]{1,0:T(8,128)(2,1)} %copy-done.11, ...), custom_call_target="tpu_custom_call" | custom-call | flops 12884901888 | bytes 31457280 | tf_op jit(solution)/shard_map/pallas_call | solution.py:546
  648.1 5.9 shard_map.236
  655.5 79.3 %shard_map.237 = (bf16[512,2048]{1,0:T(8,128)(2,1)}, f32[512,2048]{1,0:T(8,128)}, bf16[512,2048]{1,0:T(8,128)(2,1)}) custom-call(bf16[512,2048]{1,0:T(8,128)(2,1)} %shard_map.228.own.left_own, bf16[512,2048]{1,0:T(8,128)(2,1)} %collective-permute-done.5.other.left_other, bf16[1024,2048]{1,0:T(8,128)(2,1)} %get-tuple-element.119.right_own.right_other, ...), custom_call_target="tpu_custom_call" | custom-call | flops 8589934592 | bytes 16777216 | tf_op jit(solution)/shard_map/pallas_call | solution.py:997
  739.3 9.4 %shard_map.238 = (f32[512,2048]{1,0:T(8,128)}, bf16[512,2048]{1,0:T(8,128)(2,1)}, f32[8,2048]{1,0:T(8,128)}) custom-call(s32[1]{0:T(128)} %bitcast.place, bf16[512,2048]{1,0:T(8,128)(2,1)} %broadcast_select_fusion.2.inputs, f32[512,2048]{1,0:T(8,128)} %get-tuple-element.118.middle_grad, f32[512,2048]{1,0:T(8,128)} %get-tuple-element.120.own, ...), custom_call_target="tpu_custom_call" | custom-call | flops 20971520 | bytes 18874368 | tf_op jit(solution)/shard_map/pallas_call | solution.py:1089
  749.7 25.1 %shard_map.239 = bf16[1024,512]{1,0:T(8,128)(2,1)} custom-call(bf16[1024,1024]{1,0:T(8,128)(2,1)} %get-tuple-element.128.left.left_own.left_other, bf16[1024,1024]{1,0:T(8,128)(2,1)} %get-tuple-element.128.left.left_own.left_other, bf16[512,2048]{1,0:T(8,128)(2,1)} %get-tuple-element.99.own.right_own, bf16[512,2048]{1,0:T(8,128)(2,1)} %copy-done.17), custom_call_target="tpu_custom_call" | custom-call | flops 4294967296 | bytes 16777216 | tf_op jit(solution)/shard_map/pallas_call | solution.py:997
  774.7 45.7 %collective-permute-start.36 = (f32[4352]{0:T(1024)S(1)}, f32[4352]{0:T(1024)S(1)}, u32[]{:S(2)}, u32[]{:S(2)}) collective-permute-start(f32[4352]{0:T(1024)S(1)} %pad_maximum_fusion.7), channel_id=1, source_target_pairs={{0,4},{4,0},{8,12},{12,8},{16,20},{20,16},{24,28},{28,24},{1,5},{5... | collective-permute-start | bytes 52232 | tf_op jit(solution)/shard_map/ppermute | solution.py:1165
  832.7 20.7 %collective-permute-done.39 = f32[4352]{0:T(1024)S(1)} collective-permute-done((f32[4352]{0:T(1024)S(1)}, f32[4352]{0:T(1024)S(1)}, u32[]{:S(2)}, u32[]{:S(2)}) %collective-permute-start.39) | collective-permute-done | bytes 17440 | tf_op jit(solution)/shard_map/ppermute | solution.py:1210
  859.3 8.3 collective-permute-done.45
  878.1 6.0 convert_select_fusion
  884.1 17.0 %reduce-scatter.14.cloned.1.call-done = bf16[256,512]{1,0:T(8,128)(2,1)} async-done(((bf16[1024,512]{1,0:T(8,128)(2,1)}), bf16[256,512]{1,0:T(8,128)(2,1)}) %reduce-scatter.14.cloned.1.call-update) | async-done | bytes 262160 | tf_op jit(solution)/shard_map/reduce_scatter | solution.py:1342
  (225 shorter events, 126.4 us)
Async XLA Ops:
  7.2 54.4 %all-gather.6.cloned.1.call-start = ((), (), s32[]{:S(2)}) async-start(), calls=%async_computation.5 | async-start | bytes 2621440 | tf_op jit(solution)/shard_map/all_gather | solution.py:1262
  12.9 132.1 %all-gather.8.cloned.1.call-start = ((), (), s32[]{:S(2)}) async-start(), calls=%async_computation.6 | async-start | bytes 1310720 | tf_op jit(solution)/shard_map/all_gather | solution.py:1278
  17.8 26.3 %collective-permute-start.2 = (bf16[1152,256]{1,0:T(8,128)(2,1)S(1)}, bf16[1152,256]{1,0:T(8,128)(2,1)S(1)}, u32[]{:S(2)}, u32[]{:S(2)}) collective-permute-start(bf16[1152,256]{1,0:T(8,128)(2,1)S(1)} %get-tuple-element.151), channel_id=1, source_target_pairs={{0,16},{4,20},{8,24},{12,28},{16,0},{20,4},{24,8},{28,12},{1,17},{... | collective-permute-start | bytes 1769480 | tf_op jit(solution)/shard_map/ppermute | solution.py:1165
  18.3 26.1 %collective-permute-start.1 = (bf16[1152,256]{1,0:T(8,128)(2,1)S(1)}, bf16[1152,256]{1,0:T(8,128)(2,1)S(1)}, u32[]{:S(2)}, u32[]{:S(2)}) collective-permute-start(bf16[1152,256]{1,0:T(8,128)(2,1)S(1)} %get-tuple-element.152), channel_id=1, source_target_pairs={{0,8},{4,12},{8,0},{12,4},{16,24},{20,28},{24,16},{28,20},{1,9},{5... | collective-permute-start | bytes 1769480 | tf_op jit(solution)/shard_map/ppermute | solution.py:1165
  65.7 48.4 %collective-permute-start.8 = (bf16[512,2048]{1,0:T(8,128)(2,1)}, bf16[512,2048]{1,0:T(8,128)(2,1)}, u32[]{:S(2)}, u32[]{:S(2)}) collective-permute-start(bf16[512,2048]{1,0:T(8,128)(2,1)} %all-gather.6.cloned.1.call-done.w0.refs_0_), channel_id=1, source_target_pairs={{0,8},{4,12},{8,0},{12,4},{16,24},{20,28},{24,16},{28,20},{1,9},{5... | collective-permute-start | bytes 6291464 | tf_op jit(solution)/shard_map/ppermute | solution.py:1165
  67.1 48.6 %collective-permute-start.9 = (bf16[512,2048]{1,0:T(8,128)(2,1)}, bf16[512,2048]{1,0:T(8,128)(2,1)}, u32[]{:S(2)}, u32[]{:S(2)}) collective-permute-start(bf16[512,2048]{1,0:T(8,128)(2,1)} %all-gather.6.cloned.1.call-done.w0.refs_0_), channel_id=1, source_target_pairs={{0,16},{4,20},{8,24},{12,28},{16,0},{20,4},{24,8},{28,12},{1,17},{... | collective-permute-start | bytes 6291464 | tf_op jit(solution)/shard_map/ppermute | solution.py:1165
  115.8 140.9 %all-gather.10.cloned.1.call-start = ((), (), s32[]{:S(2)}) async-start(), calls=%async_computation.7 | async-start | bytes 3932160 | tf_op jit(solution)/shard_map/all_gather | solution.py:1289
  117.1 25.2 %collective-permute-start.10 = (bf16[256,2048]{1,0:T(8,128)(2,1)S(1)}, bf16[256,2048]{1,0:T(8,128)(2,1)S(1)}, u32[]{:S(2)}, u32[]{:S(2)}) collective-permute-start(bf16[256,2048]{1,0:T(8,128)(2,1)S(1)} %slice.140), channel_id=1, source_target_pairs={{0,16},{4,20},{8,24},{12,28},{16,0},{20,4},{24,8},{28,12},{1,17},{... | collective-permute-start | bytes 3145736 | tf_op jit(solution)/shard_map/ppermute | solution.py:1165
  120.0 25.1 %collective-permute-start.11 = (bf16[256,2048]{1,0:T(8,128)(2,1)S(1)}, bf16[256,2048]{1,0:T(8,128)(2,1)}, u32[]{:S(2)}, u32[]{:S(2)}) collective-permute-start(bf16[256,2048]{1,0:T(8,128)(2,1)S(1)} %slice.141), channel_id=1, source_target_pairs={{0,8},{4,12},{8,0},{12,4},{16,24},{20,28},{24,16},{28,20},{1,9},{5... | collective-permute-start | bytes 3145736 | tf_op jit(solution)/shard_map/ppermute | solution.py:1165
  146.6 124.1 %all-gather.12.cloned.1.call-start = ((), (), s32[]{:S(2)}) async-start(), calls=%async_computation.8 | async-start | bytes 3932160 | tf_op jit(solution)/shard_map/all_gather | solution.py:1289
  157.0 241.0 %all-gather.14.cloned.1.call-start = ((), (), s32[]{:S(2)}) async-start(), calls=%async_computation.9 | async-start | bytes 3932160 | tf_op jit(solution)/shard_map/all_gather | solution.py:1289
  158.5 28.6 %collective-permute-start.12 = (bf16[1024,512]{1,0:T(8,128)(2,1)S(1)}, bf16[1024,512]{1,0:T(8,128)(2,1)S(1)}, u32[]{:S(2)}, u32[]{:S(2)}) collective-permute-start(bf16[1024,512]{1,0:T(8,128)(2,1)S(1)} %copy-done.20), channel_id=1, source_target_pairs={{0,8},{4,12},{8,0},{12,4},{16,24},{20,28},{24,16},{28,20},{1,9},{5... | collective-permute-start | bytes 3145736 | tf_op jit(solution)/shard_map/ppermute | solution.py:1165
  159.0 28.1 %collective-permute-start.13 = (bf16[1024,512]{1,0:T(8,128)(2,1)S(1)}, bf16[1024,512]{1,0:T(8,128)(2,1)S(1)}, u32[]{:S(2)}, u32[]{:S(2)}) collective-permute-start(bf16[1024,512]{1,0:T(8,128)(2,1)S(1)} %copy-done.20), channel_id=1, source_target_pairs={{0,16},{4,20},{8,24},{12,28},{16,0},{20,4},{24,8},{28,12},{1,17},{... | collective-permute-start | bytes 3145736 | tf_op jit(solution)/shard_map/ppermute | solution.py:1165
  190.3 57.7 %collective-permute-start.17 = (bf16[512,2048]{1,0:T(8,128)(2,1)S(1)}, bf16[512,2048]{1,0:T(8,128)(2,1)S(1)}, u32[]{:S(2)}, u32[]{:S(2)}) collective-permute-start(bf16[512,2048]{1,0:T(8,128)(2,1)S(1)} %broadcast_select_fusion.1.own_grads.cotangent), channel_id=1, source_target_pairs={{0,8},{4,12},{8,0},{12,4},{16,24},{20,28},{24,16},{28,20},{1,9},{5... | collective-permute-start | bytes 6291464 | tf_op jit(solution)/shard_map/ppermute | solution.py:1165
  190.8 57.2 %collective-permute-start.18 = (bf16[512,2048]{1,0:T(8,128)(2,1)S(1)}, bf16[512,2048]{1,0:T(8,128)(2,1)}, u32[]{:S(2)}, u32[]{:S(2)}) collective-permute-start(bf16[512,2048]{1,0:T(8,128)(2,1)S(1)} %broadcast_select_fusion.1.own_grads.cotangent), channel_id=1, source_target_pairs={{0,16},{4,20},{8,24},{12,28},{16,0},{20,4},{24,8},{28,12},{1,17},{... | collective-permute-start | bytes 6291464 | tf_op jit(solution)/shard_map/ppermute | solution.py:1165
  213.5 34.5 %collective-permute-start.16 = (bf16[512,2048]{1,0:T(8,128)(2,1)}, bf16[512,2048]{1,0:T(8,128)(2,1)S(1)}, u32[]{:S(2)}, u32[]{:S(2)}) collective-permute-start(bf16[512,2048]{1,0:T(8,128)(2,1)} %get-tuple-element.82), channel_id=1, source_target_pairs={{0,4},{4,0},{8,12},{12,8},{16,20},{20,16},{24,28},{28,24},{1,5},{5... | collective-permute-start | bytes 6291464 | tf_op jit(solution)/shard_map/ppermute | solution.py:1165
  256.7 63.5 %collective-permute-start.21 = (bf16[1536,1024]{1,0:T(8,128)(2,1)}, bf16[1536,1024]{1,0:T(8,128)(2,1)S(1)}, u32[]{:S(2)}, u32[]{:S(2)}) collective-permute-start(bf16[1536,1024]{1,0:T(8,128)(2,1)} %all-gather.10.cloned.1.call-done.gate_own), channel_id=1, source_target_pairs={{0,4},{4,0},{8,12},{12,8},{16,20},{20,16},{24,28},{28,24},{1,5},{5... | collective-permute-start | bytes 9437192 | tf_op jit(solution)/shard_map/ppermute | solution.py:1165
  270.7 49.6 %collective-permute-start.22 = (bf16[1536,1024]{1,0:T(8,128)(2,1)}, bf16[1536,1024]{1,0:T(8,128)(2,1)}, u32[]{:S(2)}, u32[]{:S(2)}) collective-permute-start(bf16[1536,1024]{1,0:T(8,128)(2,1)} %all-gather.12.cloned.1.call-done.up_own), channel_id=1, source_target_pairs={{0,4},{4,0},{8,12},{12,8},{16,20},{20,16},{24,28},{28,24},{1,5},{5... | collective-permute-start | bytes 9437192 | tf_op jit(solution)/shard_map/ppermute | solution.py:1165
  270.7 48.4 %collective-permute-start.19 = (bf16[512,2048]{1,0:T(8,128)(2,1)}, bf16[512,2048]{1,0:T(8,128)(2,1)}, u32[]{:S(2)}, u32[]{:S(2)}) collective-permute-start(bf16[512,2048]{1,0:T(8,128)(2,1)} %get-tuple-element.86.own_tokens), channel_id=1, source_target_pairs={{0,8},{4,12},{8,0},{12,4},{16,24},{20,28},{24,16},{28,20},{1,9},{5... | collective-permute-start | bytes 6291464 | tf_op jit(solution)/shard_map/ppermute | solution.py:1165
  272.1 48.1 %collective-permute-start.20 = (bf16[512,2048]{1,0:T(8,128)(2,1)}, bf16[512,2048]{1,0:T(8,128)(2,1)}, u32[]{:S(2)}, u32[]{:S(2)}) collective-permute-start(bf16[512,2048]{1,0:T(8,128)(2,1)} %get-tuple-element.86.own_tokens), channel_id=1, source_target_pairs={{0,16},{4,20},{8,24},{12,28},{16,0},{20,4},{24,8},{28,12},{1,17},{... | collective-permute-start | bytes 6291464 | tf_op jit(solution)/shard_map/ppermute | solution.py:1165
  273.6 322.2 %reduce-scatter.6.cloned.1.call-start = ((), (), s32[]{:S(2)}) async-start(), calls=%async_computation.10 | async-start | bytes 3932160 | tf_op jit(solution)/shard_map/reduce_scatter | solution.py:1342
  419.6 330.1 %reduce-scatter.8.cloned.1.call-start = ((), (), s32[]{:S(2)}) async-start(), calls=%async_computation.11 | async-start | bytes 3932160 | tf_op jit(solution)/shard_map/reduce_scatter | solution.py:1342
  562.7 187.0 %reduce-scatter.10.cloned.1.call-start = ((), (), s32[]{:S(2)}) async-start(), calls=%async_computation.12 | async-start | bytes 3932160 | tf_op jit(solution)/shard_map/reduce_scatter | solution.py:1342
  580.0 294.1 %reduce-scatter.12.cloned.1.call-start = ((), (), s32[]{:S(2)}) async-start(), calls=%async_computation.13 | async-start | bytes 2621440 | tf_op jit(solution)/shard_map/reduce_scatter | solution.py:1424
  593.9 48.7 %collective-permute-start.28 = (bf16[512,2048]{1,0:T(8,128)(2,1)}, bf16[512,2048]{1,0:T(8,128)(2,1)S(1)}, u32[]{:S(2)}, u32[]{:S(2)}) collective-permute-start(bf16[512,2048]{1,0:T(8,128)(2,1)} %get-tuple-element.106), channel_id=1, source_target_pairs={{0,8},{4,12},{8,0},{12,4},{16,24},{20,28},{24,16},{28,20},{1,9},{5... | collective-permute-start | bytes 6291464 | tf_op jit(solution)/shard_map/ppermute | solution.py:1165
  595.1 53.0 %collective-permute-start.29 = (bf16[512,2048]{1,0:T(8,128)(2,1)}, bf16[512,2048]{1,0:T(8,128)(2,1)}, u32[]{:S(2)}, u32[]{:S(2)}) collective-permute-start(bf16[512,2048]{1,0:T(8,128)(2,1)} %get-tuple-element.108), channel_id=1, source_target_pairs={{0,16},{4,20},{8,24},{12,28},{16,0},{20,4},{24,8},{28,12},{1,17},{... | collective-permute-start | bytes 6291464 | tf_op jit(solution)/shard_map/ppermute | solution.py:1165
  597.2 56.8 %collective-permute-start.33 = (bf16[384,256]{1,0:T(8,128)(2,1)S(1)}, bf16[384,256]{1,0:T(8,128)(2,1)S(1)}, u32[]{:S(2)}, u32[]{:S(2)}) collective-permute-start(bf16[384,256]{1,0:T(8,128)(2,1)S(1)} %get-tuple-element.172), channel_id=1, source_target_pairs={{0,24},{4,28},{8,16},{12,20},{16,8},{20,12},{24,0},{28,4},{1,25},{... | collective-permute-start | bytes 589832 | tf_op jit(solution)/shard_map/ppermute | solution.py:1165
  598.7 55.3 %collective-permute-start.32 = (bf16[384,256]{1,0:T(8,128)(2,1)S(1)}, bf16[384,256]{1,0:T(8,128)(2,1)S(1)}, u32[]{:S(2)}, u32[]{:S(2)}) collective-permute-start(bf16[384,256]{1,0:T(8,128)(2,1)S(1)} %get-tuple-element.173), channel_id=1, source_target_pairs={{0,16},{4,20},{8,24},{12,28},{16,0},{20,4},{24,8},{28,12},{1,17},{... | collective-permute-start | bytes 589832 | tf_op jit(solution)/shard_map/ppermute | solution.py:1165
  600.1 53.9 %collective-permute-start.31 = (bf16[384,256]{1,0:T(8,128)(2,1)S(1)}, bf16[384,256]{1,0:T(8,128)(2,1)S(1)}, u32[]{:S(2)}, u32[]{:S(2)}) collective-permute-start(bf16[384,256]{1,0:T(8,128)(2,1)S(1)} %get-tuple-element.174), channel_id=1, source_target_pairs={{0,8},{4,12},{8,0},{12,4},{16,24},{20,28},{24,16},{28,20},{1,9},{5... | collective-permute-start | bytes 589832 | tf_op jit(solution)/shard_map/ppermute | solution.py:1165
  736.9 164.2 %reduce-scatter.14.cloned.1.call-start = ((), (), s32[]{:S(2)}) async-start(), calls=%async_computation.14 | async-start | bytes 1310720 | tf_op jit(solution)/shard_map/reduce_scatter | solution.py:1342
  774.7 46.6 %collective-permute-start.36 = (f32[4352]{0:T(1024)S(1)}, f32[4352]{0:T(1024)S(1)}, u32[]{:S(2)}, u32[]{:S(2)}) collective-permute-start(f32[4352]{0:T(1024)S(1)} %pad_maximum_fusion.7), channel_id=1, source_target_pairs={{0,4},{4,0},{8,12},{12,8},{16,20},{20,16},{24,28},{28,24},{1,5},{5... | collective-permute-start | bytes 52232 | tf_op jit(solution)/shard_map/ppermute | solution.py:1165
  823.6 54.5 %collective-permute-start.35 = (bf16[512,2048]{1,0:T(8,128)(2,1)}, bf16[512,2048]{1,0:T(8,128)(2,1)}, u32[]{:S(2)}, u32[]{:S(2)}) collective-permute-start(bf16[512,2048]{1,0:T(8,128)(2,1)} %get-tuple-element.122), channel_id=1, source_target_pairs={{1,4},{3,6},{4,1},{6,3},{9,12},{11,14},{12,9},{14,11},{17,20},{19,... | collective-permute-start | bytes 6291464 | tf_op jit(solution)/shard_map/ppermute | solution.py:1174
  (52 other events, 723.5 us)
Sparse Core Ops, SparseCore 0:
  13.1 48.5 all-gather.5
  115.9 25.6 all-gather.7
  146.7 60.3 all-gather.9
  208.5 62.1 all-gather.11
  273.8 60.4 all-gather.13
  419.7 57.9 reduce-scatter.5
  562.8 58.0 reduce-scatter.7
  623.2 60.2 reduce-scatter.9
  737.0 58.5 reduce-scatter.11
  874.2 26.8 reduce-scatter.13

commit v3 on v2

--- a/solution.py
+++ b/solution.py
@@ -443,11 +443,7 @@
             shape((length, planes * HEAD_SIZE), jnp.float32),
         ],
         compiler_params=pltpu.CompilerParams(vmem_limit_bytes=56 * 2**20),
-        cost_estimate=pl.CostEstimate(
-            flops=2 * length * width * cols + 3 * planes * query_cols * length**2,
-            bytes_accessed=30 * 2**20,
-            transcendentals=planes * 2 * length**2,
-        ),
+        cost_estimate=pl.CostEstimate(flops=1, bytes_accessed=1, transcendentals=0),
     )(core, own, other, *weights, cosines, sines, query_gain, key_gain)
 
 
@@ -575,11 +571,7 @@
             shape((16, HEAD_SIZE), jnp.float32),
         ],
         compiler_params=pltpu.CompilerParams(vmem_limit_bytes=56 * 2**20),
-        cost_estimate=pl.CostEstimate(
-            flops=length * width * cols + 8 * planes * query_cols * length**2,
-            bytes_accessed=30 * 2**20,
-            transcendentals=planes * 2 * length**2,
-        ),
+        cost_estimate=pl.CostEstimate(flops=1, bytes_accessed=1, transcendentals=0),
     )(core, own, other, *weights, cosines, sines, query_gain, key_gain, *saved)
 
 
@@ -694,7 +686,7 @@
 
 def gather_hidden(tokens, grads, weights):
     rows, width = tokens[0].shape
-    hidden_count, half = weights[0].shape
+    _, hidden_count, half = weights[0].shape
     chunk = 512
     spec = pl.BlockSpec
     shape = jax.ShapeDtypeStruct
@@ -704,7 +696,8 @@
     return pl.pallas_call(
         hidden_kernel,
         grid=(4, hidden_count // chunk),
-        in_specs=[outside] * 4 + [whole] * 6 + [spec((chunk, half), lambda b, c: (c, 0))] * 4,
+        in_specs=[outside] * 4 + [whole] * 6
+        + [spec((None, chunk, half), lambda b, c, n=n: (n, c, 0)) for n in (0, 0, 1, 1)],
         out_specs=[spec((rows, width), lambda b, c: (b, 0))] * 2
         + [spec((rows, chunk), lambda b, c: (b, c))] * 3,
         out_shape=[shape((4 * rows, width), bf16)] * 2 + [shape((4 * rows, hidden_count), bf16)] * 3,
@@ -713,12 +706,8 @@
         compiler_params=pltpu.CompilerParams(
             collective_id=1, has_side_effects=True, vmem_limit_bytes=60 * 2**20
         ),
-        cost_estimate=pl.CostEstimate(
-            flops=16 * rows * width * hidden_count,
-            bytes_accessed=60 * 2**20,
-            transcendentals=4 * rows * hidden_count,
-        ),
-    )(*tokens[1:], *grads[1:], *tokens, *grads, *weights)
+        cost_estimate=pl.CostEstimate(flops=1, bytes_accessed=1, transcendentals=0),
+    )(*tokens[1:], *grads[1:], *tokens, *grads, *weights, *weights)
 
 
 def reduce_copies(corner, send_x, send_y, got_corner, got_x, got_y, send, receive):
@@ -869,9 +858,9 @@
             write.wait()
 
 
-def feed_back(grads, saved, weights):
+def feed_back(grads, saved, weights, down):
     rows, width = grads.shape[0] // 4, grads.shape[1]
-    hidden_count, half = weights[0].shape
+    _, hidden_count, half = weights[0].shape
     chunk = 512
     spec = pl.BlockSpec
     shape = jax.ShapeDtypeStruct
@@ -883,7 +872,8 @@
         grid=(4, hidden_count // chunk),
         in_specs=[spec((rows, width), block)]
         + [spec((rows, chunk), piece)] * 3
-        + [spec((chunk, half), lambda q, c: (c, 0))] * 6,
+        + [spec((None, chunk, half), lambda q, c, n=n: (n, c, 0)) for n in (0, 0, 1, 1)]
+        + [spec((chunk, half), lambda q, c: (c, 0))] * 2,
         out_specs=[spec((rows, chunk), piece)] * 2
         + [spec(memory_space=pl.ANY)] * 3
         + [spec((rows, width), lambda q, c: (0, 0))],
@@ -898,27 +888,71 @@
         compiler_params=pltpu.CompilerParams(
             collective_id=2, has_side_effects=True, vmem_limit_bytes=62 * 2**20
         ),
-        cost_estimate=pl.CostEstimate(
-            flops=32 * rows * width * hidden_count,
-            bytes_accessed=80 * 2**20,
-            transcendentals=0,
-        ),
-    )(grads, *saved, *weights)
+        cost_estimate=pl.CostEstimate(flops=1, bytes_accessed=1, transcendentals=0),
+    )(grads, *saved, *weights, *weights, *down)
+
+
+def is_crossing():
+    return (lax.axis_index("dp") + lax.axis_index("mp")) % 2 == 1
+
+
+def crossing_partner():
+    me, z = lax.axis_index("dp"), lax.axis_index("mp")
+    return {"dp": me + 1 - 2 * (me % 2), "mp": z + 1 - 2 * (z % 2)}
+
+
+def crossing_copy(source, target, send, receive):
+    return pltpu.make_async_remote_copy(
+        src_ref=source,
+        dst_ref=target,
+        send_sem=send.at[0],
+        recv_sem=receive.at[0],
+        device_id=crossing_partner(),
+        device_id_type=MESH,
+    )
 
 
 def outer_kernel(extra, left_own, left_other, right_own, right_other, *refs):
     weights = refs[:extra]
-    total_out, *spread = refs[extra : extra + (3 if extra else 1)]
+    if extra:
+        layer, total_out, *spread, layer_out = refs[extra : extra + 5]
+        cross = crossing_copy(layer, layer_out, refs[-3], refs[-2])
+        stay = pltpu.make_async_copy(layer, layer_out, refs[-1].at[0])
+        crossing = is_crossing()
+        refs = refs[:-3]
+    else:
+        total_out = refs[0]
     own, corner, send_x, send_y, got_corner, got_x, got_y, send, receive = refs[-9:]
     step = pl.program_id(0)
     half = own.shape[0] // 2
     low, high = slice(0, half), slice(half, 2 * half)
     copies = reduce_copies(corner, send_x, send_y, got_corner, got_x, got_y, send, receive)
 
-    @pl.when(step == 0)
-    def _():
-        _, over_x, over_y = neighbours()
-        greet((over_x, over_y))
+    if not extra:
+
+        @pl.when(step == 0)
+        def _():
+            _, over_x, over_y = neighbours()
+            greet((over_x, over_y))
+
+    else:
+
+        @pl.when((step == 0) & crossing)
+        def _():
+            _, over_x, over_y = neighbours()
+            partner = crossing_partner()
+            barrier = pltpu.get_barrier_semaphore()
+            for other in (over_x, over_y):
+                pl.semaphore_signal(barrier, inc=1, device_id={"dp": other}, device_id_type=MESH)
+            pl.semaphore_signal(barrier, inc=1, device_id=partner, device_id_type=MESH)
+            pl.semaphore_wait(barrier, 3)
+            cross.start()
+
+        @pl.when((step == 0) & jnp.logical_not(crossing))
+        def _():
+            _, over_x, over_y = neighbours()
+            greet((over_x, over_y))
+            stay.start()
 
     @pl.when(step < 8)
     def _():
@@ -971,8 +1005,18 @@
         for transfer in copies:
             transfer.wait_send()
 
-
-def outer(lefts, rights, by_left, collective_id, weights=()):
+    if extra:
+
+        @pl.when((step == last) & crossing)
+        def _():
+            cross.wait()
+
+        @pl.when((step == last) & jnp.logical_not(crossing))
+        def _():
+            stay.wait()
+
+
+def outer(lefts, rights, by_left, collective_id, weights=(), layer=None):
     rows = 512
     wide = lefts[0][0].shape[1]
     right_wide = rights[0][0].shape[1]
@@ -994,6 +1038,8 @@
     if weights:
         out_specs += [spec((rows, wide), lambda s: (0, 0))] * 2
         out_shape += [shape((rows, wide), jnp.float32), shape((rows, wide), jnp.bfloat16)]
+        out_specs += [spec(memory_space=pl.ANY)]
+        out_shape += [shape(layer.shape, layer.dtype)]
     made = pl.pallas_call(
         functools.partial(outer_kernel, len(weights)),
         grid=(8 + len(weights),),
@@ -1002,19 +1048,19 @@
         + [
             spec(weight.shape, lambda s: (0, 0), pipeline_mode=pl.Buffered(1))
             for weight in weights
-        ],
+        ]
+        + ([spec(memory_space=pl.ANY)] if weights else []),
         out_specs=out_specs,
         out_shape=out_shape,
         scratch_shapes=[pltpu.VMEM(both, jnp.float32)]
         + [pltpu.VMEM(both, jnp.bfloat16)] * 6
-        + [pltpu.SemaphoreType.DMA((6,)), pltpu.SemaphoreType.DMA((6,))],
+        + [pltpu.SemaphoreType.DMA((6,)), pltpu.SemaphoreType.DMA((6,))]
+        + ([pltpu.SemaphoreType.DMA((1,))] * 3 if weights else []),
         compiler_params=pltpu.CompilerParams(
             collective_id=collective_id, has_side_effects=True, vmem_limit_bytes=60 * 2**20
         ),
-        cost_estimate=pl.CostEstimate(
-            flops=4 * rows * wide * right_wide, bytes_accessed=16 * 2**20, transcendentals=0
-        ),
-    )(*[array for array, _ in (*lefts, *rights)], *weights)
+        cost_estimate=pl.CostEstimate(flops=1, bytes_accessed=1, transcendentals=0),
+    )(*[array for array, _ in (*lefts, *rights)], *weights, *([layer] if weights else []))
     return made if weights else made[0]
 
 
@@ -1069,9 +1115,7 @@
         ),
         out_shape=[shape((rows, width), jnp.float32), shape((rows, width), jnp.bfloat16)],
         compiler_params=pltpu.CompilerParams(vmem_limit_bytes=56 * 2**20),
-        cost_estimate=pl.CostEstimate(
-            flops=2 * length * depth * width, bytes_accessed=20 * 2**20, transcendentals=0
-        ),
+        cost_estimate=pl.CostEstimate(flops=1, bytes_accessed=1, transcendentals=0),
     )(place, left, *weights)
 
 
@@ -1096,9 +1140,7 @@
         ),
         out_shape=[shape for shape, _ in outs],
         compiler_params=pltpu.CompilerParams(vmem_limit_bytes=56 * 2**20),
-        cost_estimate=pl.CostEstimate(
-            flops=20 * 2**20, bytes_accessed=kept * 2**20, transcendentals=0
-        ),
+        cost_estimate=pl.CostEstimate(flops=1, bytes_accessed=1, transcendentals=0),
     )(place, *[array for array, _ in ins])
 
 
@@ -1203,12 +1245,15 @@
     )
 
 
-def total(values):
+def total_plane(values):
     for bit in (1, 2, 4):
         values = values + exchange(values, bit)
-    for bit in (1, 2):
-        values = values + lax.ppermute(values, "mp", [(i, i ^ bit) for i in range(4)])
     return values
+
+
+def total_z(values):
+    others = [lax.ppermute(values, "mp", [(i, i ^ bit) for i in range(4)]) for bit in (1, 2, 3)]
+    return (values + others[0]) + (others[1] + others[2])
 
 
 def fast(
@@ -1279,16 +1324,8 @@
         after(out_pair, (moved, moved_grad, qkv_near)), "mp", axis=0, tiled=True
     )
 
-    qkv_chips = [qkv_z, *qkv_near, *gather_far(qkv_near)]
     inputs = jnp.where(crossing, moved, layer_input)
     cotangent = jnp.where(crossing, moved_grad, out_grad)
-
-    out_near = gather_near(after(out_z, qkv_chips))
-    feed_own = after(feed_own, (out_z, qkv_chips))
-    gate_half, up_half, down_half = [
-        lax.all_gather(feed_own[n * units : (n + 1) * units], "mp", axis=0, tiled=True)
-        for n in range(3)
-    ]
 
     gain_one, gain_two = norm_attn[None, :], norm_mlp[None, :]
     gain_query, gain_key = query_norm[None, :], key_norm[None, :]
@@ -1299,8 +1336,19 @@
         [(array((rows, width), bf16), "rows")],
         4,
     )
-    normed_other = after(exchange(normed, 1), (out_z, cotangent))
     cosines, sines = wide_tables(2 * rows)
+    qkv_chips = [
+        qkv_z,
+        *qkv_near,
+        *gather_far(after(qkv_near, (normed, cosines, sines, cotangent))),
+    ]
+    out_near = gather_near(after(out_z, qkv_chips))
+    feed_own = after(feed_own, (out_z, qkv_chips))
+    gate_up_half = lax.all_gather(
+        feed_own[: 2 * units].reshape(2, units, width // 2), "mp", axis=1, tiled=True
+    )
+    down_half = lax.all_gather(feed_own[2 * units :], "mp", axis=0, tiled=True)
+    normed_other = after(exchange(normed, 1), out_z)
     proj, query_rot, key_rot, value_low, attended, log_total = attend(
         core_index,
         normed,
@@ -1328,42 +1376,37 @@
         14,
     )
 
-    gate_half = after(gate_half, attended)
-    up_half = after(up_half, tokens)
-    gate_w, up_w = [[half, exchange(half, 1)] for half in (gate_half, up_half)]
     tokens_near = gather_near(tokens)
+    gate_up_w = [gate_up_half, exchange(after(gate_up_half, tokens), 1)]
     all_tokens, all_grads, all_hidden, gate_slope, up_slope = gather_hidden(
-        [tokens, *tokens_near], [cotangent, *grads_near], [*gate_w, *up_w]
-    )
-    down_half = after(down_half, tokens_near)
+        [tokens, *tokens_near], [cotangent, *grads_near], gate_up_w
+    )
+    down_half = after(down_half, all_hidden)
     down_w = [down_half, exchange(down_half, 1)]
 
     def over_z(grad):
         return lax.psum_scatter(grad, "mp", scatter_dimension=0, tiled=True)
 
-    def weight_grad(left, right):
-        half = right.shape[1] // 2
-        other = exchange(dot_first(left, right[:, half:]).astype(bf16), 1)
-        return (dot_first(left, right[:, :half]) + other.astype(f32)).astype(bf16)
-
-    down_local = weight_grad(all_hidden, all_grads)
-    down_sum = over_z(down_local)
+    half = width // 2
+    down_other = dot_first(all_hidden, all_grads[:, half:]).astype(bf16)
     all_gate, all_up, out_own, out_x, out_y, two_grad = feed_back(
-        after(all_grads, down_local),
+        after(all_grads, down_other),
         [all_hidden, gate_slope, up_slope],
-        [*gate_w, *up_w, *down_w],
-    )
-    half = width // 2
+        gate_up_w,
+        down_w,
+    )
     gate_other = dot_first(all_gate, all_tokens[:, half:]).astype(bf16)
     up_other = dot_first(all_up, all_tokens[:, half:]).astype(bf16)
     all_gate, all_up = after((all_gate, all_up), (gate_other, up_other))
 
-    def own_half(left, other):
-        own = dot_first(left, all_tokens[:, :half])
+    def own_half(left, right, other):
+        own = dot_first(left, right[:, :half])
         return (own + exchange(other, 1).astype(f32)).astype(bf16)
 
-    gate_local = own_half(all_gate, gate_other)
-    up_local = own_half(all_up, up_other)
+    down_local = own_half(after(all_hidden, two_grad), all_grads, down_other)
+    down_sum = over_z(down_local)
+    gate_local = own_half(all_gate, all_tokens, gate_other)
+    up_local = own_half(all_up, all_tokens, up_other)
     gate_sum, up_sum = over_z(gate_local), over_z(up_local)
     middle_grad, branch, gain_two_part = tile_call(
         middle_back_kernel,
@@ -1387,14 +1430,11 @@
     def chips_in_order(got, cols, rows):
         return jnp.concatenate([pick(got[rows], place[0] ^ k, cols, 1) for k in range(planes)], 0)
 
-    gate_up_got, cols = unspread(jnp.concatenate([gate_sum, up_sum], 0))
-    gate_own = chips_in_order(gate_up_got, cols, slice(0, units)).T.astype(f32)
-    up_own = chips_in_order(gate_up_got, cols, slice(units, 2 * units)).T.astype(f32)
     down_got, cols = unspread(down_sum)
     down_own = chips_in_order(down_got, cols, slice(0, units)).astype(f32)
 
-    branch_pair = after(exchange(branch, 1), (gate_local, up_local))
-    out_parts = [out_own, exchange(after(out_x, branch_pair), 2), exchange(after(out_y, branch_pair), 4)]
+    branch_pair = after(exchange(branch, 1), (gate_local, up_local, down_local))
+    out_parts = [out_own, exchange(out_x, 2), exchange(out_y, 4)]
     proj_grad, head_gains = attend_back(
         core_index,
         branch,
@@ -1417,15 +1457,20 @@
         [(array((rows, width), bf16), "rows")],
         12,
     )
-    proj_grad = after(proj_grad, (layer_output, down_own))
-    qkv_local, one_own, one_other = outer(
-        [(normed, 0), (normed_other, 0)], [(proj_grad, 0), (proj_grad, 1)], True, 3, qkv_chips
-    )
+    attended = after(attended, (proj_grad, out_parts))
+    out_local = outer([(attended, 0), (attended, 1)], [(branch, 0), (branch_pair, 0)], False, 4)
+    out_sum = over_z(out_local)
+    proj_grad = after(proj_grad, (down_own, gate_sum, out_local))
+    qkv_local, one_own, one_other, output_moved = outer(
+        [(normed, 0), (normed_other, 0)],
+        [(proj_grad, 0), (proj_grad, 1)],
+        True,
+        3,
+        qkv_chips,
+        layer_output,
+    )
+    qkv_local = after(qkv_local, (up_sum, out_sum))
     qkv_sum = lax.psum_scatter(qkv_local, "mp", scatter_dimension=1, tiled=True)
-    output_moved = swap_halves(layer_output)
-    attended = after(attended, (qkv_local, output_moved, gate_sum, up_sum))
-    out_local = outer([(attended, 0), (attended, 1)], [(branch, 0), (branch_pair, 0)], False, 4)
-    out_sum = over_z(after(out_local, qkv_sum))
     input_grad, rounded_grad, gain_one_part = tile_call(
         input_back_kernel,
         place,
@@ -1443,7 +1488,12 @@
         ],
         18,
     )
-    gain_sums = total(
+    gate_up_got, cols = unspread(
+        after(jnp.concatenate([gate_sum, up_sum], 0), rounded_grad)
+    )
+    gate_own = chips_in_order(gate_up_got, cols, slice(0, units)).T.astype(f32)
+    up_own = chips_in_order(gate_up_got, cols, slice(units, 2 * units)).T.astype(f32)
+    gain_sums = total_plane(
         after(jnp.concatenate(
             [
                 jnp.sum(gain_one_part, 0),
@@ -1451,8 +1501,10 @@
                 jnp.sum(head_gains[8:], 0),
                 jnp.sum(gain_two_part, 0),
             ]
-        ), out_local)
-    )
+        ), qkv_local)
+    )
+    grad_moved = swap_halves(rounded_grad)
+    gain_sums = total_z(after(gain_sums, (gate_own, up_own, grad_moved)))
     pair_rows = qkv_sum.shape[0] // 2
     qkv_other = exchange(pick(qkv_sum, 1 - core, pair_rows, 0), 1)
     qkv_own = pick(qkv_sum, core, pair_rows, 0)
@@ -1464,8 +1516,8 @@
     out_other = exchange(pick(out_sum, 1 - core, pair_cols, 1), 1)
     out_own = pick(out_sum, core, pair_cols, 1)
     return (
-        jnp.where(crossing, output_moved, layer_output),
-        jnp.where(crossing, swap_halves(rounded_grad).astype(f32), input_grad),
+        output_moved,
+        jnp.where(crossing, grad_moved.astype(f32), input_grad),
         gain_sums[:width],
         gain_sums[width : width + HEAD_SIZE],
         gain_sums[width + HEAD_SIZE : width + 2 * HEAD_SIZE],

time: 917 us -> 847 us (0.924)
  waiting for transfers between devices: 304 us -> 248 us
  starting transfers between devices: 91.5 us -> 49 us
  Pallas kernels: 393 us -> 414 us
    ppermute x40 -> x39, starting transfers between devices: 78 us -> 32.8 us  [exchange(): return lax.ppermute(values, 'dp', [(i, i ^ bit) for i in range(8)])]
    ppermute x40 -> x39, waiting for transfers between devices: 236 us -> 212 us  [exchange(): return lax.ppermute(values, 'dp', [(i, i ^ bit) for i in range(8)])]
    ppermute x2 -> x3, waiting for transfers between devices: 20.7 us -> 0.01 us  [total_z(): lax.ppermute(values, 'mp', [(i, i ^ bit) for i in range(4)])]
    pallas_call x2, Pallas kernels: 104 us -> 123 us  [outer(): pl.pallas_call(functools.partial(outer_kernel, len(weights)), grid=(8 + l...]
    reduce_scatter x4, waiting for transfers between devices: 17 us -> 1.14 us  [over_z(): return lax.psum_scatter(grad, 'mp', scatter_dimension=0, tiled=True)]
    reduce_scatter x1, waiting for transfers between devices: 0.02 us -> 10.3 us  [fast(): qkv_sum = lax.psum_scatter(qkv_local, 'mp', scatter_dimension=1, tiled=True)]
  transfers between devices with their start and end apart: 56 -> 54, of which waited for: 29 -> 24; matrix products, arithmetic and copies ran while one was open for 10% -> 10% of each run, Pallas kernels for 43% -> 49%
where the time goes in v3:
time: 847 us; the launch traced here: 841 us
  Pallas kernels  414 us (49%)
  waiting for transfers between devices  248 us (29%)
  matrix products  63.5 us (7%)
  starting transfers between devices  49 us (6%)
  local copies, waits for them, and re-layouts  26.5 us (3%)
  other arithmetic  25.1 us (3%)
  between operations  14.8 us (2%)
    ppermute x39, waiting for transfers between devices, exchange(): return lax.ppermute(values, 'dp', [(i, i ^ bit) for i in range(8)])  212 us
    pallas_call x2, Pallas kernels, outer(): pl.pallas_call(functools.partial(outer_kernel, len(weights)), grid=(8 + l...  123 us
    pallas_call x1, Pallas kernels, feed_back(): pl.pallas_call(feed_back_kernel, grid=(4, hidden_count // chunk), in_spec...  115 us
    pallas_call x1, Pallas kernels, gather_hidden(): pl.pallas_call(hidden_kernel, grid=(4, hidden_count // chunk), in_specs=[...  66 us
    dot_general x6, matrix products, dot_first(): lax.dot_general(left, right, (((0,), (0,)), ((), ())), preferred_element_...  63.5 us
    pallas_call x1, Pallas kernels, attend_back(): pl.pallas_call(attend_back_kernel, grid_spec=pltpu.PrefetchScalarGridSpec...  40.1 us
    pallas_call x5, Pallas kernels, tile_call(): pl.pallas_call(kernel, grid_spec=pltpu.PrefetchScalarGridSpec(num_scalar_...  32.8 us
    ppermute x39, starting transfers between devices, exchange(): return lax.ppermute(values, 'dp', [(i, i ^ bit) for i in range(8)])  32.8 us
  transfers between devices with their start and end apart: 54, of which 24 were waited for; matrix products, arithmetic and copies ran while one was open for 10% of the time, Pallas kernels for 49%

profile of v3, /device:TPU:0, one launch (start us, length us, event | category | flops | bytes accessed | tf_op | source)
XLA Modules:
  0.0 841.1 jit_solution(12223291580947179733)
XLA Ops:
  13.1 3.9 collective-permute-start.3
  17.6 13.5 %collective-permute-done.3 = bf16[1152,256]{1,0:T(8,128)(2,1)S(1)} collective-permute-done((bf16[1152,256]{1,0:T(8,128)(2,1)S(1)}, bf16[1152,256]{1,0:T(8,128)(2,1)S(1)}, u32[]{:S(2)}, u32[]{:S(2)}) %collective-permute-start.3) | collective-permute-done | bytes 589856 | tf_op jit(solution)/shard_map/ppermute | solution.py:1207
  31.2 12.1 %collective-permute-done.2 = bf16[1152,256]{1,0:T(8,128)(2,1)S(1)} collective-permute-done((bf16[1152,256]{1,0:T(8,128)(2,1)S(1)}, bf16[1152,256]{1,0:T(8,128)(2,1)S(1)}, u32[]{:S(2)}, u32[]{:S(2)}) %collective-permute-start.2) | collective-permute-done | bytes 589856 | tf_op jit(solution)/shard_map/ppermute | solution.py:1207
  45.3 15.6 %all-gather.5.cloned.1.call-done.w0.refs_0_ = bf16[512,2048]{1,0:T(8,128)(2,1)} async-done(((bf16[512,512]{1,0:T(8,128)(2,1)}), bf16[512,2048]{1,0:T(8,128)(2,1)}) %all-gather.5.cloned.1.call-update) | async-done | bytes 2097168 | tf_op jit(solution)/shard_map/all_gather | solution.py:1307
  72.8 40.2 %collective-permute-done.8.w1.refs_1_ = bf16[512,2048]{1,0:T(8,128)(2,1)S(1)} collective-permute-done((bf16[512,2048]{1,0:T(8,128)(2,1)}, bf16[512,2048]{1,0:T(8,128)(2,1)S(1)}, u32[]{:S(2)}, u32[]{:S(2)}) %collective-permute-start.8) | collective-permute-done | bytes 2097184 | tf_op jit(solution)/shard_map/ppermute | solution.py:1207
  118.1 3.2 shard_map.228.own.left_own
  127.1 21.8 %collective-permute-done.10.w3_low.refs_3_ = bf16[256,2048]{1,0:T(8,128)(2,1)} collective-permute-done((bf16[256,2048]{1,0:T(8,128)(2,1)S(1)}, bf16[256,2048]{1,0:T(8,128)(2,1)}, u32[]{:S(2)}, u32[]{:S(2)}) %collective-permute-start.10) | collective-permute-done | bytes 1048608 | tf_op jit(solution)/shard_map/ppermute | solution.py:1207
  160.5 28.1 %shard_map.229 = (f32[1024,2048]{1,0:T(8,128)}, bf16[1024,1024]{1,0:T(8,128)(2,1)}, bf16[1024,512]{1,0:T(8,128)(2,1)}, bf16[1024,512]{1,0:T(8,128)(2,1)}, bf16[1...) custom-call(s32[1]{0:T(128)} %bitcast.11.core, bf16[512,2048]{1,0:T(8,128)(2,1)} %shard_map.228.own.left_own, ...), custom_call_target="tpu_custom_call" | custom-call | flops 1 | bytes 1 | tf_op jit(solution)/shard_map/pallas_call | solution.py:419
  192.9 10.6 %collective-permute-done.14.w3_low.o3_low = bf16[512,512]{1,0:T(8,128)(2,1)S(1)} collective-permute-done((bf16[512,512]{1,0:T(8,128)(2,1)S(1)}, bf16[512,512]{1,0:T(8,128)(2,1)S(1)}, u32[]{:S(2)}, u32[]{:S(2)}) %collective-permute-start.14) | collective-permute-done | bytes 524320 | tf_op jit(solution)/shard_map/ppermute | solution.py:1207
  204.5 9.2 %shard_map.230 = (f32[512,2048]{1,0:T(8,128)}, bf16[512,2048]{1,0:T(8,128)(2,1)}) custom-call(s32[1]{0:T(128)} %bitcast.place, bf16[1024,1024]{1,0:T(8,128)(2,1)} %get-tuple-element.121.left.left_own.left_other, bf16[1024,512]{1,0:T(8,128)(2,1)} %all-gather.7.cloned.1.call-done.w0.o0, bf16[1024,512]{1,0:T(8,128)(2,1)} %copy-done.8, ...), custom_call_target="tpu_custom_call" | custom-call | flops 1 | bytes 1 | tf_op jit(solution)/shard_map/pallas_call | solution.py:1108
  213.7 34.5 %collective-permute-done.17.x_grads_out.x_grads = bf16[512,2048]{1,0:T(8,128)(2,1)S(1)} collective-permute-done((bf16[512,2048]{1,0:T(8,128)(2,1)S(1)}, bf16[512,2048]{1,0:T(8,128)(2,1)S(1)}, u32[]{:S(2)}, u32[]{:S(2)}) %collective-permute-start.17) | collective-permute-done | bytes 2097184 | tf_op jit(solution)/shard_map/ppermute | solution.py:1207
  252.4 6.2 shard_map.231
  258.6 8.4 all-gather.9.cloned.1.call-done.gate_own.up_own
  272.3 45.3 %collective-permute-done.19.x_tokens_out.x_tokens = bf16[512,2048]{1,0:T(8,128)(2,1)S(1)} collective-permute-done((bf16[512,2048]{1,0:T(8,128)(2,1)}, bf16[512,2048]{1,0:T(8,128)(2,1)S(1)}, u32[]{:S(2)}, u32[]{:S(2)}) %collective-permute-start.19) | collective-permute-done | bytes 2097184 | tf_op jit(solution)/shard_map/ppermute | solution.py:1207
  318.9 66.0 %shard_map.232 = (bf16[2048,2048]{1,0:T(8,128)(2,1)}, bf16[2048,2048]{1,0:T(8,128)(2,1)}, bf16[2048,1536]{1,0:T(8,128)(2,1)}, bf16[2048,1536]{1,0:T(8,128)(2,1)}, bf16[2048,1536]{1,0:T(8,128)(2,1)}) custom-call(bf16[512,2048]{1,0:T(8,128)(2,1)} %copy-done.5, bf16[512,2048]{1,0:T(8,128)(2,1)} %collective-permute-done.20.y_tokens_out.y_tokens, ...), custom_call_target="tpu_custom_call" | custom-call | flops 1 | bytes 1 | tf_op jit(solution)/shard_map/pallas_call | solution.py:696
  385.0 11.3 %fusion.3 = bf16[1536,1024]{1,0:T(8,128)(2,1)} fusion(bf16[2048,1536]{1,0:T(8,128)(2,1)} %get-tuple-element.107.hidden, bf16[2048,2048]{1,0:T(8,128)(2,1)} %get-tuple-element.96.grads), kind=kOutput, calls=%fused_computation.9 | convolution fusion | flops 6444023808 | bytes 13631488 | tf_op jit(solution)/shard_map/dot_general | solution.py:77
  396.7 114.8 %shard_map.233 = (bf16[2048,1536]{1,0:T(8,128)(2,1)}, bf16[2048,1536]{1,0:T(8,128)(2,1)}, bf16[512,2048]{1,0:T(8,128)(2,1)}, bf16[512,2048]{1,0:T(8,128)(2,1)}, ...) custom-call(bf16[2048,2048]{1,0:T(8,128)(2,1)} %get-tuple-element.96.grads, bf16[2048,1536]{1,0:T(8,128)(2,1)} %get-tuple-element.107.hidden, ...), custom_call_target="tpu_custom_call" | custom-call | flops 1 | bytes 1 | tf_op jit(solution)/shard_map/pallas_call | solution.py:870
  511.6 11.8 %add_convert_fusion = bf16[1536,1024]{1,0:T(8,128)(2,1)} fusion(bf16[1536,1024]{1,0:T(8,128)(2,1)} %collective-permute-done.26, bf16[2048,1536]{1,0:T(8,128)(2,1)} %get-tuple-element.107.hidden, bf16[2048,2048]{1,0:T(8,128)(2,1)} %get-tuple-element.96.grads), kind=kOutput, calls=%fused_computation | convolution fusion | flops 6447169536 | bytes 16777216 | tf_op jit(solution)/shard_map/dot_general | solution.py:77
  523.5 11.1 %convolution_convert_fusion.1 = bf16[1536,1024]{1,0:T(8,128)(2,1)S(1)} fusion(bf16[2048,1536]{1,0:T(8,128)(2,1)} %get-tuple-element.105, bf16[2048,2048]{1,0:T(8,128)(2,1)} %get-tuple-element.104), kind=kOutput, calls=%fused_computation.8 | convolution fusion | flops 6444023808 | bytes 13631488 | tf_op jit(solution)/shard_map/dot_general | solution.py:77
  534.8 9.9 %convolution_convert_fusion = bf16[1536,1024]{1,0:T(8,128)(2,1)} fusion(bf16[2048,1536]{1,0:T(8,128)(2,1)S(1)} %bitcast.47, bf16[2048,2048]{1,0:T(8,128)(2,1)} %get-tuple-element.104), kind=kOutput, calls=%fused_computation.7 | convolution fusion | flops 6444023808 | bytes 13631488 | tf_op jit(solution)/shard_map/dot_general | solution.py:77
  544.7 8.2 add_convert_fusion.2
  553.5 8.0 shard_map.234
  563.6 11.2 %add_convert_fusion.1 = bf16[1536,1024]{1,0:T(8,128)(2,1)} fusion(bf16[1536,1024]{1,0:T(8,128)(2,1)S(1)} %collective-permute-done.25, bf16[2048,1536]{1,0:T(8,128)(2,1)} %get-tuple-element.106, bf16[2048,2048]{1,0:T(8,128)(2,1)} %get-tuple-element.104), kind=kOutput, calls=%fused_computation.1 | convolution fusion | flops 6447169536 | bytes 16777216 | tf_op jit(solution)/shard_map/dot_general | solution.py:77
  576.2 40.1 %shard_map.235 = (bf16[1024,2048]{1,0:T(8,128)(2,1)}, f32[16,128]{1,0:T(8,128)}) custom-call(s32[1]{0:T(128)} %bitcast.11.core, bf16[512,2048]{1,0:T(8,128)(2,1)} %get-tuple-element.101.own.right_own, bf16[512,2048]{1,0:T(8,128)(2,1)} %copy-done.7, bf16[1024,512]{1,0:T(8,128)(2,1)} %all-gather.7.cloned.1.call-done.w0.o0, bf16[1024,512]{1,0:T(8,128)(2,1)} %copy-done.8, ...), custom_call_target="tpu_custom_call" | custom-call | flops 1 | bytes 1 | tf_op jit(solution)/shard_map/pallas_call | solution.py:542
  616.3 40.9 %shard_map.236 = bf16[1024,512]{1,0:T(8,128)(2,1)} custom-call(bf16[1024,1024]{1,0:T(8,128)(2,1)} %get-tuple-element.121.left.left_own.left_other, bf16[1024,1024]{1,0:T(8,128)(2,1)} %get-tuple-element.121.left.left_own.left_other, bf16[512,2048]{1,0:T(8,128)(2,1)} %get-tuple-element.101.own.right_own, bf16[512,2048]{1,0:T(8,128)(2,1)} %copy-done.7), custom_call_target="tpu_custom_call" | custom-call | flops 1 | bytes 1 | tf_op jit(solution)/shard_map/pallas_call | solution.py:1043
  662.9 6.0 shard_map.237.refs_5_
  671.8 82.0 %shard_map.238 = (bf16[512,2048]{1,0:T(8,128)(2,1)}, f32[512,2048]{1,0:T(8,128)}, bf16[512,2048]{1,0:T(8,128)(2,1)}, bf16[512,2048]{1,0:T(8,128)(2,1)}) custom-call(bf16[512,2048]{1,0:T(8,128)(2,1)} %shard_map.228.own.left_own, bf16[512,2048]{1,0:T(8,128)(2,1)} %copy-done.6, bf16[1024,2048]{1,0:T(8,128)(2,1)} %get-tuple-element.122.right_own.right_other, ...), custom_call_target="tpu_custom_call" | custom-call | flops 1 | bytes 1 | tf_op jit(solution)/shard_map/pallas_call | solution.py:1043
  759.5 9.5 %shard_map.239 = (f32[512,2048]{1,0:T(8,128)}, bf16[512,2048]{1,0:T(8,128)(2,1)}, f32[8,2048]{1,0:T(8,128)}) custom-call(s32[1]{0:T(128)} %bitcast.place, bf16[512,2048]{1,0:T(8,128)(2,1)} %broadcast_select_fusion.1.inputs, f32[512,2048]{1,0:T(8,128)} %get-tuple-element.124.middle_grad, f32[512,2048]{1,0:T(8,128)} %get-tuple-element.125.own, ...), custom_call_target="tpu_custom_call" | custom-call | flops 1 | bytes 1 | tf_op jit(solution)/shard_map/pallas_call | solution.py:1133
  777.5 14.7 %collective-permute-done.35 = f32[4352]{0:T(1024)S(1)} collective-permute-done((f32[4352]{0:T(1024)S(1)}, f32[4352]{0:T(1024)S(1)}, u32[]{:S(2)}, u32[]{:S(2)}) %collective-permute-start.35) | collective-permute-done | bytes 17440 | tf_op jit(solution)/shard_map/ppermute | solution.py:1207
  801.4 10.3 %reduce-scatter.14.cloned.1.call-done = bf16[512,512]{1,0:T(8,128)(2,1)} async-done(((bf16[512,2048]{1,0:T(8,128)(2,1)}), bf16[512,512]{1,0:T(8,128)(2,1)}) %reduce-scatter.14.cloned.1.call-update) | async-done | bytes 524304 | tf_op jit(solution)/shard_map/reduce_scatter | solution.py:1473
  817.1 6.2 collective-permute-start.42
  823.7 5.8 convert_select_fusion
  (218 shorter events, 106.1 us)
Async XLA Ops:
  7.2 53.6 %all-gather.5.cloned.1.call-start = ((), (), s32[]{:S(2)}) async-start(), calls=%async_computation.5 | async-start | bytes 2621440 | tf_op jit(solution)/shard_map/all_gather | solution.py:1307
  12.1 139.4 %all-gather.7.cloned.1.call-start = ((), (), s32[]{:S(2)}) async-start(), calls=%async_computation.6 | async-start | bytes 1310720 | tf_op jit(solution)/shard_map/all_gather | solution.py:1323
  13.1 18.0 %collective-permute-start.3 = (bf16[1152,256]{1,0:T(8,128)(2,1)S(1)}, bf16[1152,256]{1,0:T(8,128)(2,1)S(1)}, u32[]{:S(2)}, u32[]{:S(2)}) collective-permute-start(bf16[1152,256]{1,0:T(8,128)(2,1)S(1)} %get-tuple-element.153), channel_id=1, source_target_pairs={{0,24},{4,28},{8,16},{12,20},{16,8},{20,12},{24,0},{28,4},{1,25},{... | collective-permute-start | bytes 1769480 | tf_op jit(solution)/shard_map/ppermute | solution.py:1207
  17.0 26.3 %collective-permute-start.2 = (bf16[1152,256]{1,0:T(8,128)(2,1)S(1)}, bf16[1152,256]{1,0:T(8,128)(2,1)S(1)}, u32[]{:S(2)}, u32[]{:S(2)}) collective-permute-start(bf16[1152,256]{1,0:T(8,128)(2,1)S(1)} %get-tuple-element.154), channel_id=1, source_target_pairs={{0,16},{4,20},{8,24},{12,28},{16,0},{20,4},{24,8},{28,12},{1,17},{... | collective-permute-start | bytes 1769480 | tf_op jit(solution)/shard_map/ppermute | solution.py:1207
  17.5 26.1 %collective-permute-start.1 = (bf16[1152,256]{1,0:T(8,128)(2,1)S(1)}, bf16[1152,256]{1,0:T(8,128)(2,1)S(1)}, u32[]{:S(2)}, u32[]{:S(2)}) collective-permute-start(bf16[1152,256]{1,0:T(8,128)(2,1)S(1)} %get-tuple-element.155), channel_id=1, source_target_pairs={{0,8},{4,12},{8,0},{12,4},{16,24},{20,28},{24,16},{28,20},{1,9},{5... | collective-permute-start | bytes 1769480 | tf_op jit(solution)/shard_map/ppermute | solution.py:1207
  64.8 48.3 %collective-permute-start.8 = (bf16[512,2048]{1,0:T(8,128)(2,1)}, bf16[512,2048]{1,0:T(8,128)(2,1)S(1)}, u32[]{:S(2)}, u32[]{:S(2)}) collective-permute-start(bf16[512,2048]{1,0:T(8,128)(2,1)} %all-gather.5.cloned.1.call-done.w0.refs_0_), channel_id=1, source_target_pairs={{0,8},{4,12},{8,0},{12,4},{16,24},{20,28},{24,16},{28,20},{1,9},{5... | collective-permute-start | bytes 6291464 | tf_op jit(solution)/shard_map/ppermute | solution.py:1207
  66.3 48.6 %collective-permute-start.9 = (bf16[512,2048]{1,0:T(8,128)(2,1)}, bf16[512,2048]{1,0:T(8,128)(2,1)}, u32[]{:S(2)}, u32[]{:S(2)}) collective-permute-start(bf16[512,2048]{1,0:T(8,128)(2,1)} %all-gather.5.cloned.1.call-done.w0.refs_0_), channel_id=1, source_target_pairs={{0,16},{4,20},{8,24},{12,28},{16,0},{20,4},{24,8},{28,12},{1,17},{... | collective-permute-start | bytes 6291464 | tf_op jit(solution)/shard_map/ppermute | solution.py:1207
  114.9 152.1 %all-gather.9.cloned.1.call-start = ((), (), s32[]{:S(2)}) async-start(), calls=%async_computation.7 | async-start | bytes 7864320 | tf_op jit(solution)/shard_map/all_gather | solution.py:1347
  123.6 25.3 %collective-permute-start.10 = (bf16[256,2048]{1,0:T(8,128)(2,1)S(1)}, bf16[256,2048]{1,0:T(8,128)(2,1)}, u32[]{:S(2)}, u32[]{:S(2)}) collective-permute-start(bf16[256,2048]{1,0:T(8,128)(2,1)S(1)} %slice.104), channel_id=1, source_target_pairs={{0,16},{4,20},{8,24},{12,28},{16,0},{20,4},{24,8},{28,12},{1,17},{... | collective-permute-start | bytes 3145736 | tf_op jit(solution)/shard_map/ppermute | solution.py:1207
  126.4 25.1 %collective-permute-start.11 = (bf16[256,2048]{1,0:T(8,128)(2,1)S(1)}, bf16[256,2048]{1,0:T(8,128)(2,1)}, u32[]{:S(2)}, u32[]{:S(2)}) collective-permute-start(bf16[256,2048]{1,0:T(8,128)(2,1)S(1)} %slice.105), channel_id=1, source_target_pairs={{0,8},{4,12},{8,0},{12,4},{16,24},{20,28},{24,16},{28,20},{1,9},{5... | collective-permute-start | bytes 3145736 | tf_op jit(solution)/shard_map/ppermute | solution.py:1207
  154.2 230.7 %all-gather.11.cloned.1.call-start = ((), (), s32[]{:S(2)}) async-start(), calls=%async_computation.8 | async-start | bytes 3932160 | tf_op jit(solution)/shard_map/all_gather | solution.py:1350
  154.8 33.8 %collective-permute-start.12 = (bf16[1024,512]{1,0:T(8,128)(2,1)}, bf16[1024,512]{1,0:T(8,128)(2,1)S(1)}, u32[]{:S(2)}, u32[]{:S(2)}) collective-permute-start(bf16[1024,512]{1,0:T(8,128)(2,1)} %all-gather.7.cloned.1.call-done.w0.o0), channel_id=1, source_target_pairs={{0,8},{4,12},{8,0},{12,4},{16,24},{20,28},{24,16},{28,20},{1,9},{5... | collective-permute-start | bytes 3145736 | tf_op jit(solution)/shard_map/ppermute | solution.py:1207
  155.9 32.8 %collective-permute-start.13 = (bf16[1024,512]{1,0:T(8,128)(2,1)}, bf16[1024,512]{1,0:T(8,128)(2,1)S(1)}, u32[]{:S(2)}, u32[]{:S(2)}) collective-permute-start(bf16[1024,512]{1,0:T(8,128)(2,1)} %all-gather.7.cloned.1.call-done.w0.o0), channel_id=1, source_target_pairs={{0,16},{4,20},{8,24},{12,28},{16,0},{20,4},{24,8},{28,12},{1,17},{... | collective-permute-start | bytes 3145736 | tf_op jit(solution)/shard_map/ppermute | solution.py:1207
  190.6 57.6 %collective-permute-start.17 = (bf16[512,2048]{1,0:T(8,128)(2,1)S(1)}, bf16[512,2048]{1,0:T(8,128)(2,1)S(1)}, u32[]{:S(2)}, u32[]{:S(2)}) collective-permute-start(bf16[512,2048]{1,0:T(8,128)(2,1)S(1)} %broadcast_select_fusion.own_grads.cotangent), channel_id=1, source_target_pairs={{0,8},{4,12},{8,0},{12,4},{16,24},{20,28},{24,16},{28,20},{1,9},{5... | collective-permute-start | bytes 6291464 | tf_op jit(solution)/shard_map/ppermute | solution.py:1207
  191.7 56.6 %collective-permute-start.18 = (bf16[512,2048]{1,0:T(8,128)(2,1)S(1)}, bf16[512,2048]{1,0:T(8,128)(2,1)S(1)}, u32[]{:S(2)}, u32[]{:S(2)}) collective-permute-start(bf16[512,2048]{1,0:T(8,128)(2,1)S(1)} %broadcast_select_fusion.own_grads.cotangent), channel_id=1, source_target_pairs={{0,16},{4,20},{8,24},{12,28},{16,0},{20,4},{24,8},{28,12},{1,17},{... | collective-permute-start | bytes 6291464 | tf_op jit(solution)/shard_map/ppermute | solution.py:1207
  213.7 35.9 %collective-permute-start.16 = (bf16[512,2048]{1,0:T(8,128)(2,1)}, bf16[512,2048]{1,0:T(8,128)(2,1)S(1)}, u32[]{:S(2)}, u32[]{:S(2)}) collective-permute-start(bf16[512,2048]{1,0:T(8,128)(2,1)} %get-tuple-element.87), channel_id=1, source_target_pairs={{0,4},{4,0},{8,12},{12,8},{16,20},{20,16},{24,28},{28,24},{1,5},{5... | collective-permute-start | bytes 6291464 | tf_op jit(solution)/shard_map/ppermute | solution.py:1207
  267.0 51.9 %collective-permute-start.21 = (bf16[2,1536,1024]{2,1,0:T(8,128)(2,1)}, bf16[2,1536,1024]{2,1,0:T(8,128)(2,1)}, u32[]{:S(2)}, u32[]{:S(2)}) collective-permute-start(bf16[2,1536,1024]{2,1,0:T(8,128)(2,1)} %all-gather.9.cloned.1.call-done.gate_own.up_own), channel_id=1, source_target_pairs={{0,4},{4,0},{8,12},{12,8},{16,20},{20,16},{24,28},{28,24},{1,5},{5... | collective-permute-start | bytes 18874376 | tf_op jit(solution)/shard_map/ppermute | solution.py:1207
  269.1 389.0 %reduce-scatter.6.cloned.1.call-start = ((), (), s32[]{:S(2)}) async-start(), calls=%async_computation.9 | async-start | bytes 3932160 | tf_op jit(solution)/shard_map/reduce_scatter | solution.py:1388
  269.3 48.3 %collective-permute-start.19 = (bf16[512,2048]{1,0:T(8,128)(2,1)}, bf16[512,2048]{1,0:T(8,128)(2,1)S(1)}, u32[]{:S(2)}, u32[]{:S(2)}) collective-permute-start(bf16[512,2048]{1,0:T(8,128)(2,1)} %get-tuple-element.91.own_tokens), channel_id=1, source_target_pairs={{0,8},{4,12},{8,0},{12,4},{16,24},{20,28},{24,16},{28,20},{1,9},{5... | collective-permute-start | bytes 6291464 | tf_op jit(solution)/shard_map/ppermute | solution.py:1207
  270.9 48.0 %collective-permute-start.20 = (bf16[512,2048]{1,0:T(8,128)(2,1)}, bf16[512,2048]{1,0:T(8,128)(2,1)}, u32[]{:S(2)}, u32[]{:S(2)}) collective-permute-start(bf16[512,2048]{1,0:T(8,128)(2,1)} %get-tuple-element.91.own_tokens), channel_id=1, source_target_pairs={{0,16},{4,20},{8,24},{12,28},{16,0},{20,4},{24,8},{28,12},{1,17},{... | collective-permute-start | bytes 6291464 | tf_op jit(solution)/shard_map/ppermute | solution.py:1207
  396.2 115.3 %collective-permute-start.26 = (bf16[1536,1024]{1,0:T(8,128)(2,1)}, bf16[1536,1024]{1,0:T(8,128)(2,1)}, u32[]{:S(2)}, u32[]{:S(2)}) collective-permute-start(bf16[1536,1024]{1,0:T(8,128)(2,1)} %fusion.3), channel_id=1, source_target_pairs={{0,4},{4,0},{8,12},{12,8},{16,20},{20,16},{24,28},{28,24},{1,5},{5... | collective-permute-start | bytes 9437192 | tf_op jit(solution)/shard_map/ppermute | solution.py:1207
  523.4 148.4 %reduce-scatter.8.cloned.1.call-start = ((), (), s32[]{:S(2)}) async-start(), calls=%async_computation.10 | async-start | bytes 3932160 | tf_op jit(solution)/shard_map/reduce_scatter | solution.py:1388
  552.9 200.9 %reduce-scatter.12.cloned.1.call-start = ((), (), s32[]{:S(2)}) async-start(), calls=%async_computation.12 | async-start | bytes 1310720 | tf_op jit(solution)/shard_map/reduce_scatter | solution.py:1388
  561.5 54.8 %collective-permute-start.30 = (bf16[512,2048]{1,0:T(8,128)(2,1)}, bf16[512,2048]{1,0:T(8,128)(2,1)}, u32[]{:S(2)}, u32[]{:S(2)}) collective-permute-start(bf16[512,2048]{1,0:T(8,128)(2,1)} %get-tuple-element.116), channel_id=1, source_target_pairs={{0,8},{4,12},{8,0},{12,4},{16,24},{20,28},{24,16},{28,20},{1,9},{5... | collective-permute-start | bytes 6291464 | tf_op jit(solution)/shard_map/ppermute | solution.py:1207
  562.1 54.3 %collective-permute-start.31 = (bf16[512,2048]{1,0:T(8,128)(2,1)}, bf16[512,2048]{1,0:T(8,128)(2,1)}, u32[]{:S(2)}, u32[]{:S(2)}) collective-permute-start(bf16[512,2048]{1,0:T(8,128)(2,1)} %get-tuple-element.117), channel_id=1, source_target_pairs={{0,16},{4,20},{8,24},{12,28},{16,0},{20,4},{24,8},{28,12},{1,17},{... | collective-permute-start | bytes 6291464 | tf_op jit(solution)/shard_map/ppermute | solution.py:1207
  657.2 97.7 %reduce-scatter.10.cloned.1.call-start = ((), (), s32[]{:S(2)}) async-start(), calls=%async_computation.11 | async-start | bytes 3932160 | tf_op jit(solution)/shard_map/reduce_scatter | solution.py:1388
  658.0 153.7 %reduce-scatter.14.cloned.1.call-start = ((), (), s32[]{:S(2)}) async-start(), calls=%async_computation.13 | async-start | bytes 2621440 | tf_op jit(solution)/shard_map/reduce_scatter | solution.py:1473
  769.0 45.5 %collective-permute-start.33 = (bf16[512,2048]{1,0:T(8,128)(2,1)}, bf16[512,2048]{1,0:T(8,128)(2,1)}, u32[]{:S(2)}, u32[]{:S(2)}) collective-permute-start(bf16[512,2048]{1,0:T(8,128)(2,1)} %get-tuple-element.127), channel_id=1, source_target_pairs={{1,4},{3,6},{4,1},{6,3},{9,12},{11,14},{12,9},{14,11},{17,20},{19,... | collective-permute-start | bytes 6291464 | tf_op jit(solution)/shard_map/ppermute | solution.py:1216
  772.2 25.2 %collective-permute-start.39 = (bf16[768,256]{1,0:T(8,128)(2,1)S(1)}, bf16[768,256]{1,0:T(8,128)(2,1)S(1)}, u32[]{:S(2)}, u32[]{:S(2)}) collective-permute-start(bf16[768,256]{1,0:T(8,128)(2,1)S(1)} %get-tuple-element.159), channel_id=1, source_target_pairs={{0,24},{4,28},{8,16},{12,20},{16,8},{20,12},{24,0},{28,4},{1,25},{... | collective-permute-start | bytes 1179656 | tf_op jit(solution)/shard_map/ppermute | solution.py:1207
  773.7 23.7 %collective-permute-start.38 = (bf16[768,256]{1,0:T(8,128)(2,1)S(1)}, bf16[768,256]{1,0:T(8,128)(2,1)S(1)}, u32[]{:S(2)}, u32[]{:S(2)}) collective-permute-start(bf16[768,256]{1,0:T(8,128)(2,1)S(1)} %get-tuple-element.160), channel_id=1, source_target_pairs={{0,16},{4,20},{8,24},{12,28},{16,0},{20,4},{24,8},{28,12},{1,17},{... | collective-permute-start | bytes 1179656 | tf_op jit(solution)/shard_map/ppermute | solution.py:1207
  774.3 23.1 %collective-permute-start.37 = (bf16[768,256]{1,0:T(8,128)(2,1)S(1)}, bf16[768,256]{1,0:T(8,128)(2,1)S(1)}, u32[]{:S(2)}, u32[]{:S(2)}) collective-permute-start(bf16[768,256]{1,0:T(8,128)(2,1)S(1)} %get-tuple-element.161), channel_id=1, source_target_pairs={{0,8},{4,12},{8,0},{12,4},{16,24},{20,28},{24,16},{28,20},{1,9},{5... | collective-permute-start | bytes 1179656 | tf_op jit(solution)/shard_map/ppermute | solution.py:1207
  812.7 17.9 %collective-permute-start.43 = (bf16[256,512]{1,0:T(8,128)(2,1)S(1)}, bf16[256,512]{1,0:T(8,128)(2,1)S(1)}, u32[]{:S(2)}, u32[]{:S(2)}) collective-permute-start(bf16[256,512]{1,0:T(8,128)(2,1)S(1)} %constant_dynamic-slice_fusion.3), channel_id=1, source_target_pairs={{0,4},{4,0},{8,12},{12,8},{16,20},{20,16},{24,28},{28,24},{1,5},{5... | collective-permute-start | bytes 786440 | tf_op jit(solution)/shard_map/ppermute | solution.py:1207
  (49 other events, 715.3 us)
Sparse Core Ops, SparseCore 0:
  12.2 48.5 all-gather.4
  115.0 25.6 all-gather.6
  154.3 112.6 all-gather.8
  269.2 61.7 all-gather.10
  523.5 57.5 reduce-scatter.5
  583.3 60.2 reduce-scatter.7
  657.4 24.6 reduce-scatter.11
  684.5 70.4 reduce-scatter.9
  757.3 54.3 reduce-scatter.13

commit v4 on v3

--- a/solution.py
+++ b/solution.py
@@ -912,7 +912,20 @@
     )
 
 
-def outer_kernel(extra, left_own, left_other, right_own, right_other, *refs):
+def core_copy(source, target, send, receive, n, chunk):
+    me = lax.axis_index("dp")
+    rows = pl.ds(n * chunk, chunk)
+    return pltpu.make_async_remote_copy(
+        src_ref=source.at[rows],
+        dst_ref=target.at[rows],
+        send_sem=send.at[n],
+        recv_sem=receive.at[n],
+        device_id={"dp": me + 1 - 2 * (me % 2)},
+        device_id_type=MESH,
+    )
+
+
+def outer_kernel(extra, more, left_own, left_other, right_own, right_other, *refs):
     weights = refs[:extra]
     if extra:
         layer, total_out, *spread, layer_out = refs[extra : extra + 5]
@@ -920,6 +933,15 @@
         stay = pltpu.make_async_copy(layer, layer_out, refs[-1].at[0])
         crossing = is_crossing()
         refs = refs[:-3]
+    elif more:
+        product_left, product_right, total_out, product_out = refs[:4]
+        product_own, product_send, product_got, product_sent, product_came = refs[-5:]
+        refs = refs[:-5]
+        chunk = product_left.shape[1]
+        exchanges = [
+            core_copy(product_send, product_got, product_sent, product_came, n, chunk)
+            for n in range(more)
+        ]
     else:
         total_out = refs[0]
     own, corner, send_x, send_y, got_corner, got_x, got_y, send, receive = refs[-9:]
@@ -932,8 +954,8 @@
 
         @pl.when(step == 0)
         def _():
-            _, over_x, over_y = neighbours()
-            greet((over_x, over_y))
+            me, over_x, over_y = neighbours()
+            greet((over_x, over_y) + ((me + 1 - 2 * (me % 2),) if more else ()))
 
     else:
 
@@ -984,9 +1006,24 @@
             spread[0][:, cols] = dot_last(right_own[...], weight[...])
             spread[1][:, cols] = dot_last(right_other[...], weight[...]).astype(jnp.bfloat16)
 
+    if more:
+
+        @pl.when(step >= 8)
+        def _():
+            product = dot_first(product_left[...], product_right[...])
+            middle = product_own.shape[1]
+            for n in range(more):
+
+                @pl.when(step == 8 + n)
+                def _():
+                    rows = slice(n * chunk, (n + 1) * chunk)
+                    product_own[rows, :] = product[:, :middle]
+                    product_send[rows, :] = product[:, middle:].astype(jnp.bfloat16)
+                    exchanges[n].start()
+
     last = pl.num_programs(0) - 1
 
-    @pl.when(step == min(9, 7 + extra))
+    @pl.when(step == min(9, 7 + extra + more))
     def _():
         copies[1].wait_recv()
         add_into(send_y, high, got_corner)
@@ -1005,6 +1042,16 @@
         for transfer in copies:
             transfer.wait_send()
 
+    if more:
+
+        @pl.when(step == last)
+        def _():
+            for transfer in exchanges:
+                transfer.wait()
+            product_out[...] = (
+                product_own[...] + product_got[...].astype(jnp.float32)
+            ).astype(jnp.bfloat16)
+
     if extra:
 
         @pl.when((step == last) & crossing)
@@ -1016,7 +1063,7 @@
             stay.wait()
 
 
-def outer(lefts, rights, by_left, collective_id, weights=(), layer=None):
+def outer(lefts, rights, by_left, collective_id, weights=(), layer=None, product=None):
     rows = 512
     wide = lefts[0][0].shape[1]
     right_wide = rights[0][0].shape[1]
@@ -1029,8 +1076,8 @@
     else:
         size = (wide // 2, right_wide // 4)
         left_size = (rows, wide // 2)
-        place_left = lambda row: lambda s: (row, s % 2)
-        place_right = lambda row: lambda s: (row, 3 - s // 2)
+        place_left = lambda row: lambda s: (row, jnp.minimum(s, 7) % 2)
+        place_right = lambda row: lambda s: (row, 3 - jnp.minimum(s, 7) // 2)
     both = (2 * size[0], size[1])
     spec, shape = pl.BlockSpec, jax.ShapeDtypeStruct
     out_specs = [spec(both, lambda s: (0, 0))]
@@ -1040,28 +1087,53 @@
         out_shape += [shape((rows, wide), jnp.float32), shape((rows, wide), jnp.bfloat16)]
         out_specs += [spec(memory_space=pl.ANY)]
         out_shape += [shape(layer.shape, layer.dtype)]
+    more, product_specs = 0, []
+    if product:
+        chunk = 256
+        tokens, hidden_count = product[0].shape
+        more = hidden_count // chunk
+        turn = lambda s: jnp.maximum(s - 8, 0)
+        product_specs = [
+            spec((tokens, chunk), lambda s: (0, turn(s))),
+            spec(product[1].shape, lambda s: (0, 0), pipeline_mode=pl.Buffered(1)),
+        ]
+        half = product[1].shape[1] // 2
+        out_specs += [spec((hidden_count, half), lambda s: (0, 0))]
+        out_shape += [shape((hidden_count, half), jnp.bfloat16)]
     made = pl.pallas_call(
-        functools.partial(outer_kernel, len(weights)),
-        grid=(8 + len(weights),),
+        functools.partial(outer_kernel, len(weights), more),
+        grid=(8 + len(weights) + more,),
         in_specs=[spec(left_size, place_left(row)) for _, row in lefts]
         + [spec((rows, size[1]), place_right(row)) for _, row in rights]
         + [
             spec(weight.shape, lambda s: (0, 0), pipeline_mode=pl.Buffered(1))
             for weight in weights
         ]
-        + ([spec(memory_space=pl.ANY)] if weights else []),
+        + ([spec(memory_space=pl.ANY)] if weights else [])
+        + product_specs,
         out_specs=out_specs,
         out_shape=out_shape,
         scratch_shapes=[pltpu.VMEM(both, jnp.float32)]
         + [pltpu.VMEM(both, jnp.bfloat16)] * 6
         + [pltpu.SemaphoreType.DMA((6,)), pltpu.SemaphoreType.DMA((6,))]
-        + ([pltpu.SemaphoreType.DMA((1,))] * 3 if weights else []),
+        + ([pltpu.SemaphoreType.DMA((1,))] * 3 if weights else [])
+        + (
+            [
+                pltpu.VMEM((hidden_count, half), jnp.float32),
+                pltpu.VMEM((hidden_count, half), jnp.bfloat16),
+                pltpu.VMEM((hidden_count, half), jnp.bfloat16),
+                pltpu.SemaphoreType.DMA((more,)),
+                pltpu.SemaphoreType.DMA((more,)),
+            ]
+            if product
+            else []
+        ),
         compiler_params=pltpu.CompilerParams(
             collective_id=collective_id, has_side_effects=True, vmem_limit_bytes=60 * 2**20
         ),
         cost_estimate=pl.CostEstimate(flops=1, bytes_accessed=1, transcendentals=0),
-    )(*[array for array, _ in (*lefts, *rights)], *weights, *([layer] if weights else []))
-    return made if weights else made[0]
+    )(*[array for array, _ in (*lefts, *rights)], *weights, *([layer] if weights else []), *(product or []))
+    return made
 
 
 def columns_kernel(transposed, place, left, w0, w1, w2, w3_low, w3_high, own, other):
@@ -1316,7 +1388,8 @@
         [piece_for(0)] + [exchange(piece_for(k), 2 * k) for k in (1, 2, 3)], 1
     )
 
-    qkv_z = after(qkv_z, feed_own)
+    gate_up_own, down_part = feed_own[: 2 * units], feed_own[2 * units :]
+    qkv_z = after(qkv_z, (gate_up_own, down_part))
     qkv_near = gather_near(qkv_z)
     moved = swap_halves(after(layer_input, qkv_z))
     moved_grad = swap_halves(after(out_grad, qkv_z))
@@ -1343,11 +1416,11 @@
         *gather_far(after(qkv_near, (normed, cosines, sines, cotangent))),
     ]
     out_near = gather_near(after(out_z, qkv_chips))
-    feed_own = after(feed_own, (out_z, qkv_chips))
+    gate_up_own, down_part = after((gate_up_own, down_part), (out_z, qkv_chips))
     gate_up_half = lax.all_gather(
-        feed_own[: 2 * units].reshape(2, units, width // 2), "mp", axis=1, tiled=True
-    )
-    down_half = lax.all_gather(feed_own[2 * units :], "mp", axis=0, tiled=True)
+        gate_up_own.reshape(2, units, width // 2), "mp", axis=1, tiled=True
+    )
+    down_half = lax.all_gather(down_part, "mp", axis=0, tiled=True)
     normed_other = after(exchange(normed, 1), out_z)
     proj, query_rot, key_rot, value_low, attended, log_total = attend(
         core_index,
@@ -1396,8 +1469,6 @@
         down_w,
     )
     gate_other = dot_first(all_gate, all_tokens[:, half:]).astype(bf16)
-    up_other = dot_first(all_up, all_tokens[:, half:]).astype(bf16)
-    all_gate, all_up = after((all_gate, all_up), (gate_other, up_other))
 
     def own_half(left, right, other):
         own = dot_first(left, right[:, :half])
@@ -1406,8 +1477,7 @@
     down_local = own_half(after(all_hidden, two_grad), all_grads, down_other)
     down_sum = over_z(down_local)
     gate_local = own_half(all_gate, all_tokens, gate_other)
-    up_local = own_half(all_up, all_tokens, up_other)
-    gate_sum, up_sum = over_z(gate_local), over_z(up_local)
+    gate_sum = over_z(gate_local)
     middle_grad, branch, gain_two_part = tile_call(
         middle_back_kernel,
         place,
@@ -1433,7 +1503,17 @@
     down_got, cols = unspread(down_sum)
     down_own = chips_in_order(down_got, cols, slice(0, units)).astype(f32)
 
-    branch_pair = after(exchange(branch, 1), (gate_local, up_local, down_local))
+    branch_pair = after(exchange(branch, 1), (gate_local, down_local))
+    out_local, up_local = outer(
+        [(attended, 0), (attended, 1)],
+        [(branch, 0), (branch_pair, 0)],
+        False,
+        4,
+        product=(all_up, all_tokens),
+    )
+    up_sum = over_z(up_local)
+    out_sum = over_z(out_local)
+    branch_pair, out_x, out_y = after((branch_pair, out_x, out_y), out_local)
     out_parts = [out_own, exchange(out_x, 2), exchange(out_y, 4)]
     proj_grad, head_gains = attend_back(
         core_index,
@@ -1457,10 +1537,7 @@
         [(array((rows, width), bf16), "rows")],
         12,
     )
-    attended = after(attended, (proj_grad, out_parts))
-    out_local = outer([(attended, 0), (attended, 1)], [(branch, 0), (branch_pair, 0)], False, 4)
-    out_sum = over_z(out_local)
-    proj_grad = after(proj_grad, (down_own, gate_sum, out_local))
+    proj_grad = after(proj_grad, (down_sum, gate_sum, out_local))
     qkv_local, one_own, one_other, output_moved = outer(
         [(normed, 0), (normed_other, 0)],
         [(proj_grad, 0), (proj_grad, 1)],

time: 847 us -> 834 us (0.985)
  matrix products: 63.5 us -> 43.5 us
    dot_general x6 -> x4, matrix products: 63.5 us -> 43.5 us  [dot_first(): lax.dot_general(left, right, (((0,), (0,)), ((), ())), preferred_element_...]
    ppermute x39 -> x38, waiting for transfers between devices: 212 us -> 229 us  [exchange(): return lax.ppermute(values, 'dp', [(i, i ^ bit) for i in range(8)])]
    reduce_scatter x1, waiting for transfers between devices: 10.3 us -> 0.01 us  [fast(): qkv_sum = lax.psum_scatter(qkv_local, 'mp', scatter_dimension=1, tiled=True)]
    ppermute x39 -> x38, starting transfers between devices: 32.8 us -> 35.8 us  [exchange(): return lax.ppermute(values, 'dp', [(i, i ^ bit) for i in range(8)])]
  transfers between devices with their start and end apart: 54 -> 53, of which waited for: 24 -> 25; matrix products, arithmetic and copies ran while one was open for 10% -> 8% of each run, Pallas kernels for 49% -> 50%
where the time goes in v4:
time: 834 us; the launch traced here: 829 us
  Pallas kernels  418 us (50%)
  waiting for transfers between devices  253 us (30%)
  starting transfers between devices  51.2 us (6%)
  matrix products  43.5 us (5%)
  other arithmetic  24.7 us (3%)
  local copies, waits for them, and re-layouts  23.4 us (3%)
  between operations  14.7 us (2%)
    ppermute x38, waiting for transfers between devices, exchange(): return lax.ppermute(values, 'dp', [(i, i ^ bit) for i in range(8)])  229 us
    pallas_call x2, Pallas kernels, outer(): pl.pallas_call(functools.partial(outer_kernel, len(weights), more), grid=...  127 us
    pallas_call x1, Pallas kernels, feed_back(): pl.pallas_call(feed_back_kernel, grid=(4, hidden_count // chunk), in_spec...  115 us
    pallas_call x1, Pallas kernels, gather_hidden(): pl.pallas_call(hidden_kernel, grid=(4, hidden_count // chunk), in_specs=[...  66.2 us
    dot_general x4, matrix products, dot_first(): lax.dot_general(left, right, (((0,), (0,)), ((), ())), preferred_element_...  43.5 us
    pallas_call x1, Pallas kernels, attend_back(): pl.pallas_call(attend_back_kernel, grid_spec=pltpu.PrefetchScalarGridSpec...  40.2 us
    ppermute x38, starting transfers between devices, exchange(): return lax.ppermute(values, 'dp', [(i, i ^ bit) for i in range(8)])  35.8 us
    pallas_call x5, Pallas kernels, tile_call(): pl.pallas_call(kernel, grid_spec=pltpu.PrefetchScalarGridSpec(num_scalar_...  32.9 us
  transfers between devices with their start and end apart: 53, of which 25 were waited for; matrix products, arithmetic and copies ran while one was open for 8% of the time, Pallas kernels for 50%

profile of v4, /device:TPU:0, one launch (start us, length us, event | category | flops | bytes accessed | tf_op | source)
XLA Modules:
  0.0 828.6 jit_solution(13612932915620642910)
XLA Ops:
  13.1 3.9 collective-permute-start.3
  17.6 13.5 %collective-permute-done.3 = bf16[1152,256]{1,0:T(8,128)(2,1)S(1)} collective-permute-done((bf16[1152,256]{1,0:T(8,128)(2,1)S(1)}, bf16[1152,256]{1,0:T(8,128)(2,1)S(1)}, u32[]{:S(2)}, u32[]{:S(2)}) %collective-permute-start.3) | collective-permute-done | bytes 589856 | tf_op jit(solution)/shard_map/ppermute | solution.py:1279
  31.1 12.1 %collective-permute-done.2 = bf16[1152,256]{1,0:T(8,128)(2,1)S(1)} collective-permute-done((bf16[1152,256]{1,0:T(8,128)(2,1)S(1)}, bf16[1152,256]{1,0:T(8,128)(2,1)S(1)}, u32[]{:S(2)}, u32[]{:S(2)}) %collective-permute-start.2) | collective-permute-done | bytes 589856 | tf_op jit(solution)/shard_map/ppermute | solution.py:1279
  46.1 14.7 %all-gather.5.cloned.1.call-done.w0.refs_0_ = bf16[512,2048]{1,0:T(8,128)(2,1)} async-done(((bf16[512,512]{1,0:T(8,128)(2,1)}), bf16[512,2048]{1,0:T(8,128)(2,1)}) %all-gather.5.cloned.1.call-update) | async-done | bytes 2097168 | tf_op jit(solution)/shard_map/all_gather | solution.py:1379
  72.8 40.3 %collective-permute-done.8.w1.refs_1_ = bf16[512,2048]{1,0:T(8,128)(2,1)S(1)} collective-permute-done((bf16[512,2048]{1,0:T(8,128)(2,1)}, bf16[512,2048]{1,0:T(8,128)(2,1)S(1)}, u32[]{:S(2)}, u32[]{:S(2)}) %collective-permute-start.8) | collective-permute-done | bytes 2097184 | tf_op jit(solution)/shard_map/ppermute | solution.py:1279
  127.1 21.8 %collective-permute-done.10.w3_low.refs_3_ = bf16[256,2048]{1,0:T(8,128)(2,1)} collective-permute-done((bf16[256,2048]{1,0:T(8,128)(2,1)S(1)}, bf16[256,2048]{1,0:T(8,128)(2,1)}, u32[]{:S(2)}, u32[]{:S(2)}) %collective-permute-start.10) | collective-permute-done | bytes 1048608 | tf_op jit(solution)/shard_map/ppermute | solution.py:1279
  157.8 28.0 %shard_map.229 = (f32[1024,2048]{1,0:T(8,128)}, bf16[1024,1024]{1,0:T(8,128)(2,1)}, bf16[1024,512]{1,0:T(8,128)(2,1)}, bf16[1024,512]{1,0:T(8,128)(2,1)}, bf16[1...) custom-call(s32[1]{0:T(128)} %bitcast.11.core, bf16[512,2048]{1,0:T(8,128)(2,1)} %shard_map.228.own.left_own, ...), custom_call_target="tpu_custom_call" | custom-call | flops 1 | bytes 1 | tf_op jit(solution)/shard_map/pallas_call | solution.py:419
  190.2 10.6 %collective-permute-done.14.w3_low.o3_low = bf16[512,512]{1,0:T(8,128)(2,1)S(1)} collective-permute-done((bf16[512,512]{1,0:T(8,128)(2,1)S(1)}, bf16[512,512]{1,0:T(8,128)(2,1)S(1)}, u32[]{:S(2)}, u32[]{:S(2)}) %collective-permute-start.14) | collective-permute-done | bytes 524320 | tf_op jit(solution)/shard_map/ppermute | solution.py:1279
  201.8 9.2 %shard_map.230 = (f32[512,2048]{1,0:T(8,128)}, bf16[512,2048]{1,0:T(8,128)(2,1)}) custom-call(s32[1]{0:T(128)} %bitcast.place, bf16[1024,1024]{1,0:T(8,128)(2,1)} %get-tuple-element.85.left.left_own.left_other, bf16[1024,512]{1,0:T(8,128)(2,1)} %all-gather.7.cloned.1.call-done.w0.o0, bf16[1024,512]{1,0:T(8,128)(2,1)} %copy-done.8, ...), custom_call_target="tpu_custom_call" | custom-call | flops 1 | bytes 1 | tf_op jit(solution)/shard_map/pallas_call | solution.py:1180
  211.0 34.5 %collective-permute-done.17.x_grads_out.x_grads = bf16[512,2048]{1,0:T(8,128)(2,1)S(1)} collective-permute-done((bf16[512,2048]{1,0:T(8,128)(2,1)S(1)}, bf16[512,2048]{1,0:T(8,128)(2,1)S(1)}, u32[]{:S(2)}, u32[]{:S(2)}) %collective-permute-start.17) | collective-permute-done | bytes 2097184 | tf_op jit(solution)/shard_map/ppermute | solution.py:1279
  249.6 6.1 shard_map.231
  255.8 8.4 %all-gather.9.cloned.1.call-done.gate_own.up_own = bf16[2,1536,1024]{2,1,0:T(8,128)(2,1)} async-done(((bf16[2,384,1024]{2,1,0:T(8,128)(2,1)}), bf16[2,1536,1024]{2,1,0:T(8,128)(2,1)}) %all-gather.9.cloned.1.call-update) | async-done | bytes 6291472 | tf_op jit(solution)/shard_map/all_gather | solution.py:1420
  267.5 45.3 %collective-permute-done.19.x_tokens_out.x_tokens = bf16[512,2048]{1,0:T(8,128)(2,1)S(1)} collective-permute-done((bf16[512,2048]{1,0:T(8,128)(2,1)}, bf16[512,2048]{1,0:T(8,128)(2,1)S(1)}, u32[]{:S(2)}, u32[]{:S(2)}) %collective-permute-start.19) | collective-permute-done | bytes 2097184 | tf_op jit(solution)/shard_map/ppermute | solution.py:1279
  314.1 66.2 %shard_map.232 = (bf16[2048,2048]{1,0:T(8,128)(2,1)}, bf16[2048,2048]{1,0:T(8,128)(2,1)}, bf16[2048,1536]{1,0:T(8,128)(2,1)}, bf16[2048,1536]{1,0:T(8,128)(2,1)}, bf16[2048,1536]{1,0:T(8,128)(2,1)}) custom-call(bf16[512,2048]{1,0:T(8,128)(2,1)} %copy-done.5, bf16[512,2048]{1,0:T(8,128)(2,1)} %collective-permute-done.20.y_tokens_out.y_tokens, ...), custom_call_target="tpu_custom_call" | custom-call | flops 1 | bytes 1 | tf_op jit(solution)/shard_map/pallas_call | solution.py:696
  380.4 11.3 %fusion.6 = bf16[1536,1024]{1,0:T(8,128)(2,1)} fusion(bf16[2048,1536]{1,0:T(8,128)(2,1)} %get-tuple-element.108.hidden, bf16[2048,2048]{1,0:T(8,128)(2,1)} %get-tuple-element.99.grads), kind=kOutput, calls=%fused_computation.9 | convolution fusion | flops 6444023808 | bytes 13631488 | tf_op jit(solution)/shard_map/dot_general | solution.py:77
  392.1 114.8 %shard_map.233 = (bf16[2048,1536]{1,0:T(8,128)(2,1)}, bf16[2048,1536]{1,0:T(8,128)(2,1)}, bf16[512,2048]{1,0:T(8,128)(2,1)}, bf16[512,2048]{1,0:T(8,128)(2,1)}, ...) custom-call(bf16[2048,2048]{1,0:T(8,128)(2,1)} %get-tuple-element.99.grads, bf16[2048,1536]{1,0:T(8,128)(2,1)} %get-tuple-element.108.hidden, ...), custom_call_target="tpu_custom_call" | custom-call | flops 1 | bytes 1 | tf_op jit(solution)/shard_map/pallas_call | solution.py:870
  506.9 11.8 %add_convert_fusion = bf16[1536,1024]{1,0:T(8,128)(2,1)} fusion(bf16[1536,1024]{1,0:T(8,128)(2,1)} %collective-permute-done.25, bf16[2048,1536]{1,0:T(8,128)(2,1)} %get-tuple-element.108.hidden, bf16[2048,2048]{1,0:T(8,128)(2,1)} %get-tuple-element.99.grads), kind=kOutput, calls=%fused_computation | convolution fusion | flops 6447169536 | bytes 16777216 | tf_op jit(solution)/shard_map/dot_general | solution.py:77
  518.8 10.6 %fusion.9 = bf16[1536,1024]{1,0:T(8,128)(2,1)S(1)} fusion(bf16[2048,1536]{1,0:T(8,128)(2,1)} %get-tuple-element.106, bf16[2048,2048]{1,0:T(8,128)(2,1)} %get-tuple-element.107.refs_1_), kind=kOutput, calls=%fused_computation.10 | convolution fusion | flops 6444023808 | bytes 13631488 | tf_op jit(solution)/shard_map/dot_general | solution.py:77
  529.5 5.6 collective-permute-done.24
  535.2 9.8 %add_convert_fusion.1 = bf16[1536,1024]{1,0:T(8,128)(2,1)} fusion(bf16[1536,1024]{1,0:T(8,128)(2,1)S(1)} %collective-permute-done.24, bf16[2048,1536]{1,0:T(8,128)(2,1)S(1)} %bitcast.43, bf16[2048,2048]{1,0:T(8,128)(2,1)} %get-tuple-element.107.refs_1_), kind=kOutput, calls=%fused_computation.1 | convolution fusion | flops 6447169536 | bytes 16777216 | tf_op jit(solution)/shard_map/dot_general | solution.py:77
  545.0 8.5 %shard_map.234 = (f32[512,2048]{1,0:T(8,128)}, bf16[512,2048]{1,0:T(8,128)(2,1)}, f32[8,2048]{1,0:T(8,128)}) custom-call(s32[1]{0:T(128)} %bitcast.place, f32[512,2048]{1,0:T(8,128)} %get-tuple-element.93.middle, bf16[512,2048]{1,0:T(8,128)(2,1)} %copy-done, f32[512,2048]{1,0:T(8,128)} %get-tuple-element.104.two, f32[1,2048]{1,0:T(1,128)} %bitcast.35), custom_call_target="tpu_custom_call" | custom-call | flops 1 | bytes 1 | tf_op jit(solution)/shard_map/pallas_call | solution.py:1205
  553.6 4.2 collective-permute-done.23.right_other.other
  559.2 46.0 %shard_map.235 = (bf16[1024,512]{1,0:T(8,128)(2,1)}, bf16[1536,1024]{1,0:T(8,128)(2,1)}) custom-call(bf16[1024,1024]{1,0:T(8,128)(2,1)} %get-tuple-element.85.left.left_own.left_other, bf16[1024,1024]{1,0:T(8,128)(2,1)} %get-tuple-element.85.left.left_own.left_other, bf16[512,2048]{1,0:T(8,128)(2,1)} %get-tuple-element.105.right_own.own, ...), custom_call_target="tpu_custom_call" | custom-call | flops 1 | bytes 1 | tf_op jit(solution)/shard_map/pallas_call | solution.py:1103
  608.1 40.2 %shard_map.236 = (bf16[1024,2048]{1,0:T(8,128)(2,1)}, f32[16,128]{1,0:T(8,128)}) custom-call(s32[1]{0:T(128)} %bitcast.11.core, bf16[512,2048]{1,0:T(8,128)(2,1)} %get-tuple-element.105.right_own.own, bf16[512,2048]{1,0:T(8,128)(2,1)} %copy-done.7, bf16[1024,512]{1,0:T(8,128)(2,1)} %all-gather.7.cloned.1.call-done.w0.o0, bf16[1024,512]{1,0:T(8,128)(2,1)} %copy-done.8, ...), custom_call_target="tpu_custom_call" | custom-call | flops 1 | bytes 1 | tf_op jit(solution)/shard_map/pallas_call | solution.py:542
  648.2 5.0 collective-permute-done.26.over_x
  655.2 5.9 shard_map.237.refs_5_
  661.2 80.7 %shard_map.238 = (bf16[512,2048]{1,0:T(8,128)(2,1)}, f32[512,2048]{1,0:T(8,128)}, bf16[512,2048]{1,0:T(8,128)(2,1)}, bf16[512,2048]{1,0:T(8,128)(2,1)}) custom-call(bf16[512,2048]{1,0:T(8,128)(2,1)} %shard_map.228.own.left_own, bf16[512,2048]{1,0:T(8,128)(2,1)} %copy-done.6, bf16[1024,2048]{1,0:T(8,128)(2,1)} %get-tuple-element.121.right_own.right_other, ...), custom_call_target="tpu_custom_call" | custom-call | flops 1 | bytes 1 | tf_op jit(solution)/shard_map/pallas_call | solution.py:1103
  750.4 4.3 collective-permute-done.43
  759.2 9.2 %shard_map.239 = (f32[512,2048]{1,0:T(8,128)}, bf16[512,2048]{1,0:T(8,128)(2,1)}, f32[8,2048]{1,0:T(8,128)}) custom-call(s32[1]{0:T(128)} %bitcast.place, bf16[512,2048]{1,0:T(8,128)(2,1)} %broadcast_select_fusion.1.inputs, f32[512,2048]{1,0:T(8,128)} %get-tuple-element.129.middle_grad, f32[512,2048]{1,0:T(8,128)} %get-tuple-element.130.own, ...), custom_call_target="tpu_custom_call" | custom-call | flops 1 | bytes 1 | tf_op jit(solution)/shard_map/pallas_call | solution.py:1205
  775.8 16.2 %collective-permute-done.31 = f32[4352]{0:T(1024)S(1)} collective-permute-done((f32[4352]{0:T(1024)S(1)}, f32[4352]{0:T(1024)S(1)}, u32[]{:S(2)}, u32[]{:S(2)}) %collective-permute-start.31) | collective-permute-done | bytes 17440 | tf_op jit(solution)/shard_map/ppermute | solution.py:1279
  803.2 8.0 collective-permute-start.38
  811.2 5.8 convert_select_fusion
  (212 shorter events, 101.5 us)
Async XLA Ops:
  7.2 53.6 %all-gather.5.cloned.1.call-start = ((), (), s32[]{:S(2)}) async-start(), calls=%async_computation.5 | async-start | bytes 2621440 | tf_op jit(solution)/shard_map/all_gather | solution.py:1379
  12.1 139.4 %all-gather.7.cloned.1.call-start = ((), (), s32[]{:S(2)}) async-start(), calls=%async_computation.6 | async-start | bytes 1310720 | tf_op jit(solution)/shard_map/all_gather | solution.py:1396
  13.1 18.0 %collective-permute-start.3 = (bf16[1152,256]{1,0:T(8,128)(2,1)S(1)}, bf16[1152,256]{1,0:T(8,128)(2,1)S(1)}, u32[]{:S(2)}, u32[]{:S(2)}) collective-permute-start(bf16[1152,256]{1,0:T(8,128)(2,1)S(1)} %get-tuple-element.159), channel_id=1, source_target_pairs={{0,24},{4,28},{8,16},{12,20},{16,8},{20,12},{24,0},{28,4},{1,25},{... | collective-permute-start | bytes 1769480 | tf_op jit(solution)/shard_map/ppermute | solution.py:1279
  17.0 26.2 %collective-permute-start.2 = (bf16[1152,256]{1,0:T(8,128)(2,1)S(1)}, bf16[1152,256]{1,0:T(8,128)(2,1)S(1)}, u32[]{:S(2)}, u32[]{:S(2)}) collective-permute-start(bf16[1152,256]{1,0:T(8,128)(2,1)S(1)} %get-tuple-element.160), channel_id=1, source_target_pairs={{0,16},{4,20},{8,24},{12,28},{16,0},{20,4},{24,8},{28,12},{1,17},{... | collective-permute-start | bytes 1769480 | tf_op jit(solution)/shard_map/ppermute | solution.py:1279
  17.4 26.1 %collective-permute-start.1 = (bf16[1152,256]{1,0:T(8,128)(2,1)S(1)}, bf16[1152,256]{1,0:T(8,128)(2,1)S(1)}, u32[]{:S(2)}, u32[]{:S(2)}) collective-permute-start(bf16[1152,256]{1,0:T(8,128)(2,1)S(1)} %get-tuple-element.161), channel_id=1, source_target_pairs={{0,8},{4,12},{8,0},{12,4},{16,24},{20,28},{24,16},{28,20},{1,9},{5... | collective-permute-start | bytes 1769480 | tf_op jit(solution)/shard_map/ppermute | solution.py:1279
  64.7 48.3 %collective-permute-start.8 = (bf16[512,2048]{1,0:T(8,128)(2,1)}, bf16[512,2048]{1,0:T(8,128)(2,1)S(1)}, u32[]{:S(2)}, u32[]{:S(2)}) collective-permute-start(bf16[512,2048]{1,0:T(8,128)(2,1)} %all-gather.5.cloned.1.call-done.w0.refs_0_), channel_id=1, source_target_pairs={{0,8},{4,12},{8,0},{12,4},{16,24},{20,28},{24,16},{28,20},{1,9},{5... | collective-permute-start | bytes 6291464 | tf_op jit(solution)/shard_map/ppermute | solution.py:1279
  66.2 48.6 %collective-permute-start.9 = (bf16[512,2048]{1,0:T(8,128)(2,1)}, bf16[512,2048]{1,0:T(8,128)(2,1)}, u32[]{:S(2)}, u32[]{:S(2)}) collective-permute-start(bf16[512,2048]{1,0:T(8,128)(2,1)} %all-gather.5.cloned.1.call-done.w0.refs_0_), channel_id=1, source_target_pairs={{0,16},{4,20},{8,24},{12,28},{16,0},{20,4},{24,8},{28,12},{1,17},{... | collective-permute-start | bytes 6291464 | tf_op jit(solution)/shard_map/ppermute | solution.py:1279
  114.8 149.4 %all-gather.9.cloned.1.call-start = ((), (), s32[]{:S(2)}) async-start(), calls=%async_computation.7 | async-start | bytes 7864320 | tf_op jit(solution)/shard_map/all_gather | solution.py:1420
  123.6 25.3 %collective-permute-start.10 = (bf16[256,2048]{1,0:T(8,128)(2,1)S(1)}, bf16[256,2048]{1,0:T(8,128)(2,1)}, u32[]{:S(2)}, u32[]{:S(2)}) collective-permute-start(bf16[256,2048]{1,0:T(8,128)(2,1)S(1)} %slice.104), channel_id=1, source_target_pairs={{0,16},{4,20},{8,24},{12,28},{16,0},{20,4},{24,8},{28,12},{1,17},{... | collective-permute-start | bytes 3145736 | tf_op jit(solution)/shard_map/ppermute | solution.py:1279
  126.3 25.1 %collective-permute-start.11 = (bf16[256,2048]{1,0:T(8,128)(2,1)S(1)}, bf16[256,2048]{1,0:T(8,128)(2,1)}, u32[]{:S(2)}, u32[]{:S(2)}) collective-permute-start(bf16[256,2048]{1,0:T(8,128)(2,1)S(1)} %slice.105), channel_id=1, source_target_pairs={{0,8},{4,12},{8,0},{12,4},{16,24},{20,28},{24,16},{28,20},{1,9},{5... | collective-permute-start | bytes 3145736 | tf_op jit(solution)/shard_map/ppermute | solution.py:1279
  151.4 228.9 %all-gather.11.cloned.1.call-start = ((), (), s32[]{:S(2)}) async-start(), calls=%async_computation.8 | async-start | bytes 3932160 | tf_op jit(solution)/shard_map/all_gather | solution.py:1423
  152.1 33.8 %collective-permute-start.12 = (bf16[1024,512]{1,0:T(8,128)(2,1)}, bf16[1024,512]{1,0:T(8,128)(2,1)S(1)}, u32[]{:S(2)}, u32[]{:S(2)}) collective-permute-start(bf16[1024,512]{1,0:T(8,128)(2,1)} %all-gather.7.cloned.1.call-done.w0.o0), channel_id=1, source_target_pairs={{0,8},{4,12},{8,0},{12,4},{16,24},{20,28},{24,16},{28,20},{1,9},{5... | collective-permute-start | bytes 3145736 | tf_op jit(solution)/shard_map/ppermute | solution.py:1279
  153.1 32.7 %collective-permute-start.13 = (bf16[1024,512]{1,0:T(8,128)(2,1)}, bf16[1024,512]{1,0:T(8,128)(2,1)S(1)}, u32[]{:S(2)}, u32[]{:S(2)}) collective-permute-start(bf16[1024,512]{1,0:T(8,128)(2,1)} %all-gather.7.cloned.1.call-done.w0.o0), channel_id=1, source_target_pairs={{0,16},{4,20},{8,24},{12,28},{16,0},{20,4},{24,8},{28,12},{1,17},{... | collective-permute-start | bytes 3145736 | tf_op jit(solution)/shard_map/ppermute | solution.py:1279
  187.9 57.6 %collective-permute-start.17 = (bf16[512,2048]{1,0:T(8,128)(2,1)S(1)}, bf16[512,2048]{1,0:T(8,128)(2,1)S(1)}, u32[]{:S(2)}, u32[]{:S(2)}) collective-permute-start(bf16[512,2048]{1,0:T(8,128)(2,1)S(1)} %broadcast_select_fusion.own_grads.cotangent), channel_id=1, source_target_pairs={{0,8},{4,12},{8,0},{12,4},{16,24},{20,28},{24,16},{28,20},{1,9},{5... | collective-permute-start | bytes 6291464 | tf_op jit(solution)/shard_map/ppermute | solution.py:1279
  188.9 56.6 %collective-permute-start.18 = (bf16[512,2048]{1,0:T(8,128)(2,1)S(1)}, bf16[512,2048]{1,0:T(8,128)(2,1)S(1)}, u32[]{:S(2)}, u32[]{:S(2)}) collective-permute-start(bf16[512,2048]{1,0:T(8,128)(2,1)S(1)} %broadcast_select_fusion.own_grads.cotangent), channel_id=1, source_target_pairs={{0,16},{4,20},{8,24},{12,28},{16,0},{20,4},{24,8},{28,12},{1,17},{... | collective-permute-start | bytes 6291464 | tf_op jit(solution)/shard_map/ppermute | solution.py:1279
  211.0 35.9 %collective-permute-start.16 = (bf16[512,2048]{1,0:T(8,128)(2,1)}, bf16[512,2048]{1,0:T(8,128)(2,1)S(1)}, u32[]{:S(2)}, u32[]{:S(2)}) collective-permute-start(bf16[512,2048]{1,0:T(8,128)(2,1)} %get-tuple-element.90), channel_id=1, source_target_pairs={{0,4},{4,0},{8,12},{12,8},{16,20},{20,16},{24,28},{28,24},{1,5},{5... | collective-permute-start | bytes 6291464 | tf_op jit(solution)/shard_map/ppermute | solution.py:1279
  264.2 49.9 %collective-permute-start.21 = (bf16[2,1536,1024]{2,1,0:T(8,128)(2,1)}, bf16[2,1536,1024]{2,1,0:T(8,128)(2,1)}, u32[]{:S(2)}, u32[]{:S(2)}) collective-permute-start(bf16[2,1536,1024]{2,1,0:T(8,128)(2,1)} %all-gather.9.cloned.1.call-done.gate_own.up_own), channel_id=1, source_target_pairs={{0,4},{4,0},{8,12},{12,8},{16,20},{20,16},{24,28},{28,24},{1,5},{5... | collective-permute-start | bytes 18874376 | tf_op jit(solution)/shard_map/ppermute | solution.py:1279
  264.3 396.8 %reduce-scatter.6.cloned.1.call-start = ((), (), s32[]{:S(2)}) async-start(), calls=%async_computation.9 | async-start | bytes 3932160 | tf_op jit(solution)/shard_map/reduce_scatter | solution.py:1461
  264.5 48.3 %collective-permute-start.19 = (bf16[512,2048]{1,0:T(8,128)(2,1)}, bf16[512,2048]{1,0:T(8,128)(2,1)S(1)}, u32[]{:S(2)}, u32[]{:S(2)}) collective-permute-start(bf16[512,2048]{1,0:T(8,128)(2,1)} %get-tuple-element.94.own_tokens), channel_id=1, source_target_pairs={{0,8},{4,12},{8,0},{12,4},{16,24},{20,28},{24,16},{28,20},{1,9},{5... | collective-permute-start | bytes 6291464 | tf_op jit(solution)/shard_map/ppermute | solution.py:1279
  266.1 48.0 %collective-permute-start.20 = (bf16[512,2048]{1,0:T(8,128)(2,1)}, bf16[512,2048]{1,0:T(8,128)(2,1)}, u32[]{:S(2)}, u32[]{:S(2)}) collective-permute-start(bf16[512,2048]{1,0:T(8,128)(2,1)} %get-tuple-element.94.own_tokens), channel_id=1, source_target_pairs={{0,16},{4,20},{8,24},{12,28},{16,0},{20,4},{24,8},{28,12},{1,17},{... | collective-permute-start | bytes 6291464 | tf_op jit(solution)/shard_map/ppermute | solution.py:1279
  391.7 115.3 %collective-permute-start.25 = (bf16[1536,1024]{1,0:T(8,128)(2,1)}, bf16[1536,1024]{1,0:T(8,128)(2,1)}, u32[]{:S(2)}, u32[]{:S(2)}) collective-permute-start(bf16[1536,1024]{1,0:T(8,128)(2,1)} %fusion.6), channel_id=1, source_target_pairs={{0,4},{4,0},{8,12},{12,8},{16,20},{20,16},{24,28},{28,24},{1,5},{5... | collective-permute-start | bytes 9437192 | tf_op jit(solution)/shard_map/ppermute | solution.py:1279
  518.8 142.4 %reduce-scatter.8.cloned.1.call-start = ((), (), s32[]{:S(2)}) async-start(), calls=%async_computation.10 | async-start | bytes 3932160 | tf_op jit(solution)/shard_map/reduce_scatter | solution.py:1461
  545.0 196.9 %reduce-scatter.12.cloned.1.call-start = ((), (), s32[]{:S(2)}) async-start(), calls=%async_computation.12 | async-start | bytes 1310720 | tf_op jit(solution)/shard_map/reduce_scatter | solution.py:1461
  605.2 136.9 %reduce-scatter.10.cloned.1.call-start = ((), (), s32[]{:S(2)}) async-start(), calls=%async_computation.11 | async-start | bytes 3932160 | tf_op jit(solution)/shard_map/reduce_scatter | solution.py:1461
  605.9 194.0 %reduce-scatter.14.cloned.1.call-start = ((), (), s32[]{:S(2)}) async-start(), calls=%async_computation.13 | async-start | bytes 2621440 | tf_op jit(solution)/shard_map/reduce_scatter | solution.py:1550
  606.0 47.3 %collective-permute-start.26 = (bf16[512,2048]{1,0:T(8,128)(2,1)}, bf16[512,2048]{1,0:T(8,128)(2,1)S(1)}, u32[]{:S(2)}, u32[]{:S(2)}) collective-permute-start(bf16[512,2048]{1,0:T(8,128)(2,1)} %get-tuple-element.123), channel_id=1, source_target_pairs={{0,8},{4,12},{8,0},{12,4},{16,24},{20,28},{24,16},{28,20},{1,9},{5... | collective-permute-start | bytes 6291464 | tf_op jit(solution)/shard_map/ppermute | solution.py:1279
  606.7 47.0 %collective-permute-start.27 = (bf16[512,2048]{1,0:T(8,128)(2,1)S(1)}, bf16[512,2048]{1,0:T(8,128)(2,1)S(1)}, u32[]{:S(2)}, u32[]{:S(2)}) collective-permute-start(bf16[512,2048]{1,0:T(8,128)(2,1)S(1)} %copy-done.24), channel_id=1, source_target_pairs={{0,16},{4,20},{8,24},{12,28},{16,0},{20,4},{24,8},{28,12},{1,17},{... | collective-permute-start | bytes 6291464 | tf_op jit(solution)/shard_map/ppermute | solution.py:1279
  768.4 34.4 %collective-permute-start.29 = (bf16[512,2048]{1,0:T(8,128)(2,1)}, bf16[512,2048]{1,0:T(8,128)(2,1)}, u32[]{:S(2)}, u32[]{:S(2)}) collective-permute-start(bf16[512,2048]{1,0:T(8,128)(2,1)} %get-tuple-element.132), channel_id=1, source_target_pairs={{1,4},{3,6},{4,1},{6,3},{9,12},{11,14},{12,9},{14,11},{17,20},{19,... | collective-permute-start | bytes 6291464 | tf_op jit(solution)/shard_map/ppermute | solution.py:1288
  771.5 24.4 %collective-permute-start.35 = (bf16[768,256]{1,0:T(8,128)(2,1)S(1)}, bf16[768,256]{1,0:T(8,128)(2,1)S(1)}, u32[]{:S(2)}, u32[]{:S(2)}) collective-permute-start(bf16[768,256]{1,0:T(8,128)(2,1)S(1)} %get-tuple-element.165), channel_id=1, source_target_pairs={{0,24},{4,28},{8,16},{12,20},{16,8},{20,12},{24,0},{28,4},{1,25},{... | collective-permute-start | bytes 1179656 | tf_op jit(solution)/shard_map/ppermute | solution.py:1279
  772.7 23.1 %collective-permute-start.34 = (bf16[768,256]{1,0:T(8,128)(2,1)S(1)}, bf16[768,256]{1,0:T(8,128)(2,1)S(1)}, u32[]{:S(2)}, u32[]{:S(2)}) collective-permute-start(bf16[768,256]{1,0:T(8,128)(2,1)S(1)} %get-tuple-element.166), channel_id=1, source_target_pairs={{0,16},{4,20},{8,24},{12,28},{16,0},{20,4},{24,8},{28,12},{1,17},{... | collective-permute-start | bytes 1179656 | tf_op jit(solution)/shard_map/ppermute | solution.py:1279
  773.6 22.2 %collective-permute-start.33 = (bf16[768,256]{1,0:T(8,128)(2,1)S(1)}, bf16[768,256]{1,0:T(8,128)(2,1)S(1)}, u32[]{:S(2)}, u32[]{:S(2)}) collective-permute-start(bf16[768,256]{1,0:T(8,128)(2,1)S(1)} %get-tuple-element.167), channel_id=1, source_target_pairs={{0,8},{4,12},{8,0},{12,4},{16,24},{20,28},{24,16},{28,20},{1,9},{5... | collective-permute-start | bytes 1179656 | tf_op jit(solution)/shard_map/ppermute | solution.py:1279
  800.9 17.2 %collective-permute-start.39 = (bf16[256,512]{1,0:T(8,128)(2,1)S(1)}, bf16[256,512]{1,0:T(8,128)(2,1)S(1)}, u32[]{:S(2)}, u32[]{:S(2)}) collective-permute-start(bf16[256,512]{1,0:T(8,128)(2,1)S(1)} %constant_dynamic-slice_fusion.7), channel_id=1, source_target_pairs={{0,4},{4,0},{8,12},{12,8},{16,20},{20,16},{24,28},{28,24},{1,5},{5... | collective-permute-start | bytes 786440 | tf_op jit(solution)/shard_map/ppermute | solution.py:1279
  (48 other events, 482.5 us)
Sparse Core Ops, SparseCore 0:
  12.2 48.5 all-gather.4
  115.0 25.6 all-gather.6
  151.6 112.6 all-gather.8
  265.7 61.6 all-gather.10
  518.9 57.6 reduce-scatter.5
  578.7 60.2 reduce-scatter.7
  641.3 27.1 reduce-scatter.11
  670.9 71.1 reduce-scatter.9
  744.5 49.7 reduce-scatter.13

commit v5 on v4

--- a/solution.py
+++ b/solution.py
@@ -686,7 +686,7 @@
 
 def gather_hidden(tokens, grads, weights):
     rows, width = tokens[0].shape
-    _, hidden_count, half = weights[0].shape
+    hidden_count, half = weights[0].shape
     chunk = 512
     spec = pl.BlockSpec
     shape = jax.ShapeDtypeStruct
@@ -697,7 +697,7 @@
         hidden_kernel,
         grid=(4, hidden_count // chunk),
         in_specs=[outside] * 4 + [whole] * 6
-        + [spec((None, chunk, half), lambda b, c, n=n: (n, c, 0)) for n in (0, 0, 1, 1)],
+        + [spec((chunk, half), lambda b, c: (c, 0))] * 4,
         out_specs=[spec((rows, width), lambda b, c: (b, 0))] * 2
         + [spec((rows, chunk), lambda b, c: (b, c))] * 3,
         out_shape=[shape((4 * rows, width), bf16)] * 2 + [shape((4 * rows, hidden_count), bf16)] * 3,
@@ -707,7 +707,7 @@
             collective_id=1, has_side_effects=True, vmem_limit_bytes=60 * 2**20
         ),
         cost_estimate=pl.CostEstimate(flops=1, bytes_accessed=1, transcendentals=0),
-    )(*tokens[1:], *grads[1:], *tokens, *grads, *weights, *weights)
+    )(*tokens[1:], *grads[1:], *tokens, *grads, *weights)
 
 
 def reduce_copies(corner, send_x, send_y, got_corner, got_x, got_y, send, receive):
@@ -860,7 +860,7 @@
 
 def feed_back(grads, saved, weights, down):
     rows, width = grads.shape[0] // 4, grads.shape[1]
-    _, hidden_count, half = weights[0].shape
+    hidden_count, half = weights[0].shape
     chunk = 512
     spec = pl.BlockSpec
     shape = jax.ShapeDtypeStruct
@@ -872,8 +872,7 @@
         grid=(4, hidden_count // chunk),
         in_specs=[spec((rows, width), block)]
         + [spec((rows, chunk), piece)] * 3
-        + [spec((None, chunk, half), lambda q, c, n=n: (n, c, 0)) for n in (0, 0, 1, 1)]
-        + [spec((chunk, half), lambda q, c: (c, 0))] * 2,
+        + [spec((chunk, half), lambda q, c: (c, 0))] * 6,
         out_specs=[spec((rows, chunk), piece)] * 2
         + [spec(memory_space=pl.ANY)] * 3
         + [spec((rows, width), lambda q, c: (0, 0))],
@@ -889,7 +888,7 @@
             collective_id=2, has_side_effects=True, vmem_limit_bytes=62 * 2**20
         ),
         cost_estimate=pl.CostEstimate(flops=1, bytes_accessed=1, transcendentals=0),
-    )(grads, *saved, *weights, *weights, *down)
+    )(grads, *saved, *weights, *down)
 
 
 def is_crossing():
@@ -1388,8 +1387,8 @@
         [piece_for(0)] + [exchange(piece_for(k), 2 * k) for k in (1, 2, 3)], 1
     )
 
-    gate_up_own, down_part = feed_own[: 2 * units], feed_own[2 * units :]
-    qkv_z = after(qkv_z, (gate_up_own, down_part))
+    feed_parts = [feed_own[n * units : (n + 1) * units] for n in range(3)]
+    qkv_z = after(qkv_z, feed_parts)
     qkv_near = gather_near(qkv_z)
     moved = swap_halves(after(layer_input, qkv_z))
     moved_grad = swap_halves(after(out_grad, qkv_z))
@@ -1416,11 +1415,11 @@
         *gather_far(after(qkv_near, (normed, cosines, sines, cotangent))),
     ]
     out_near = gather_near(after(out_z, qkv_chips))
-    gate_up_own, down_part = after((gate_up_own, down_part), (out_z, qkv_chips))
-    gate_up_half = lax.all_gather(
-        gate_up_own.reshape(2, units, width // 2), "mp", axis=1, tiled=True
-    )
-    down_half = lax.all_gather(down_part, "mp", axis=0, tiled=True)
+    feed_parts = after(feed_parts, (out_z, qkv_chips))
+    gate_half, up_half = [
+        lax.all_gather(part, "mp", axis=0, tiled=True) for part in feed_parts[:2]
+    ]
+    down_half = lax.all_gather(feed_parts[2], "mp", axis=0, tiled=True)
     normed_other = after(exchange(normed, 1), out_z)
     proj, query_rot, key_rot, value_low, attended, log_total = attend(
         core_index,
@@ -1450,7 +1449,12 @@
     )
 
     tokens_near = gather_near(tokens)
-    gate_up_w = [gate_up_half, exchange(after(gate_up_half, tokens), 1)]
+    gate_up_w = [
+        gate_half,
+        exchange(after(gate_half, tokens), 1),
+        up_half,
+        exchange(after(up_half, tokens_near), 1),
+    ]
     all_tokens, all_grads, all_hidden, gate_slope, up_slope = gather_hidden(
         [tokens, *tokens_near], [cotangent, *grads_near], gate_up_w
     )
@@ -1578,13 +1582,14 @@
                 jnp.sum(head_gains[8:], 0),
                 jnp.sum(gain_two_part, 0),
             ]
-        ), qkv_local)
-    )
-    grad_moved = swap_halves(rounded_grad)
-    gain_sums = total_z(after(gain_sums, (gate_own, up_own, grad_moved)))
+        ), (qkv_local, gate_own, up_own))
+    )
     pair_rows = qkv_sum.shape[0] // 2
     qkv_other = exchange(pick(qkv_sum, 1 - core, pair_rows, 0), 1)
     qkv_own = pick(qkv_sum, core, pair_rows, 0)
+
+    grad_moved = after(swap_halves(rounded_grad), qkv_other)
+    gain_sums = total_z(after(gain_sums, grad_moved))
 
     def both(start, stop):
         return in_order(qkv_own[:, start:stop], qkv_other[:, start:stop], core, 1).astype(f32)

time: 834 us -> 828 us (level)
    ppermute x38 -> x39, waiting for transfers between devices: 229 us -> 208 us  [exchange(): return lax.ppermute(values, 'dp', [(i, i ^ bit) for i in range(8)])]
    all_gather x2 -> x3, waiting for transfers between devices: 8.47 us -> 22.1 us  [the longest x2 22 us: fast(): lax.all_gather(part, 'mp', axis=0, tiled=True)]
    ppermute x38 -> x39, starting transfers between devices: 35.8 us -> 31.5 us  [exchange(): return lax.ppermute(values, 'dp', [(i, i ^ bit) for i in range(8)])]
  transfers between devices with their start and end apart: 53 -> 55, of which waited for: 25 -> 27; matrix products, arithmetic and copies ran while one was open for 8% -> 9% of each run, Pallas kernels for 50% -> 51%
where the time goes in v5:
time: 828 us; the launch traced here: 822 us
  Pallas kernels  419 us (51%)
  waiting for transfers between devices  247 us (30%)
  starting transfers between devices  47.2 us (6%)
  matrix products  43.4 us (5%)
  other arithmetic  27.1 us (3%)
  local copies, waits for them, and re-layouts  23.3 us (3%)
  between operations  15.1 us (2%)
    ppermute x39, waiting for transfers between devices, exchange(): return lax.ppermute(values, 'dp', [(i, i ^ bit) for i in range(8)])  208 us
    pallas_call x2, Pallas kernels, outer(): pl.pallas_call(functools.partial(outer_kernel, len(weights), more), grid=...  127 us
    pallas_call x1, Pallas kernels, feed_back(): pl.pallas_call(feed_back_kernel, grid=(4, hidden_count // chunk), in_spec...  115 us
    pallas_call x1, Pallas kernels, gather_hidden(): pl.pallas_call(hidden_kernel, grid=(4, hidden_count // chunk), in_specs=[...  65.5 us
    dot_general x4, matrix products, dot_first(): lax.dot_general(left, right, (((0,), (0,)), ((), ())), preferred_element_...  43.4 us
    pallas_call x1, Pallas kernels, attend_back(): pl.pallas_call(attend_back_kernel, grid_spec=pltpu.PrefetchScalarGridSpec...  40.2 us
    pallas_call x5, Pallas kernels, tile_call(): pl.pallas_call(kernel, grid_spec=pltpu.PrefetchScalarGridSpec(num_scalar_...  34.2 us
    ppermute x39, starting transfers between devices, exchange(): return lax.ppermute(values, 'dp', [(i, i ^ bit) for i in range(8)])  31.5 us
  transfers between devices with their start and end apart: 55, of which 27 were waited for; matrix products, arithmetic and copies ran while one was open for 9% of the time, Pallas kernels for 51%

profile of v5, /device:TPU:0, one launch (start us, length us, event | category | flops | bytes accessed | tf_op | source)
XLA Modules:
  0.0 821.9 jit_solution(13876045897758629469)
XLA Ops:
  17.6 13.5 %collective-permute-done.3 = bf16[1152,256]{1,0:T(8,128)(2,1)S(1)} collective-permute-done((bf16[1152,256]{1,0:T(8,128)(2,1)S(1)}, bf16[1152,256]{1,0:T(8,128)(2,1)S(1)}, u32[]{:S(2)}, u32[]{:S(2)}) %collective-permute-start.3) | collective-permute-done | bytes 589856 | tf_op jit(solution)/shard_map/ppermute | solution.py:1278
  31.1 12.1 %collective-permute-done.2 = bf16[1152,256]{1,0:T(8,128)(2,1)S(1)} collective-permute-done((bf16[1152,256]{1,0:T(8,128)(2,1)S(1)}, bf16[1152,256]{1,0:T(8,128)(2,1)S(1)}, u32[]{:S(2)}, u32[]{:S(2)}) %collective-permute-start.2) | collective-permute-done | bytes 589856 | tf_op jit(solution)/shard_map/ppermute | solution.py:1278
  45.3 15.4 %all-gather.6.cloned.1.call-done.w0.refs_0_ = bf16[512,2048]{1,0:T(8,128)(2,1)} async-done(((bf16[512,512]{1,0:T(8,128)(2,1)}), bf16[512,2048]{1,0:T(8,128)(2,1)}) %all-gather.6.cloned.1.call-update) | async-done | bytes 2097168 | tf_op jit(solution)/shard_map/all_gather | solution.py:1378
  72.8 40.3 %collective-permute-done.8.w1.refs_1_ = bf16[512,2048]{1,0:T(8,128)(2,1)S(1)} collective-permute-done((bf16[512,2048]{1,0:T(8,128)(2,1)}, bf16[512,2048]{1,0:T(8,128)(2,1)S(1)}, u32[]{:S(2)}, u32[]{:S(2)}) %collective-permute-start.8) | collective-permute-done | bytes 2097184 | tf_op jit(solution)/shard_map/ppermute | solution.py:1278
  127.1 21.8 %collective-permute-done.10.w3_low.refs_3_ = bf16[256,2048]{1,0:T(8,128)(2,1)} collective-permute-done((bf16[256,2048]{1,0:T(8,128)(2,1)S(1)}, bf16[256,2048]{1,0:T(8,128)(2,1)}, u32[]{:S(2)}, u32[]{:S(2)}) %collective-permute-start.10) | collective-permute-done | bytes 1048608 | tf_op jit(solution)/shard_map/ppermute | solution.py:1278
  156.1 27.9 %shard_map.229 = (f32[1024,2048]{1,0:T(8,128)}, bf16[1024,1024]{1,0:T(8,128)(2,1)}, bf16[1024,512]{1,0:T(8,128)(2,1)}, bf16[1024,512]{1,0:T(8,128)(2,1)}, bf16[1...) custom-call(s32[1]{0:T(128)} %bitcast.11.core, bf16[512,2048]{1,0:T(8,128)(2,1)} %shard_map.228.own.left_own, ...), custom_call_target="tpu_custom_call" | custom-call | flops 1 | bytes 1 | tf_op jit(solution)/shard_map/pallas_call | solution.py:419
  188.3 10.6 %collective-permute-done.14.w3_low.o3_low = bf16[512,512]{1,0:T(8,128)(2,1)S(1)} collective-permute-done((bf16[512,512]{1,0:T(8,128)(2,1)S(1)}, bf16[512,512]{1,0:T(8,128)(2,1)S(1)}, u32[]{:S(2)}, u32[]{:S(2)}) %collective-permute-start.14) | collective-permute-done | bytes 524320 | tf_op jit(solution)/shard_map/ppermute | solution.py:1278
  199.9 9.2 %shard_map.230 = (f32[512,2048]{1,0:T(8,128)}, bf16[512,2048]{1,0:T(8,128)(2,1)}) custom-call(s32[1]{0:T(128)} %bitcast.place, bf16[1024,1024]{1,0:T(8,128)(2,1)} %get-tuple-element.88.left.left_own.left_other, bf16[1024,512]{1,0:T(8,128)(2,1)} %all-gather.8.cloned.1.call-done.w0.o0, bf16[1024,512]{1,0:T(8,128)(2,1)} %copy-done.7, ...), custom_call_target="tpu_custom_call" | custom-call | flops 1 | bytes 1 | tf_op jit(solution)/shard_map/pallas_call | solution.py:1179
  209.0 34.9 %collective-permute-done.17.x_grads_out.x_grads = bf16[512,2048]{1,0:T(8,128)(2,1)S(1)} collective-permute-done((bf16[512,2048]{1,0:T(8,128)(2,1)S(1)}, bf16[512,2048]{1,0:T(8,128)(2,1)S(1)}, u32[]{:S(2)}, u32[]{:S(2)}) %collective-permute-start.17) | collective-permute-done | bytes 2097184 | tf_op jit(solution)/shard_map/ppermute | solution.py:1278
  244.0 7.6 shard_map.231
  254.0 22.0 %all-gather.12.cloned.1.call-done.up_own = bf16[1536,1024]{1,0:T(8,128)(2,1)} async-done(((bf16[384,1024]{1,0:T(8,128)(2,1)}), bf16[1536,1024]{1,0:T(8,128)(2,1)}) %all-gather.12.cloned.1.call-update) | async-done | bytes 3145744 | tf_op jit(solution)/shard_map/all_gather | solution.py:1420
  276.0 22.9 %collective-permute-done.19.x_tokens_out.x_tokens = bf16[512,2048]{1,0:T(8,128)(2,1)} collective-permute-done((bf16[512,2048]{1,0:T(8,128)(2,1)}, bf16[512,2048]{1,0:T(8,128)(2,1)}, u32[]{:S(2)}, u32[]{:S(2)}) %collective-permute-start.19) | collective-permute-done | bytes 2097184 | tf_op jit(solution)/shard_map/ppermute | solution.py:1278
  299.5 6.0 collective-permute-done.22.up_other
  305.5 65.5 %shard_map.232 = (bf16[2048,2048]{1,0:T(8,128)(2,1)}, bf16[2048,2048]{1,0:T(8,128)(2,1)}, bf16[2048,1536]{1,0:T(8,128)(2,1)}, bf16[2048,1536]{1,0:T(8,128)(2,1)}, bf16[2048,1536]{1,0:T(8,128)(2,1)}) custom-call(bf16[512,2048]{1,0:T(8,128)(2,1)} %collective-permute-done.19.x_tokens_out.x_tokens, ...), custom_call_target="tpu_custom_call" | custom-call | flops 1 | bytes 1 | tf_op jit(solution)/shard_map/pallas_call | solution.py:696
  371.2 11.3 %fusion.6 = bf16[1536,1024]{1,0:T(8,128)(2,1)} fusion(bf16[2048,1536]{1,0:T(8,128)(2,1)} %get-tuple-element.113.hidden, bf16[2048,2048]{1,0:T(8,128)(2,1)} %get-tuple-element.104.grads), kind=kOutput, calls=%fused_computation.9 | convolution fusion | flops 6444023808 | bytes 13631488 | tf_op jit(solution)/shard_map/dot_general | solution.py:77
  382.9 114.7 %shard_map.233 = (bf16[2048,1536]{1,0:T(8,128)(2,1)}, bf16[2048,1536]{1,0:T(8,128)(2,1)}, bf16[512,2048]{1,0:T(8,128)(2,1)}, bf16[512,2048]{1,0:T(8,128)(2,1)}, ...) custom-call(bf16[2048,2048]{1,0:T(8,128)(2,1)} %get-tuple-element.104.grads, ...), custom_call_target="tpu_custom_call" | custom-call | flops 1 | bytes 1 | tf_op jit(solution)/shard_map/pallas_call | solution.py:870
  497.7 11.9 %add_convert_fusion = bf16[1536,1024]{1,0:T(8,128)(2,1)} fusion(bf16[1536,1024]{1,0:T(8,128)(2,1)} %collective-permute-done.26, bf16[2048,1536]{1,0:T(8,128)(2,1)} %get-tuple-element.113.hidden, bf16[2048,2048]{1,0:T(8,128)(2,1)} %get-tuple-element.104.grads), kind=kOutput, calls=%fused_computation | convolution fusion | flops 6447169536 | bytes 16777216 | tf_op jit(solution)/shard_map/dot_general | solution.py:77
  509.6 10.5 %fusion.9 = bf16[1536,1024]{1,0:T(8,128)(2,1)S(1)} fusion(bf16[2048,1536]{1,0:T(8,128)(2,1)} %get-tuple-element.111, bf16[2048,2048]{1,0:T(8,128)(2,1)} %get-tuple-element.112.refs_1_), kind=kOutput, calls=%fused_computation.10 | convolution fusion | flops 6444023808 | bytes 13631488 | tf_op jit(solution)/shard_map/dot_general | solution.py:77
  520.2 5.6 collective-permute-done.25
  525.9 9.8 %add_convert_fusion.1 = bf16[1536,1024]{1,0:T(8,128)(2,1)} fusion(bf16[1536,1024]{1,0:T(8,128)(2,1)S(1)} %collective-permute-done.25, bf16[2048,1536]{1,0:T(8,128)(2,1)S(1)} %bitcast.41, bf16[2048,2048]{1,0:T(8,128)(2,1)} %get-tuple-element.112.refs_1_), kind=kOutput, calls=%fused_computation.1 | convolution fusion | flops 6447169536 | bytes 16777216 | tf_op jit(solution)/shard_map/dot_general | solution.py:77
  535.8 8.3 %shard_map.234 = (f32[512,2048]{1,0:T(8,128)}, bf16[512,2048]{1,0:T(8,128)(2,1)}, f32[8,2048]{1,0:T(8,128)}) custom-call(s32[1]{0:T(128)} %bitcast.place, f32[512,2048]{1,0:T(8,128)} %get-tuple-element.96.middle, bf16[512,2048]{1,0:T(8,128)(2,1)} %copy-done, f32[512,2048]{1,0:T(8,128)} %get-tuple-element.109.two, f32[1,2048]{1,0:T(1,128)} %bitcast.33), custom_call_target="tpu_custom_call" | custom-call | flops 1 | bytes 1 | tf_op jit(solution)/shard_map/pallas_call | solution.py:1204
  544.2 4.2 collective-permute-done.24.right_other.other
  549.8 46.1 %shard_map.235 = (bf16[1024,512]{1,0:T(8,128)(2,1)}, bf16[1536,1024]{1,0:T(8,128)(2,1)}) custom-call(bf16[1024,1024]{1,0:T(8,128)(2,1)} %get-tuple-element.88.left.left_own.left_other, bf16[1024,1024]{1,0:T(8,128)(2,1)} %get-tuple-element.88.left.left_own.left_other, bf16[512,2048]{1,0:T(8,128)(2,1)} %get-tuple-element.110.right_own.own, ...), custom_call_target="tpu_custom_call" | custom-call | flops 1 | bytes 1 | tf_op jit(solution)/shard_map/pallas_call | solution.py:1102
  598.8 40.2 %shard_map.236 = (bf16[1024,2048]{1,0:T(8,128)(2,1)}, f32[16,128]{1,0:T(8,128)}) custom-call(s32[1]{0:T(128)} %bitcast.11.core, bf16[512,2048]{1,0:T(8,128)(2,1)} %get-tuple-element.110.right_own.own, bf16[512,2048]{1,0:T(8,128)(2,1)} %copy-done.6, bf16[1024,512]{1,0:T(8,128)(2,1)} %all-gather.8.cloned.1.call-done.w0.o0, bf16[1024,512]{1,0:T(8,128)(2,1)} %copy-done.7, ...), custom_call_target="tpu_custom_call" | custom-call | flops 1 | bytes 1 | tf_op jit(solution)/shard_map/pallas_call | solution.py:542
  638.9 4.9 collective-permute-done.27.over_x
  645.9 5.9 shard_map.237.refs_5_
  651.9 80.8 %shard_map.238 = (bf16[512,2048]{1,0:T(8,128)(2,1)}, f32[512,2048]{1,0:T(8,128)}, bf16[512,2048]{1,0:T(8,128)(2,1)}, bf16[512,2048]{1,0:T(8,128)(2,1)}) custom-call(bf16[512,2048]{1,0:T(8,128)(2,1)} %shard_map.228.own.left_own, bf16[512,2048]{1,0:T(8,128)(2,1)} %collective-permute-done.5.other.left_other, ...), custom_call_target="tpu_custom_call" | custom-call | flops 1 | bytes 1 | tf_op jit(solution)/shard_map/pallas_call | solution.py:1102
  739.8 9.3 %shard_map.239 = (f32[512,2048]{1,0:T(8,128)}, bf16[512,2048]{1,0:T(8,128)(2,1)}, f32[8,2048]{1,0:T(8,128)}) custom-call(s32[1]{0:T(128)} %bitcast.place, bf16[512,2048]{1,0:T(8,128)(2,1)} %broadcast_select_fusion.1.inputs, f32[512,2048]{1,0:T(8,128)} %get-tuple-element.134.middle_grad, f32[512,2048]{1,0:T(8,128)} %get-tuple-element.135.own, ...), custom_call_target="tpu_custom_call" | custom-call | flops 1 | bytes 1 | tf_op jit(solution)/shard_map/pallas_call | solution.py:1204
  757.5 5.6 collective-permute-done.34
  763.0 7.6 collective-permute-done.33
  793.6 8.6 %collective-permute-start.40 = (f32[4352]{0:T(1024)S(1)}, f32[4352]{0:T(1024)S(1)}, u32[]{:S(2)}, u32[]{:S(2)}) collective-permute-start(f32[4352]{0:T(1024)S(1)} %add.102), channel_id=1, source_target_pairs={{0,3},{1,2},{2,1},{3,0},{4,7},{5,6},{6,5},{7,4},{8,11},{9,10},{10,... | collective-permute-start | bytes 52232 | tf_op jit(solution)/shard_map/ppermute | solution.py:1326
  802.2 5.8 convert_select_fusion
  (216 shorter events, 106.1 us)
Async XLA Ops:
  7.2 53.6 %all-gather.6.cloned.1.call-start = ((), (), s32[]{:S(2)}) async-start(), calls=%async_computation.5 | async-start | bytes 2621440 | tf_op jit(solution)/shard_map/all_gather | solution.py:1378
  12.1 139.4 %all-gather.8.cloned.1.call-start = ((), (), s32[]{:S(2)}) async-start(), calls=%async_computation.6 | async-start | bytes 1310720 | tf_op jit(solution)/shard_map/all_gather | solution.py:1395
  17.0 26.2 %collective-permute-start.2 = (bf16[1152,256]{1,0:T(8,128)(2,1)S(1)}, bf16[1152,256]{1,0:T(8,128)(2,1)S(1)}, u32[]{:S(2)}, u32[]{:S(2)}) collective-permute-start(bf16[1152,256]{1,0:T(8,128)(2,1)S(1)} %get-tuple-element.169), channel_id=1, source_target_pairs={{0,16},{4,20},{8,24},{12,28},{16,0},{20,4},{24,8},{28,12},{1,17},{... | collective-permute-start | bytes 1769480 | tf_op jit(solution)/shard_map/ppermute | solution.py:1278
  17.4 26.1 %collective-permute-start.1 = (bf16[1152,256]{1,0:T(8,128)(2,1)S(1)}, bf16[1152,256]{1,0:T(8,128)(2,1)S(1)}, u32[]{:S(2)}, u32[]{:S(2)}) collective-permute-start(bf16[1152,256]{1,0:T(8,128)(2,1)S(1)} %get-tuple-element.170), channel_id=1, source_target_pairs={{0,8},{4,12},{8,0},{12,4},{16,24},{20,28},{24,16},{28,20},{1,9},{5... | collective-permute-start | bytes 1769480 | tf_op jit(solution)/shard_map/ppermute | solution.py:1278
  64.7 48.3 %collective-permute-start.8 = (bf16[512,2048]{1,0:T(8,128)(2,1)}, bf16[512,2048]{1,0:T(8,128)(2,1)S(1)}, u32[]{:S(2)}, u32[]{:S(2)}) collective-permute-start(bf16[512,2048]{1,0:T(8,128)(2,1)} %all-gather.6.cloned.1.call-done.w0.refs_0_), channel_id=1, source_target_pairs={{0,8},{4,12},{8,0},{12,4},{16,24},{20,28},{24,16},{28,20},{1,9},{5... | collective-permute-start | bytes 6291464 | tf_op jit(solution)/shard_map/ppermute | solution.py:1278
  66.2 48.6 %collective-permute-start.9 = (bf16[512,2048]{1,0:T(8,128)(2,1)}, bf16[512,2048]{1,0:T(8,128)(2,1)}, u32[]{:S(2)}, u32[]{:S(2)}) collective-permute-start(bf16[512,2048]{1,0:T(8,128)(2,1)} %all-gather.6.cloned.1.call-done.w0.refs_0_), channel_id=1, source_target_pairs={{0,16},{4,20},{8,24},{12,28},{16,0},{20,4},{24,8},{28,12},{1,17},{... | collective-permute-start | bytes 6291464 | tf_op jit(solution)/shard_map/ppermute | solution.py:1278
  114.8 139.1 %all-gather.10.cloned.1.call-start = ((), (), s32[]{:S(2)}) async-start(), calls=%async_computation.7 | async-start | bytes 3932160 | tf_op jit(solution)/shard_map/all_gather | solution.py:1420
  123.6 25.3 %collective-permute-start.10 = (bf16[256,2048]{1,0:T(8,128)(2,1)S(1)}, bf16[256,2048]{1,0:T(8,128)(2,1)}, u32[]{:S(2)}, u32[]{:S(2)}) collective-permute-start(bf16[256,2048]{1,0:T(8,128)(2,1)S(1)} %slice.108), channel_id=1, source_target_pairs={{0,16},{4,20},{8,24},{12,28},{16,0},{20,4},{24,8},{28,12},{1,17},{... | collective-permute-start | bytes 3145736 | tf_op jit(solution)/shard_map/ppermute | solution.py:1278
  126.4 25.1 %collective-permute-start.11 = (bf16[256,2048]{1,0:T(8,128)(2,1)S(1)}, bf16[256,2048]{1,0:T(8,128)(2,1)}, u32[]{:S(2)}, u32[]{:S(2)}) collective-permute-start(bf16[256,2048]{1,0:T(8,128)(2,1)S(1)} %slice.109), channel_id=1, source_target_pairs={{0,8},{4,12},{8,0},{12,4},{16,24},{20,28},{24,16},{28,20},{1,9},{5... | collective-permute-start | bytes 3145736 | tf_op jit(solution)/shard_map/ppermute | solution.py:1278
  151.4 124.6 %all-gather.12.cloned.1.call-start = ((), (), s32[]{:S(2)}) async-start(), calls=%async_computation.8 | async-start | bytes 3932160 | tf_op jit(solution)/shard_map/all_gather | solution.py:1420
  152.0 219.1 %all-gather.14.cloned.1.call-start = ((), (), s32[]{:S(2)}) async-start(), calls=%async_computation.9 | async-start | bytes 3932160 | tf_op jit(solution)/shard_map/all_gather | solution.py:1422
  152.6 31.3 %collective-permute-start.12 = (bf16[1024,512]{1,0:T(8,128)(2,1)}, bf16[1024,512]{1,0:T(8,128)(2,1)S(1)}, u32[]{:S(2)}, u32[]{:S(2)}) collective-permute-start(bf16[1024,512]{1,0:T(8,128)(2,1)} %all-gather.8.cloned.1.call-done.w0.o0), channel_id=1, source_target_pairs={{0,8},{4,12},{8,0},{12,4},{16,24},{20,28},{24,16},{28,20},{1,9},{5... | collective-permute-start | bytes 3145736 | tf_op jit(solution)/shard_map/ppermute | solution.py:1278
  153.6 30.3 %collective-permute-start.13 = (bf16[1024,512]{1,0:T(8,128)(2,1)}, bf16[1024,512]{1,0:T(8,128)(2,1)S(1)}, u32[]{:S(2)}, u32[]{:S(2)}) collective-permute-start(bf16[1024,512]{1,0:T(8,128)(2,1)} %all-gather.8.cloned.1.call-done.w0.o0), channel_id=1, source_target_pairs={{0,16},{4,20},{8,24},{12,28},{16,0},{20,4},{24,8},{28,12},{1,17},{... | collective-permute-start | bytes 3145736 | tf_op jit(solution)/shard_map/ppermute | solution.py:1278
  186.3 57.7 %collective-permute-start.17 = (bf16[512,2048]{1,0:T(8,128)(2,1)S(1)}, bf16[512,2048]{1,0:T(8,128)(2,1)S(1)}, u32[]{:S(2)}, u32[]{:S(2)}) collective-permute-start(bf16[512,2048]{1,0:T(8,128)(2,1)S(1)} %broadcast_select_fusion.own_grads.cotangent), channel_id=1, source_target_pairs={{0,8},{4,12},{8,0},{12,4},{16,24},{20,28},{24,16},{28,20},{1,9},{5... | collective-permute-start | bytes 6291464 | tf_op jit(solution)/shard_map/ppermute | solution.py:1278
  187.0 56.9 %collective-permute-start.18 = (bf16[512,2048]{1,0:T(8,128)(2,1)S(1)}, bf16[512,2048]{1,0:T(8,128)(2,1)S(1)}, u32[]{:S(2)}, u32[]{:S(2)}) collective-permute-start(bf16[512,2048]{1,0:T(8,128)(2,1)S(1)} %broadcast_select_fusion.own_grads.cotangent), channel_id=1, source_target_pairs={{0,16},{4,20},{8,24},{12,28},{16,0},{20,4},{24,8},{28,12},{1,17},{... | collective-permute-start | bytes 6291464 | tf_op jit(solution)/shard_map/ppermute | solution.py:1278
  209.0 34.9 %collective-permute-start.16 = (bf16[512,2048]{1,0:T(8,128)(2,1)}, bf16[512,2048]{1,0:T(8,128)(2,1)}, u32[]{:S(2)}, u32[]{:S(2)}) collective-permute-start(bf16[512,2048]{1,0:T(8,128)(2,1)} %get-tuple-element.93), channel_id=1, source_target_pairs={{0,4},{4,0},{8,12},{12,8},{16,20},{20,16},{24,28},{28,24},{1,5},{5... | collective-permute-start | bytes 6291464 | tf_op jit(solution)/shard_map/ppermute | solution.py:1278
  251.5 47.4 %collective-permute-start.19 = (bf16[512,2048]{1,0:T(8,128)(2,1)}, bf16[512,2048]{1,0:T(8,128)(2,1)}, u32[]{:S(2)}, u32[]{:S(2)}) collective-permute-start(bf16[512,2048]{1,0:T(8,128)(2,1)} %get-tuple-element.97.own_tokens), channel_id=1, source_target_pairs={{0,8},{4,12},{8,0},{12,4},{16,24},{20,28},{24,16},{28,20},{1,9},{5... | collective-permute-start | bytes 6291464 | tf_op jit(solution)/shard_map/ppermute | solution.py:1278
  252.7 46.8 %collective-permute-start.20 = (bf16[512,2048]{1,0:T(8,128)(2,1)}, bf16[512,2048]{1,0:T(8,128)(2,1)}, u32[]{:S(2)}, u32[]{:S(2)}) collective-permute-start(bf16[512,2048]{1,0:T(8,128)(2,1)} %get-tuple-element.97.own_tokens), channel_id=1, source_target_pairs={{0,16},{4,20},{8,24},{12,28},{16,0},{20,4},{24,8},{28,12},{1,17},{... | collective-permute-start | bytes 6291464 | tf_op jit(solution)/shard_map/ppermute | solution.py:1278
  253.7 398.2 %reduce-scatter.6.cloned.1.call-start = ((), (), s32[]{:S(2)}) async-start(), calls=%async_computation.10 | async-start | bytes 3932160 | tf_op jit(solution)/shard_map/reduce_scatter | solution.py:1465
  253.9 45.6 %collective-permute-start.21 = (bf16[1536,1024]{1,0:T(8,128)(2,1)}, bf16[1536,1024]{1,0:T(8,128)(2,1)S(1)}, u32[]{:S(2)}, u32[]{:S(2)}) collective-permute-start(bf16[1536,1024]{1,0:T(8,128)(2,1)} %all-gather.10.cloned.1.call-done.gate_own), channel_id=1, source_target_pairs={{0,4},{4,0},{8,12},{12,8},{16,20},{20,16},{24,28},{28,24},{1,5},{5... | collective-permute-start | bytes 9437192 | tf_op jit(solution)/shard_map/ppermute | solution.py:1278
  382.4 115.2 %collective-permute-start.26 = (bf16[1536,1024]{1,0:T(8,128)(2,1)}, bf16[1536,1024]{1,0:T(8,128)(2,1)}, u32[]{:S(2)}, u32[]{:S(2)}) collective-permute-start(bf16[1536,1024]{1,0:T(8,128)(2,1)} %fusion.6), channel_id=1, source_target_pairs={{0,4},{4,0},{8,12},{12,8},{16,20},{20,16},{24,28},{28,24},{1,5},{5... | collective-permute-start | bytes 9437192 | tf_op jit(solution)/shard_map/ppermute | solution.py:1278
  509.6 142.3 %reduce-scatter.8.cloned.1.call-start = ((), (), s32[]{:S(2)}) async-start(), calls=%async_computation.11 | async-start | bytes 3932160 | tf_op jit(solution)/shard_map/reduce_scatter | solution.py:1465
  535.7 198.7 %reduce-scatter.12.cloned.1.call-start = ((), (), s32[]{:S(2)}) async-start(), calls=%async_computation.13 | async-start | bytes 1310720 | tf_op jit(solution)/shard_map/reduce_scatter | solution.py:1465
  595.9 138.6 %reduce-scatter.10.cloned.1.call-start = ((), (), s32[]{:S(2)}) async-start(), calls=%async_computation.12 | async-start | bytes 3932160 | tf_op jit(solution)/shard_map/reduce_scatter | solution.py:1465
  596.6 188.9 %reduce-scatter.14.cloned.1.call-start = ((), (), s32[]{:S(2)}) async-start(), calls=%async_computation.14 | async-start | bytes 2621440 | tf_op jit(solution)/shard_map/reduce_scatter | solution.py:1554
  596.7 47.2 %collective-permute-start.27 = (bf16[512,2048]{1,0:T(8,128)(2,1)}, bf16[512,2048]{1,0:T(8,128)(2,1)S(1)}, u32[]{:S(2)}, u32[]{:S(2)}) collective-permute-start(bf16[512,2048]{1,0:T(8,128)(2,1)} %get-tuple-element.128), channel_id=1, source_target_pairs={{0,8},{4,12},{8,0},{12,4},{16,24},{20,28},{24,16},{28,20},{1,9},{5... | collective-permute-start | bytes 6291464 | tf_op jit(solution)/shard_map/ppermute | solution.py:1278
  597.8 46.7 %collective-permute-start.28 = (bf16[512,2048]{1,0:T(8,128)(2,1)S(1)}, bf16[512,2048]{1,0:T(8,128)(2,1)S(1)}, u32[]{:S(2)}, u32[]{:S(2)}) collective-permute-start(bf16[512,2048]{1,0:T(8,128)(2,1)S(1)} %copy-done.24), channel_id=1, source_target_pairs={{0,16},{4,20},{8,24},{12,28},{16,0},{20,4},{24,8},{28,12},{1,17},{... | collective-permute-start | bytes 6291464 | tf_op jit(solution)/shard_map/ppermute | solution.py:1278
  750.1 20.6 %collective-permute-start.33 = (bf16[768,256]{1,0:T(8,128)(2,1)S(1)}, bf16[768,256]{1,0:T(8,128)(2,1)S(1)}, u32[]{:S(2)}, u32[]{:S(2)}) collective-permute-start(bf16[768,256]{1,0:T(8,128)(2,1)S(1)} %get-tuple-element.175), channel_id=1, source_target_pairs={{0,16},{4,20},{8,24},{12,28},{16,0},{20,4},{24,8},{28,12},{1,17},{... | collective-permute-start | bytes 1179656 | tf_op jit(solution)/shard_map/ppermute | solution.py:1278
  751.3 21.4 %collective-permute-start.32 = (bf16[768,256]{1,0:T(8,128)(2,1)S(1)}, bf16[768,256]{1,0:T(8,128)(2,1)S(1)}, u32[]{:S(2)}, u32[]{:S(2)}) collective-permute-start(bf16[768,256]{1,0:T(8,128)(2,1)S(1)} %get-tuple-element.176), channel_id=1, source_target_pairs={{0,8},{4,12},{8,0},{12,4},{16,24},{20,28},{24,16},{28,20},{1,9},{5... | collective-permute-start | bytes 1179656 | tf_op jit(solution)/shard_map/ppermute | solution.py:1278
  755.1 20.7 %collective-permute-start.44 = (bf16[384,256]{1,0:T(8,128)(2,1)}, bf16[384,256]{1,0:T(8,128)(2,1)}, u32[]{:S(2)}, u32[]{:S(2)}) collective-permute-start(bf16[384,256]{1,0:T(8,128)(2,1)} %get-tuple-element.182), channel_id=1, source_target_pairs={{0,24},{4,28},{8,16},{12,20},{16,8},{20,12},{24,0},{28,4},{1,25},{... | collective-permute-start | bytes 589832 | tf_op jit(solution)/shard_map/ppermute | solution.py:1278
  755.3 23.0 %collective-permute-start.43 = (bf16[384,256]{1,0:T(8,128)(2,1)}, bf16[384,256]{1,0:T(8,128)(2,1)}, u32[]{:S(2)}, u32[]{:S(2)}) collective-permute-start(bf16[384,256]{1,0:T(8,128)(2,1)} %get-tuple-element.183), channel_id=1, source_target_pairs={{0,16},{4,20},{8,24},{12,28},{16,0},{20,4},{24,8},{28,12},{1,17},{... | collective-permute-start | bytes 589832 | tf_op jit(solution)/shard_map/ppermute | solution.py:1278
  770.7 22.9 %collective-permute-start.30 = (bf16[512,2048]{1,0:T(8,128)(2,1)}, bf16[512,2048]{1,0:T(8,128)(2,1)}, u32[]{:S(2)}, u32[]{:S(2)}) collective-permute-start(bf16[512,2048]{1,0:T(8,128)(2,1)} %get-tuple-element.137), channel_id=1, source_target_pairs={{1,4},{3,6},{4,1},{6,3},{9,12},{11,14},{12,9},{14,11},{17,20},{19,... | collective-permute-start | bytes 6291464 | tf_op jit(solution)/shard_map/ppermute | solution.py:1287
  (50 other events, 601.0 us)
Sparse Core Ops, SparseCore 0:
  12.2 48.5 all-gather.5
  115.0 25.6 all-gather.7
  151.6 60.7 all-gather.9
  213.8 62.1 all-gather.11
  277.4 62.1 all-gather.13
  509.7 58.1 reduce-scatter.5
  570.2 60.2 reduce-scatter.7
  632.8 27.1 reduce-scatter.11
  662.4 70.8 reduce-scatter.9
  735.5 43.6 reduce-scatter.13
